TPU v7x, 32 devices: a whole 2x2x4 slice. The times are simulated.
32 devices in a mesh: row: 8 (over y, x, core), col: 4 (over z).
Axes of the slice: x: 2, y: 2, z: 4, core: 2. Of those that a mesh axis runs over, the one named last changes fastest.
Arguments:
- samples: bfloat16 [1536, 16384], P('col', 'row'), may hold values from -24 to 24
- omega: float32 [16384, 8, 4, 512], P('row', None, 'col'), may hold values from -0.4 to 2, as said below
- sign_mask: int32 [16384, 8, 4, 512], P('row', None, 'col'), may hold values from -1 to 1, as said below
- step_size: float32 [1], replicated, may hold values from 0.3 to 1
Outputs:
- next_omega: float32 [16384, 8, 4, 512], P('row', None, 'col')
Inputs may be any that keep to these rules, and one draw needn't show every extreme that they name: sign_mask is symmetric as a 16384 x 16384 matrix, holds only -1, 0 and 1, and is 1 on the diagonal. omega is symmetric as a 16384 x 16384 matrix, its diagonal lies in 0.5 to 2, and each off-diagonal entry is 0 or has the sign that sign_mask allows.
All inputs are finite; a program needn't handle non-finite values.
Results may differ from a plain program's by a relative error of at most 0.0041.
Values may be sent and summed in bfloat16 or wider, within the bound.
No kernel may reach another device: no remote copies, remote signals or barrier semaphores. Data moves between devices by JAX's collectives and lax.ppermute only.
A program may use at most 384 MiB of HBM per device.

v0:
```python
import functools

import jax
import jax.numpy as jnp
from jax import lax
from jax.experimental import pallas as pl
from jax.experimental.pallas import tpu as pltpu
from jax.sharding import PartitionSpec as P

PENALTY = 0.05
LANES = 128
SUBS = 8
GROUPS = 2
PIECES = 2
X_STEPS = (1, 2, 1)
MIB = 1 << 20


def convert_kernel(omega_ref, out_ref):
    rows = omega_ref.shape[0]
    blocks, _, width = out_ref.shape
    flat = omega_ref.reshape(rows * SUBS, LANES)
    per_block = width // LANES
    for c in range(SUBS):
        piece = flat[pl.ds(c, rows, stride=SUBS), :].astype(jnp.bfloat16)
        lane = (c % per_block) * LANES
        out_ref[c // per_block, :, lane : lane + LANES] = piece


def convert(omega3, group_count, sub_width):
    row_total, lane_tiles, _ = omega3.shape
    tile = min(512, row_total)
    blocks = SUBS * LANES // sub_width
    return pl.pallas_call(
        convert_kernel,
        grid=(row_total // tile, lane_tiles // SUBS),
        in_specs=[pl.BlockSpec((tile, SUBS, LANES), lambda i, j: (i, j, 0))],
        out_specs=pl.BlockSpec((blocks, tile, sub_width), lambda i, j: (j, i, 0)),
        out_shape=jax.ShapeDtypeStruct((group_count, row_total, sub_width), jnp.bfloat16),
        compiler_params=pltpu.CompilerParams(vmem_limit_bytes=32 * MIB),
        cost_estimate=pl.CostEstimate(flops=0, bytes_accessed=omega3.size * 6, transcendentals=0),
        name="omega_to_bf16",
    )(omega3)


def turn_kernel(*refs):
    refs[-1][...] = jnp.concatenate([r[...] for r in refs[:-1]], axis=0).T


def turn(pieces, width):
    rows, total = pieces[0].shape
    count = rows * len(pieces)
    return pl.pallas_call(
        turn_kernel,
        grid=(total // width,),
        in_specs=[pl.BlockSpec((rows, width), lambda i: (0, i)) for _ in pieces],
        out_specs=pl.BlockSpec((width, count), lambda i: (i, 0)),
        out_shape=jax.ShapeDtypeStruct((total, count), pieces[0].dtype),
        compiler_params=pltpu.CompilerParams(vmem_limit_bytes=16 * MIB),
        cost_estimate=pl.CostEstimate(
            flops=0, bytes_accessed=4 * count * total, transcendentals=0
        ),
        name="turn",
    )(*pieces)


def tie(values, done):
    return lax.optimization_barrier((values, done))[0] if done else values


def multiply_rows(x_refs, weight):
    rows = jnp.concatenate([x[...] for x in x_refs], axis=0)
    return jnp.dot(rows, weight, preferred_element_type=jnp.float32)


def sent_kernel(count, order_ref, *refs):
    x_refs, w_ref, out_ref = refs[:count], refs[count], refs[count + 1]
    out_ref[0] = multiply_rows(x_refs, w_ref[0]).astype(jnp.bfloat16)


def reversed_bits(value, bits):
    return sum(((value >> b) & 1) << (bits - 1 - b) for b in range(bits))


def kept_kernel(count, bits, order_ref, *refs):
    x_refs, w_ref, other_ref = refs[:count], refs[count], refs[count + 1]
    halves = (refs[count + 2 : count + 4], refs[count + 4 : count + 6])
    total = multiply_rows(x_refs, w_ref[0]) + other_ref[0].astype(jnp.float32)
    rows = total.shape[0] // 2
    step = pl.program_id(0)
    split = 1 << (bits - 1)
    for relative in range(1 << bits):

        @pl.when(step == relative)
        def _():
            for h, (sent_ref, kept_ref) in enumerate(halves):
                place = relative if h else reversed_bits(relative, bits)
                target = sent_ref if place >= split else kept_ref
                target[place % split] = total[h * rows : (h + 1) * rows].astype(target.dtype)


def pair_products(xs, weights, order_sent, order_kept, row_partner, beside):
    count = len(xs)
    rows, depth = xs[0].shape
    group_count, _, width = weights.shape
    blocks = group_count // 2
    bits = blocks.bit_length() - 1
    total_rows = count * rows
    x_spec = pl.BlockSpec((rows, depth), lambda g, order: (0, 0))
    w_spec = pl.BlockSpec((1, depth, width), lambda g, order: (order[g], 0, 0))
    block_spec = pl.BlockSpec((1, total_rows, width), lambda g, order: (g, 0, 0))
    cost = pl.CostEstimate(
        flops=2 * total_rows * depth * blocks * width,
        bytes_accessed=weights.size + 2 * count * xs[0].size + 2 * blocks * total_rows * width,
        transcendentals=0,
    )
    params = pltpu.CompilerParams(vmem_limit_bytes=48 * MIB)
    sent = pl.pallas_call(
        functools.partial(sent_kernel, count),
        grid_spec=pltpu.PrefetchScalarGridSpec(
            num_scalar_prefetch=1,
            grid=(blocks,),
            in_specs=[x_spec] * count + [w_spec],
            out_specs=block_spec,
        ),
        out_shape=jax.ShapeDtypeStruct((blocks, total_rows, width), jnp.bfloat16),
        compiler_params=params,
        cost_estimate=cost,
        name="products_sent",
    )(order_sent, *xs, weights)
    other = tie(lax.ppermute(sent, "row", row_partner(1)), beside(0))
    half = (blocks // 2, total_rows // 2, width)
    half_spec = pl.BlockSpec(half, lambda g, order: (0, 0, 0))
    outs = pl.pallas_call(
        functools.partial(kept_kernel, count, bits),
        grid_spec=pltpu.PrefetchScalarGridSpec(
            num_scalar_prefetch=1,
            grid=(blocks,),
            in_specs=[x_spec] * count + [w_spec, block_spec],
            out_specs=[half_spec] * 4,
        ),
        out_shape=[
            jax.ShapeDtypeStruct(half, jnp.bfloat16),
            jax.ShapeDtypeStruct(half, jnp.float32),
        ]
        * 2,
        compiler_params=params,
        cost_estimate=cost,
        name="products_kept",
    )(order_kept, *xs, weights, other)
    return [(outs[0], outs[1]), (outs[2], outs[3])]


def halve_kernel(split, *refs):
    for h in range(2):
        kept_ref, other_ref, next_sent, next_kept = refs[2 * h], refs[2 * h + 1], refs[4 + 2 * h], refs[5 + 2 * h]
        next_kept[...] = kept_ref[:split] + other_ref[:split].astype(jnp.float32)
        total = kept_ref[split:] + other_ref[split:].astype(jnp.float32)
        next_sent[...] = total.astype(jnp.bfloat16)


def halve(pieces, others):
    kept = pieces[0][1]
    split = kept.shape[0] // 2
    shape = (split,) + kept.shape[1:]
    outs = pl.pallas_call(
        functools.partial(halve_kernel, split),
        out_shape=[
            jax.ShapeDtypeStruct(shape, jnp.bfloat16),
            jax.ShapeDtypeStruct(shape, jnp.float32),
        ]
        * 2,
        compiler_params=pltpu.CompilerParams(vmem_limit_bytes=32 * MIB),
        cost_estimate=pl.CostEstimate(flops=0, bytes_accessed=18 * kept.size, transcendentals=0),
        name="halve",
    )(pieces[0][1], others[0], pieces[1][1], others[1])
    return [(outs[0], outs[1]), (outs[2], outs[3])]


def share_kernel(*refs):
    share_ref, turned_ref = refs[4:]
    rows = refs[0].shape[1]
    for h in range(2):
        total = refs[2 * h][0] + refs[2 * h + 1][0].astype(jnp.float32)
        share_ref[h * rows : (h + 1) * rows, :] = total.astype(jnp.bfloat16)
    turned_ref[...] = share_ref[...].T


def finish_share(pieces, others):
    _, rows, width = pieces[0][1].shape
    return pl.pallas_call(
        share_kernel,
        out_shape=[
            jax.ShapeDtypeStruct((2 * rows, width), jnp.bfloat16),
            jax.ShapeDtypeStruct((width, 2 * rows), jnp.bfloat16),
        ],
        compiler_params=pltpu.CompilerParams(vmem_limit_bytes=24 * MIB),
        cost_estimate=pl.CostEstimate(
            flops=0, bytes_accessed=20 * rows * width, transcendentals=0
        ),
        name="share",
    )(pieces[0][1], others[0], pieces[1][1], others[1])


def sum_over_rows(xs, weights, order_sent, order_kept, row_partner, beside):
    pieces = pair_products(xs, weights, order_sent, order_kept, row_partner, beside)
    bits = weights.shape[0].bit_length() - 2
    for level in range(bits):
        masks = (2 << level, 1 << (bits - level))
        others = [
            lax.ppermute(sent, "row", row_partner(mask)) for (sent, _), mask in zip(pieces, masks)
        ]
        others = tie(others, beside(level + 1))
        if level < bits - 1:
            pieces = halve(pieces, others)
    share, turned = finish_share(pieces, others)
    return share, turned


def update_kernel(sizes, group, sub_width, scale, last, info_ref, *refs):
    col_count, per_group = sizes
    xs, refs = refs[:per_group], refs[per_group:]
    ys, refs = refs[:col_count], refs[col_count:]
    y_cols, refs = refs[:per_group], refs[per_group:]
    x_cols, refs = refs[:col_count], refs[col_count:]
    omega_ref, row_ref, col_ref = refs[:3]
    sign_ref = refs[3] if last else None
    out_ref, cross_ref, rate_ref = refs[3 + last :]
    rows = omega_ref.shape[0]
    cross = cross_ref.reshape(rows * SUBS, LANES)
    per_block = sub_width // LANES
    blocks = SUBS // per_block
    distance = pl.program_id(1)

    @pl.when(pl.program_id(0) == 0)
    def _():
        rate = rate_ref.at[distance].reshape(rows * SUBS, LANES)
        for c in range(SUBS):
            rate[pl.ds(c, rows, stride=SUBS), :] = jnp.broadcast_to(row_ref[...], (rows, LANES))

    for value in range(col_count):

        @pl.when(distance == value)
        def _():
            met = [x_cols[(group * per_group + s + value) % col_count] for s in range(per_group)]
            left = jnp.concatenate([x[...] for x in xs] + [ys[value][...]], axis=1)
            for b in range(blocks):
                right = jnp.concatenate([r[b] for r in (*y_cols, *met)], axis=0)
                total = jnp.dot(left, right, preferred_element_type=jnp.float32)
                for lane in range(0, sub_width, LANES):
                    spot = pl.ds(b * per_block + lane // LANES, rows, stride=SUBS)
                    cross[spot, :] = total[:, lane : lane + LANES]

    col_rate = col_ref[...][None]
    col_shift = col_rate * PENALTY
    col_smooth = col_rate * scale
    for first in range(0, rows, 64):
        span = slice(first, min(first + 64, rows))
        row_rate = rate_ref[distance, span]
        trial = omega_ref[span] - (row_rate * col_smooth) * cross_ref[span]
        if last:
            sign = sign_ref[span].astype(jnp.float32)
            trial = sign * jnp.maximum(sign * trial - row_rate * col_shift, 0.0)
        out_ref[span] = trial

    if last:
        @pl.when(jnp.logical_and(distance == 0, pl.program_id(0) == info_ref[0] // blocks))
        def _():
            first_tile = info_ref[0] % blocks * per_block
            for first in range(0, rows, 64):
                span = slice(first, min(first + 64, rows))
                shape = out_ref[span].shape
                rate = rate_ref[distance, span] * col_rate
                trial = omega_ref[span] - rate * (cross_ref[span] * scale)
                value = 0.5 * (trial + jnp.sqrt(trial * trial + 4.0 * rate))
                row_ids = lax.broadcasted_iota(jnp.int32, shape, 0) + first
                tile_ids = lax.broadcasted_iota(jnp.int32, shape, 1) - first_tile
                col_ids = tile_ids * LANES + lax.broadcasted_iota(jnp.int32, shape, 2)
                out_ref[span] = jnp.where(row_ids == col_ids, value, out_ref[span])


def update(group, xs, ys, y_cols, x_cols, omega3, row_rate, col_rate, sign3, info, scale):
    row_total, lane_tiles, _ = omega3.shape
    part = xs[0].shape[1]
    tile = sub_width = ys[0].shape[0]
    blocks = SUBS * LANES // sub_width
    last = sign3 is not None
    sizes = (len(ys), len(xs))
    grid_block = pl.BlockSpec((tile, SUBS, LANES), lambda j, d, p: (p[1 + d], j, 0))
    columns = list(y_cols) + list(x_cols)
    operands = [*xs, *ys, *[b for b, _ in columns], omega3, row_rate, col_rate]
    return pl.pallas_call(
        functools.partial(update_kernel, sizes, group, sub_width, scale, last),
        grid_spec=pltpu.PrefetchScalarGridSpec(
            num_scalar_prefetch=1,
            grid=(lane_tiles // SUBS, row_total // tile),
            in_specs=[pl.BlockSpec((tile, part), lambda j, d, p: (p[1 + d], 0)) for _ in xs]
            + [pl.BlockSpec(y.shape, lambda j, d, p: (0, 0)) for y in ys]
            + [
                pl.BlockSpec((blocks, part, sub_width), lambda j, d, p, at=at: (j, at, 0))
                for _, at in columns
            ]
            + [
                grid_block,
                pl.BlockSpec((tile, 1), lambda j, d, p: (p[1 + d], 0)),
                pl.BlockSpec((SUBS, LANES), lambda j, d, p: (j, 0)),
            ]
            + [grid_block] * last,
            out_specs=grid_block,
            scratch_shapes=[
                pltpu.VMEM((tile, SUBS, LANES), jnp.float32),
                pltpu.VMEM((row_total // tile, tile, SUBS, LANES), jnp.float32),
            ],
        ),
        out_shape=jax.ShapeDtypeStruct(omega3.shape, jnp.float32),
        compiler_params=pltpu.CompilerParams(vmem_limit_bytes=56 * MIB),
        cost_estimate=pl.CostEstimate(
            flops=4 * part * len(xs) * omega3.size,
            bytes_accessed=omega3.size * 12,
            transcendentals=0,
        ),
        name="last_terms" if last else "first_terms",
    )(info, *operands, *([sign3] if last else []))


def body(samples, omega, sign_mask, step_size):
    row_total, group_count, _, sub_width = omega.shape
    lane_tiles = group_count * sub_width // LANES
    row_count = lax.axis_size("row")
    col_count = lax.axis_size("col")
    row_index = lax.axis_index("row").astype(jnp.int32)
    col_index = lax.axis_index("col").astype(jnp.int32)
    part = samples.shape[0]
    sample_total = part * col_count
    per_group = col_count // GROUPS
    omega3 = omega.reshape(row_total, lane_tiles, LANES)
    sign3 = sign_mask.reshape(row_total, lane_tiles, LANES)

    def row_partner(mask):
        return [(r, r ^ mask) for r in range(row_count)]

    ring = [(c, (c + 1) % col_count) for c in range(col_count)]
    relative = jnp.arange(row_count // 2, dtype=jnp.int32)
    order_kept = ((row_index >> 1) ^ relative) * 2 + (row_index & 1)
    order_sent = order_kept ^ 1

    xs = [[samples[k * part // PIECES : (k + 1) * part // PIECES] for k in range(PIECES)]]
    x_turned, y_planes = [], []
    weights = convert(omega3, group_count, sub_width)

    def advance():
        if len(xs[-1]) == PIECES:
            xs.append([])
        done = lax.ppermute(xs[-2][len(xs[-1])], "col", ring)
        xs[-1].append(done)
        return done

    def to_distance(y, distance):
        if not distance:
            return y
        return lax.ppermute(y, "col", [(c, (c + distance) % col_count) for c in range(col_count)])

    def complete(length):
        return len(xs) >= length and len(xs[length - 1]) == PIECES

    def gather(rows):
        return lax.all_gather(jnp.concatenate(rows, axis=0), "row", axis=0, tiled=False)

    x_cols, y_cols, waiting = [], [], []
    for k in range(GROUPS):
        first = k * per_group
        while not complete(first + per_group):
            advance()
        if not k:
            xs[-1] = tie(xs[-1], [weights])
        group = xs[first : first + per_group]
        own = [
            lax.dynamic_slice_in_dim(x, col_index * sub_width, sub_width, 1)
            for pieces in group
            for x in pieces
        ]
        block = gather(own + waiting)
        x_cols.append((block, 0))
        if waiting:
            y_cols.append((block, 1))

        def beside(exchange):
            done = []
            if exchange == 0:
                x_turned.extend(turn(x, sub_width) for x in group)
                done.extend(x_turned[first:])
                done.extend(block for block, _ in x_cols[:-1])
            for _ in range(X_STEPS[min(exchange, len(X_STEPS) - 1)]):
                if not complete(col_count):
                    done.append(advance())
            if y_planes and exchange == 1:
                done.append(y_planes[0][1])
            if y_planes and exchange == 2:
                done.extend(y_planes[0][2:])
            return done

        share, turned = sum_over_rows(
            [x for pieces in group for x in pieces],
            weights,
            order_sent,
            order_kept,
            row_partner,
            beside,
        )
        waiting = [share]
        y_planes.append([to_distance(turned, distance) for distance in range(col_count)])
    last = gather(tie(waiting, [x_cols[-1][0]]))
    y_cols.append((last, 0))
    group_rows = part * per_group

    def mean_square(pieces, axis):
        total = sum(jnp.sum(jnp.square(p.astype(jnp.float32)), axis=axis) for p in pieces)
        total = lax.optimization_barrier(total) / sample_total + 1e-06
        return lax.optimization_barrier(total.astype(jnp.bfloat16)).astype(jnp.float32)

    x_pieces = [x for pieces in xs for x in pieces]
    row_rate = (step_size[0] * lax.rsqrt(mean_square(x_pieces, 0)))[:, None]
    col_rate = lax.rsqrt(mean_square([block[:, :group_rows] for block, _ in x_cols], 1))
    col_rate = col_rate.reshape(lane_tiles, LANES)

    planes = (col_index - jnp.arange(col_count, dtype=jnp.int32) + col_count) % col_count
    info = jnp.concatenate([row_index[None], planes])
    x_entries = [(block, at * per_group + s) for block, at in x_cols for s in range(per_group)]
    updated = omega3
    for k in range(GROUPS):
        block, at = y_cols[k]
        first = k * per_group
        updated = update(
            k,
            x_turned[first : first + per_group],
            y_planes[k],
            [(block, at * per_group + s) for s in range(per_group)],
            x_entries,
            updated,
            row_rate,
            col_rate,
            sign3 if k == GROUPS - 1 else None,
            info,
            0.5 / sample_total,
        )
    return updated.reshape(omega.shape)


def solution(mesh):
    in_specs = (P("col", "row"), P("row", None, "col", None), P("row", None, "col", None), P())
    out_specs = P("row", None, "col", None)
    return jax.shard_map(body, mesh=mesh, in_specs=in_specs, out_specs=out_specs, check_vma=False)
```

profile of v0, /device:TPU:0, one launch (start us, length us, event | category | flops | bytes accessed | tf_op | source)
XLA Modules:
  0.0 375.8 jit_solution(4972026741568167871)
XLA Ops:
  6.5 1.5 fusion.1
  8.1 3.1 collective-permute-start.1
  11.2 1.6 collective-permute-start
  12.8 19.2 %omega_to_bf16.1.refs_4_ = bf16[8,2048,512]{2,1,0:T(8,128)(2,1)S(1)} custom-call(f32[2048,32,128]{2,1,0:T(8,128)} %bitcast.22), custom_call_target="tpu_custom_call" | custom-call | bytes 50331648 | tf_op jit(solution)/shard_map/omega_to_bf16/pallas_call | solution.py:34
  31.9 6.2 %copy-done = bf16[8,2048,512]{2,1,0:T(8,128)(2,1)} copy-done((bf16[8,2048,512]{2,1,0:T(8,128)(2,1)}, bf16[8,2048,512]{2,1,0:T(8,128)(2,1)S(1)}, u32[]{:S(2)}) %copy-start) | copy-done | bytes 16777240
  38.1 9.5 %collective-permute-done.refs_2_.refs_0_ = bf16[192,2048]{1,0:T(8,128)(2,1)S(1)} collective-permute-done((bf16[192,2048]{1,0:T(8,128)(2,1)S(1)}, bf16[192,2048]{1,0:T(8,128)(2,1)S(1)}, u32[]{:S(2)}, u32[]{:S(2)}) %collective-permute-start) | collective-permute-done | bytes 786464 | tf_op jit(solution)/shard_map/ppermute | solution.py:354
  48.8 10.6 %products_sent.3 = bf16[4,768,512]{2,1,0:T(8,128)(2,1)} custom-call(s32[4]{0:T(128)S(1)} %get-tuple-element.73.order_ref, bf16[192,2048]{1,0:T(8,128)(2,1)S(1)} %get-tuple-element.76.refs_0_, bf16[192,2048]{1,0:T(8,128)(2,1)S(1)} %get-tuple-element.75.refs_1_, bf16[192,2048]{1,0:T(8,128)(2,1)S(1)} %collective-permute-done.refs_2_.refs_0_, ...), custom_call_target="tpu_custom_call" | custom-call | flops 6442450944 | bytes 14680064 | tf_op jit(solution)/shard_map/products_sent/pallas_call | solution.py:118
  59.3 1.1 copy-done.13
  61.3 1.2 copy-done.1
  62.5 1.1 collective-permute-start.3
  64.3 1.1 copy-done.2
  65.4 16.0 %collective-permute-done.2.refs_0_ = bf16[192,2048]{1,0:T(8,128)(2,1)S(1)} collective-permute-done((bf16[192,2048]{1,0:T(8,128)(2,1)S(1)}, bf16[192,2048]{1,0:T(8,128)(2,1)S(1)}, u32[]{:S(2)}, u32[]{:S(2)}) %collective-permute-start.2) | collective-permute-done | bytes 786464 | tf_op jit(solution)/shard_map/ppermute | solution.py:354
  81.5 1.6 copy-done.27
  83.1 1.1 copy-done.8
  84.2 11.5 %products_kept.3 = (bf16[2,384,512]{2,1,0:T(8,128)(2,1)S(1)}, f32[2,384,512]{2,1,0:T(8,128)}, bf16[2,384,512]{2,1,0:T(8,128)(2,1)S(1)}, f32[2,384,512]{2,1,0:T(8,128)}) custom-call(s32[4]{0:T(128)S(1)} %get-tuple-element.74.order_ref, bf16[192,2048]{1,0:T(8,128)(2,1)S(1)} %copy-done.14, bf16[192,2048]{1,0:T(8,128)(2,1)S(1)} %copy-done.11, ...), custom_call_target="tpu_custom_call" | custom-call | flops 6442450944 | bytes 14680064 | tf_op jit(solution)/shard_map/products_kept/pallas_call | solution.py:134
  95.8 1.5 collective-permute-start.10
  97.3 1.7 collective-permute-start.11
  98.9 16.2 %collective-permute-done.4.refs_0_.refs_2_ = bf16[192,2048]{1,0:T(8,128)(2,1)S(1)} collective-permute-done((bf16[192,2048]{1,0:T(8,128)(2,1)S(1)}, bf16[192,2048]{1,0:T(8,128)(2,1)S(1)}, u32[]{:S(2)}, u32[]{:S(2)}) %collective-permute-start.4) | collective-permute-done | bytes 786464 | tf_op jit(solution)/shard_map/ppermute | solution.py:354
  115.8 1.4 copy-done.17
  117.2 1.4 copy-done.18
  118.8 1.6 collective-permute-start.12
  123.4 8.3 %collective-permute-done.5.refs_1_.refs_3_ = bf16[192,2048]{1,0:T(8,128)(2,1)S(1)} collective-permute-done((bf16[192,2048]{1,0:T(8,128)(2,1)S(1)}, bf16[192,2048]{1,0:T(8,128)(2,1)S(1)}, u32[]{:S(2)}, u32[]{:S(2)}) %collective-permute-start.5) | collective-permute-done | bytes 786464 | tf_op jit(solution)/shard_map/ppermute | solution.py:354
  132.4 1.1 share.2
  134.5 10.6 %products_sent.2 = bf16[4,768,512]{2,1,0:T(8,128)(2,1)} custom-call(s32[4]{0:T(128)S(1)} %get-tuple-element.73.order_ref, bf16[192,2048]{1,0:T(8,128)(2,1)S(1)} %collective-permute-done.2.refs_0_, bf16[192,2048]{1,0:T(8,128)(2,1)S(1)} %collective-permute-done.3.refs_1_, bf16[192,2048]{1,0:T(8,128)(2,1)S(1)} %collective-permute-done.4.refs_0_.refs_2_, ...), custom_call_target="tpu_custom_call" | custom-call | flops 6442450944 | bytes 14680064 | tf_op jit(solution)/shard_map/products_sent/pallas_call | solution.py:118
  146.0 1.2 copy-done.3
  147.9 1.1 copy-done.4
  149.1 2.1 collective-permute-done.6.refs_5_
  151.2 11.5 %products_kept.2 = (bf16[2,384,512]{2,1,0:T(8,128)(2,1)S(1)}, f32[2,384,512]{2,1,0:T(8,128)}, bf16[2,384,512]{2,1,0:T(8,128)(2,1)S(1)}, f32[2,384,512]{2,1,0:T(8,128)}) custom-call(s32[4]{0:T(128)S(1)} %get-tuple-element.74.order_ref, bf16[192,2048]{1,0:T(8,128)(2,1)S(1)} %collective-permute-done.2.refs_0_, ...), custom_call_target="tpu_custom_call" | custom-call | flops 6442450944 | bytes 14680064 | tf_op jit(solution)/shard_map/products_kept/pallas_call | solution.py:134
  162.7 1.5 collective-permute-start.7
  164.2 1.5 collective-permute-start.8
  165.7 1.8 collective-permute-start.18
  167.5 4.1 %collective-permute-done.14.refs_3_ = bf16[512,768]{1,0:T(8,128)(2,1)} collective-permute-done((bf16[512,768]{1,0:T(8,128)(2,1)}, bf16[512,768]{1,0:T(8,128)(2,1)}, u32[]{:S(2)}, u32[]{:S(2)}) %collective-permute-start.14) | collective-permute-done | bytes 786464 | tf_op jit(solution)/shard_map/ppermute | solution.py:361
  171.6 24.9 %collective-permute-done.7.refs_1_ = bf16[2,384,512]{2,1,0:T(8,128)(2,1)S(1)} collective-permute-done((bf16[2,384,512]{2,1,0:T(8,128)(2,1)S(1)}, bf16[2,384,512]{2,1,0:T(8,128)(2,1)S(1)}, u32[]{:S(2)}, u32[]{:S(2)}) %collective-permute-start.7) | collective-permute-done | bytes 786464 | tf_op jit(solution)/shard_map/ppermute | solution.py:211
  196.5 2.9 collective-permute-done.8.refs_3_
  199.4 1.4 copy-done.15
  200.8 1.6 copy-done.16
  202.7 2.4 collective-permute-start.15
  205.1 16.5 %collective-permute-done.17.refs_4_ = bf16[512,768]{1,0:T(8,128)(2,1)S(1)} collective-permute-done((bf16[512,768]{1,0:T(8,128)(2,1)}, bf16[512,768]{1,0:T(8,128)(2,1)S(1)}, u32[]{:S(2)}, u32[]{:S(2)}) %collective-permute-start.17) | collective-permute-done | bytes 786464 | tf_op jit(solution)/shard_map/ppermute | solution.py:361
  222.2 1.8 collective-permute-done.16.refs_3_
  226.1 1.9 all-gather.9.cloned.1.call-done
  229.4 1.7 multiply_reduce_fusion.8
  232.3 1.4 copy.6.refs_13_
  233.7 4.6 %multiply_reduce_fusion.1 = f32[8,512]{1,0:T(8,128)S(1)} fusion(bf16[8,768,512]{2,1,0:T(8,128)(2,1)} %bitcast.17), kind=kLoop, calls=%fused_computation.1 | loop fusion | flops 9433088 | bytes 6307840 | tf_op jit(solution)/shard_map/reduce_sum | solution.py:417
  238.3 1.4 collective-permute-start.21
  240.4 4.0 %multiply_reduce_fusion = f32[8,512]{1,0:T(8,128)S(1)} fusion(bf16[8,1536,512]{2,1,0:T(8,128)(2,1)} %bitcast.10), kind=kLoop, calls=%fused_computation | loop fusion | flops 9433088 | bytes 6307840 | tf_op jit(solution)/shard_map/reduce_sum | solution.py:417
  245.1 53.3 %first_terms.1.refs_12_ = f32[2048,32,128]{2,1,0:T(8,128)} custom-call(s32[5]{0:T(128)} %pad_add_fusion.info_ref, bf16[2048,384]{1,0:T(8,128)(2,1)} %copy-done.1, bf16[2048,384]{1,0:T(8,128)(2,1)} %copy-done.2, bf16[512,768]{1,0:T(8,128)(2,1)} %get-tuple-element.57.refs_2_, bf16[512,768]{1,0:T(8,128)(2,1)} %collective-permute-done.14.refs_3_, ...), custom_call_target="tpu_custom_call" | custom-call | flops 25769803776 | bytes 100663296 | tf_op jit(solution)/shard_map/first_terms/pallas_call | solution.py:292
  298.4 7.3 %collective-permute-done.20.refs_4_ = bf16[512,768]{1,0:T(8,128)(2,1)S(1)} collective-permute-done((bf16[512,768]{1,0:T(8,128)(2,1)S(1)}, bf16[512,768]{1,0:T(8,128)(2,1)S(1)}, u32[]{:S(2)}, u32[]{:S(2)}) %collective-permute-start.20) | collective-permute-done | bytes 786464 | tf_op jit(solution)/shard_map/ppermute | solution.py:361
  306.8 62.4 %last_terms.1 = f32[2048,32,128]{2,1,0:T(8,128)} custom-call(s32[5]{0:T(128)} %pad_add_fusion.info_ref, bf16[2048,384]{1,0:T(8,128)(2,1)} %copy-done.3, bf16[2048,384]{1,0:T(8,128)(2,1)} %copy-done.4, bf16[512,768]{1,0:T(8,128)(2,1)} %copy-done.19, bf16[512,768]{1,0:T(8,128)(2,1)} %copy-done.26, bf16[512,768]{1,0:T(8,128)(2,1)} %copy-done.25, ...), custom_call_target="tpu_custom_call" | custom-call | flops 25769803776 | bytes 100663296 | tf_op jit(solution)/shard_map/last_terms/pallas_call | solution.py:292
  (104 shorter events, 16.9 us)
Async XLA Ops:
  6.5 144.6 %all-gather.7.cloned.1.call-start = ((), (), s32[]{:S(2)}) async-start(), calls=%async_computation | async-start | bytes 7077888 | tf_op jit(solution)/shard_map/all_gather | solution.py:367
  8.1 40.7 %copy-start.12 = (bf16[192,2048]{1,0:T(8,128)(2,1)}, bf16[192,2048]{1,0:T(8,128)(2,1)S(1)}, u32[]{:S(2)}) copy-start(bf16[192,2048]{1,0:T(8,128)(2,1)S(1)} %get-tuple-element.76.refs_0_) | copy-start | bytes 2359300
  8.1 51.2 %copy-start.10 = (bf16[192,2048]{1,0:T(8,128)(2,1)}, bf16[192,2048]{1,0:T(8,128)(2,1)S(1)}, u32[]{:S(2)}) copy-start(bf16[192,2048]{1,0:T(8,128)(2,1)S(1)} %get-tuple-element.75.refs_1_) | copy-start | bytes 2359300
  8.1 30.0 %collective-permute-start.1 = (bf16[192,2048]{1,0:T(8,128)(2,1)S(1)}, bf16[192,2048]{1,0:T(8,128)(2,1)S(1)}, u32[]{:S(2)}, u32[]{:S(2)}) collective-permute-start(bf16[192,2048]{1,0:T(8,128)(2,1)S(1)} %get-tuple-element.75.refs_1_), channel_id=1, source_target_pairs={{0,1},{1,2},{2,3},{3,0},{4,5},{5,6},{6,7},{7,4},{8,9},{9,10},{10,1... | collective-permute-start | bytes 2359304 | tf_op jit(solution)/shard_map/ppermute | solution.py:354
  11.2 36.4 %collective-permute-start = (bf16[192,2048]{1,0:T(8,128)(2,1)S(1)}, bf16[192,2048]{1,0:T(8,128)(2,1)S(1)}, u32[]{:S(2)}, u32[]{:S(2)}) collective-permute-start(bf16[192,2048]{1,0:T(8,128)(2,1)S(1)} %get-tuple-element.76.refs_0_), channel_id=1, source_target_pairs={{0,1},{1,2},{2,3},{3,0},{4,5},{5,6},{6,7},{7,4},{8,9},{9,10},{10,1... | collective-permute-start | bytes 2359304 | tf_op jit(solution)/shard_map/ppermute | solution.py:354
  31.9 6.2 %copy-start = (bf16[8,2048,512]{2,1,0:T(8,128)(2,1)}, bf16[8,2048,512]{2,1,0:T(8,128)(2,1)S(1)}, u32[]{:S(2)}) copy-start(bf16[8,2048,512]{2,1,0:T(8,128)(2,1)S(1)} %omega_to_bf16.1.refs_4_) | copy-start | bytes 50331652
  38.1 43.3 %copy-start.5 = (bf16[192,2048]{1,0:T(8,128)(2,1)}, bf16[192,2048]{1,0:T(8,128)(2,1)S(1)}, u32[]{:S(2)}) copy-start(bf16[192,2048]{1,0:T(8,128)(2,1)S(1)} %collective-permute-done.1.refs_3_.refs_1_) | copy-start | bytes 2359300
  47.6 15.9 %copy-start.7 = (bf16[192,2048]{1,0:T(8,128)(2,1)}, bf16[192,2048]{1,0:T(8,128)(2,1)S(1)}, u32[]{:S(2)}) copy-start(bf16[192,2048]{1,0:T(8,128)(2,1)S(1)} %collective-permute-done.refs_2_.refs_0_) | copy-start | bytes 2359300
  48.7 179.3 %all-gather.9.cloned.1.call-start = ((), (), s32[]{:S(2)}) async-start(), calls=%async_computation.1 | async-start | bytes 14155776 | tf_op jit(solution)/shard_map/all_gather | solution.py:367
  59.3 22.1 %collective-permute-start.9 = (bf16[4,768,512]{2,1,0:T(8,128)(2,1)}, bf16[4,768,512]{2,1,0:T(8,128)(2,1)S(1)}, u32[]{:S(2)}, u32[]{:S(2)}) collective-permute-start(bf16[4,768,512]{2,1,0:T(8,128)(2,1)} %products_sent.3), channel_id=1, source_target_pairs={{0,4},{4,0},{8,12},{12,8},{16,20},{20,16},{24,28},{28,24},{1,5},{5... | collective-permute-start | bytes 9437192 | tf_op jit(solution)/shard_map/ppermute | solution.py:131
  59.3 22.1 %collective-permute-start.2 = (bf16[192,2048]{1,0:T(8,128)(2,1)S(1)}, bf16[192,2048]{1,0:T(8,128)(2,1)S(1)}, u32[]{:S(2)}, u32[]{:S(2)}) collective-permute-start(bf16[192,2048]{1,0:T(8,128)(2,1)S(1)} %collective-permute-done.refs_2_.refs_0_), channel_id=1, source_target_pairs={{0,1},{1,2},{2,3},{3,0},{4,5},{5,6},{6,7},{7,4},{8,9},{9,10},{10,1... | collective-permute-start | bytes 2359304 | tf_op jit(solution)/shard_map/ppermute | solution.py:354
  59.3 1.1 copy-start.13
  61.3 1.2 copy-start.1
  62.5 20.6 %copy-start.11 = (bf16[192,2048]{1,0:T(8,128)(2,1)S(1)}, bf16[192,2048]{1,0:T(8,128)(2,1)}, u32[]{:S(2)}) copy-start(bf16[192,2048]{1,0:T(8,128)(2,1)} %copy-done.10) | copy-start | bytes 2359300
  62.5 20.6 %copy-start.14 = (bf16[192,2048]{1,0:T(8,128)(2,1)S(1)}, bf16[192,2048]{1,0:T(8,128)(2,1)}, u32[]{:S(2)}) copy-start(bf16[192,2048]{1,0:T(8,128)(2,1)} %copy-done.12) | copy-start | bytes 2359300
  62.5 36.5 %collective-permute-start.3 = (bf16[192,2048]{1,0:T(8,128)(2,1)S(1)}, bf16[192,2048]{1,0:T(8,128)(2,1)S(1)}, u32[]{:S(2)}, u32[]{:S(2)}) collective-permute-start(bf16[192,2048]{1,0:T(8,128)(2,1)S(1)} %collective-permute-done.1.refs_3_.refs_1_), channel_id=1, source_target_pairs={{0,1},{1,2},{2,3},{3,0},{4,5},{5,6},{6,7},{7,4},{8,9},{9,10},{10,1... | collective-permute-start | bytes 2359304 | tf_op jit(solution)/shard_map/ppermute | solution.py:354
  81.5 33.7 %collective-permute-start.4 = (bf16[192,2048]{1,0:T(8,128)(2,1)S(1)}, bf16[192,2048]{1,0:T(8,128)(2,1)S(1)}, u32[]{:S(2)}, u32[]{:S(2)}) collective-permute-start(bf16[192,2048]{1,0:T(8,128)(2,1)S(1)} %collective-permute-done.2.refs_0_), channel_id=1, source_target_pairs={{0,1},{1,2},{2,3},{3,0},{4,5},{5,6},{6,7},{7,4},{8,9},{9,10},{10,1... | collective-permute-start | bytes 2359304 | tf_op jit(solution)/shard_map/ppermute | solution.py:354
  81.5 1.6 copy-start.27
  95.8 19.4 %collective-permute-start.10 = (bf16[2,384,512]{2,1,0:T(8,128)(2,1)S(1)}, bf16[2,384,512]{2,1,0:T(8,128)(2,1)S(1)}, u32[]{:S(2)}, u32[]{:S(2)}) collective-permute-start(bf16[2,384,512]{2,1,0:T(8,128)(2,1)S(1)} %get-tuple-element.46), channel_id=1, source_target_pairs={{0,8},{4,12},{8,0},{12,4},{16,24},{20,28},{24,16},{28,20},{1,9},{5... | collective-permute-start | bytes 2359304 | tf_op jit(solution)/shard_map/ppermute | solution.py:211
  97.3 18.5 %collective-permute-start.11 = (bf16[2,384,512]{2,1,0:T(8,128)(2,1)S(1)}, bf16[2,384,512]{2,1,0:T(8,128)(2,1)S(1)}, u32[]{:S(2)}, u32[]{:S(2)}) collective-permute-start(bf16[2,384,512]{2,1,0:T(8,128)(2,1)S(1)} %get-tuple-element.47), channel_id=1, source_target_pairs={{0,16},{4,20},{8,24},{12,28},{16,0},{20,4},{24,8},{28,12},{1,17},{... | collective-permute-start | bytes 2359304 | tf_op jit(solution)/shard_map/ppermute | solution.py:211
  98.9 32.7 %collective-permute-start.5 = (bf16[192,2048]{1,0:T(8,128)(2,1)S(1)}, bf16[192,2048]{1,0:T(8,128)(2,1)S(1)}, u32[]{:S(2)}, u32[]{:S(2)}) collective-permute-start(bf16[192,2048]{1,0:T(8,128)(2,1)S(1)} %collective-permute-done.3.refs_1_), channel_id=1, source_target_pairs={{0,1},{1,2},{2,3},{3,0},{4,5},{5,6},{6,7},{7,4},{8,9},{9,10},{10,1... | collective-permute-start | bytes 2359304 | tf_op jit(solution)/shard_map/ppermute | solution.py:354
  115.8 1.4 copy-start.17
  117.2 1.4 copy-start.18
  118.8 13.5 %collective-permute-start.12 = (bf16[1,384,512]{2,1,0:T(8,128)(2,1)S(1)}, bf16[1,384,512]{2,1,0:T(8,128)(2,1)S(1)}, u32[]{:S(2)}, u32[]{:S(2)}) collective-permute-start(bf16[1,384,512]{2,1,0:T(8,128)(2,1)S(1)} %get-tuple-element.52), channel_id=1, source_target_pairs={{0,16},{4,20},{8,24},{12,28},{16,0},{20,4},{24,8},{28,12},{1,17},{... | collective-permute-start | bytes 1179656 | tf_op jit(solution)/shard_map/ppermute | solution.py:211
  120.5 11.9 %collective-permute-start.13 = (bf16[1,384,512]{2,1,0:T(8,128)(2,1)S(1)}, bf16[1,384,512]{2,1,0:T(8,128)(2,1)S(1)}, u32[]{:S(2)}, u32[]{:S(2)}) collective-permute-start(bf16[1,384,512]{2,1,0:T(8,128)(2,1)S(1)} %get-tuple-element.53), channel_id=1, source_target_pairs={{0,8},{4,12},{8,0},{12,4},{16,24},{20,28},{24,16},{28,20},{1,9},{5... | collective-permute-start | bytes 1179656 | tf_op jit(solution)/shard_map/ppermute | solution.py:211
  134.5 171.3 %all-gather.11.cloned.1.call-start = ((), (), s32[]{:S(2)}) async-start(), calls=%async_computation.2 | async-start | bytes 7077888 | tf_op jit(solution)/shard_map/all_gather | solution.py:367
  145.2 6.0 %collective-permute-start.6 = (bf16[4,768,512]{2,1,0:T(8,128)(2,1)}, bf16[4,768,512]{2,1,0:T(8,128)(2,1)}, u32[]{:S(2)}, u32[]{:S(2)}) collective-permute-start(bf16[4,768,512]{2,1,0:T(8,128)(2,1)} %products_sent.2), channel_id=1, source_target_pairs={{0,4},{4,0},{8,12},{12,8},{16,20},{20,16},{24,28},{28,24},{1,5},{5... | collective-permute-start | bytes 9437192 | tf_op jit(solution)/shard_map/ppermute | solution.py:131
  146.0 1.2 copy-start.3
  147.9 1.2 copy-start.4
  149.1 22.5 %collective-permute-start.14 = (bf16[512,768]{1,0:T(8,128)(2,1)}, bf16[512,768]{1,0:T(8,128)(2,1)}, u32[]{:S(2)}, u32[]{:S(2)}) collective-permute-start(bf16[512,768]{1,0:T(8,128)(2,1)} %get-tuple-element.57.refs_2_), channel_id=1, source_target_pairs={{0,1},{1,2},{2,3},{3,0},{4,5},{5,6},{6,7},{7,4},{8,9},{9,10},{10,1... | collective-permute-start | bytes 2359304 | tf_op jit(solution)/shard_map/ppermute | solution.py:361
  162.7 33.8 %collective-permute-start.7 = (bf16[2,384,512]{2,1,0:T(8,128)(2,1)S(1)}, bf16[2,384,512]{2,1,0:T(8,128)(2,1)S(1)}, u32[]{:S(2)}, u32[]{:S(2)}) collective-permute-start(bf16[2,384,512]{2,1,0:T(8,128)(2,1)S(1)} %get-tuple-element.42), channel_id=1, source_target_pairs={{0,8},{4,12},{8,0},{12,4},{16,24},{20,28},{24,16},{28,20},{1,9},{5... | collective-permute-start | bytes 2359304 | tf_op jit(solution)/shard_map/ppermute | solution.py:211
  164.2 35.2 %collective-permute-start.8 = (bf16[2,384,512]{2,1,0:T(8,128)(2,1)S(1)}, bf16[2,384,512]{2,1,0:T(8,128)(2,1)S(1)}, u32[]{:S(2)}, u32[]{:S(2)}) collective-permute-start(bf16[2,384,512]{2,1,0:T(8,128)(2,1)S(1)} %get-tuple-element.43), channel_id=1, source_target_pairs={{0,16},{4,20},{8,24},{12,28},{16,0},{20,4},{24,8},{28,12},{1,17},{... | collective-permute-start | bytes 2359304 | tf_op jit(solution)/shard_map/ppermute | solution.py:211
  165.7 39.3 %collective-permute-start.18 = (bf16[512,768]{1,0:T(8,128)(2,1)}, bf16[512,768]{1,0:T(8,128)(2,1)S(1)}, u32[]{:S(2)}, u32[]{:S(2)}) collective-permute-start(bf16[512,768]{1,0:T(8,128)(2,1)} %get-tuple-element.57.refs_2_), channel_id=1, source_target_pairs={{0,3},{1,0},{2,1},{3,2},{4,7},{5,4},{6,5},{7,6},{8,11},{9,8},{10,9... | collective-permute-start | bytes 2359304 | tf_op jit(solution)/shard_map/ppermute | solution.py:361
  167.5 54.1 %collective-permute-start.17 = (bf16[512,768]{1,0:T(8,128)(2,1)}, bf16[512,768]{1,0:T(8,128)(2,1)S(1)}, u32[]{:S(2)}, u32[]{:S(2)}) collective-permute-start(bf16[512,768]{1,0:T(8,128)(2,1)} %get-tuple-element.57.refs_2_), channel_id=1, source_target_pairs={{0,2},{1,3},{2,0},{3,1},{4,6},{5,7},{6,4},{7,5},{8,10},{9,11},{10,... | collective-permute-start | bytes 2359304 | tf_op jit(solution)/shard_map/ppermute | solution.py:361
  199.4 1.4 copy-start.15
  200.8 1.6 copy-start.16
  202.7 19.5 %collective-permute-start.15 = (bf16[1,384,512]{2,1,0:T(8,128)(2,1)S(1)}, bf16[1,384,512]{2,1,0:T(8,128)(2,1)S(1)}, u32[]{:S(2)}, u32[]{:S(2)}) collective-permute-start(bf16[1,384,512]{2,1,0:T(8,128)(2,1)S(1)} %get-tuple-element.62), channel_id=1, source_target_pairs={{0,16},{4,20},{8,24},{12,28},{16,0},{20,4},{24,8},{28,12},{1,17},{... | collective-permute-start | bytes 1179656 | tf_op jit(solution)/shard_map/ppermute | solution.py:211
  205.1 19.0 %collective-permute-start.16 = (bf16[1,384,512]{2,1,0:T(8,128)(2,1)S(1)}, bf16[1,384,512]{2,1,0:T(8,128)(2,1)S(1)}, u32[]{:S(2)}, u32[]{:S(2)}) collective-permute-start(bf16[1,384,512]{2,1,0:T(8,128)(2,1)S(1)} %get-tuple-element.63), channel_id=1, source_target_pairs={{0,8},{4,12},{8,0},{12,4},{16,24},{20,28},{24,16},{28,20},{1,9},{5... | collective-permute-start | bytes 1179656 | tf_op jit(solution)/shard_map/ppermute | solution.py:211
  205.1 19.0 %copy-start.22 = (bf16[512,768]{1,0:T(8,128)(2,1)}, bf16[512,768]{1,0:T(8,128)(2,1)S(1)}, u32[]{:S(2)}) copy-start(bf16[512,768]{1,0:T(8,128)(2,1)S(1)} %collective-permute-done.18.refs_5_) | copy-start | bytes 2359300
  221.6 2.4 copy-start.23
  228.0 3.2 copy-start.6
  228.0 3.2 copy-start.9
  233.7 4.6 %copy-start.20 = (bf16[512,768]{1,0:T(8,128)(2,1)S(1)}, bf16[512,768]{1,0:T(8,128)(2,1)}, u32[]{:S(2)}) copy-start(bf16[512,768]{1,0:T(8,128)(2,1)} %copy-done.19) | copy-start | bytes 2359300
  238.3 60.1 %collective-permute-start.21 = (bf16[512,768]{1,0:T(8,128)(2,1)S(1)}, bf16[512,768]{1,0:T(8,128)(2,1)S(1)}, u32[]{:S(2)}, u32[]{:S(2)}) collective-permute-start(bf16[512,768]{1,0:T(8,128)(2,1)S(1)} %copy-done.20), channel_id=1, source_target_pairs={{0,3},{1,0},{2,1},{3,2},{4,7},{5,4},{6,5},{7,6},{8,11},{9,8},{10,9... | collective-permute-start | bytes 2359304 | tf_op jit(solution)/shard_map/ppermute | solution.py:361
  239.7 66.0 %collective-permute-start.20 = (bf16[512,768]{1,0:T(8,128)(2,1)S(1)}, bf16[512,768]{1,0:T(8,128)(2,1)S(1)}, u32[]{:S(2)}, u32[]{:S(2)}) collective-permute-start(bf16[512,768]{1,0:T(8,128)(2,1)S(1)} %copy-done.20), channel_id=1, source_target_pairs={{0,2},{1,3},{2,0},{3,1},{4,6},{5,7},{6,4},{7,5},{8,10},{9,11},{10,... | collective-permute-start | bytes 2359304 | tf_op jit(solution)/shard_map/ppermute | solution.py:361
  239.7 66.0 %collective-permute-start.19 = (bf16[512,768]{1,0:T(8,128)(2,1)S(1)}, bf16[512,768]{1,0:T(8,128)(2,1)S(1)}, u32[]{:S(2)}, u32[]{:S(2)}) collective-permute-start(bf16[512,768]{1,0:T(8,128)(2,1)S(1)} %copy-done.20), channel_id=1, source_target_pairs={{0,1},{1,2},{2,3},{3,0},{4,5},{5,6},{6,7},{7,4},{8,9},{9,10},{10,1... | collective-permute-start | bytes 2359304 | tf_op jit(solution)/shard_map/ppermute | solution.py:361
  298.4 7.4 %copy-start.24 = (bf16[512,768]{1,0:T(8,128)(2,1)}, bf16[512,768]{1,0:T(8,128)(2,1)S(1)}, u32[]{:S(2)}) copy-start(bf16[512,768]{1,0:T(8,128)(2,1)S(1)} %collective-permute-done.21.refs_5_) | copy-start | bytes 2359300
  305.7 1.1 copy-start.26
  (5 other events, 4.9 us)
Sparse Core Ops, SparseCore 0:
  48.8 44.9 all-gather.6
  134.6 93.3 all-gather.8
  229.8 44.0 all-gather.10
where the time goes:
time: 377 us; the launch traced here: 376 us
  Pallas kernels  184 us (49%)
  waiting for transfers between devices  113 us (30%)
  local copies, waits for them, and re-layouts  30.6 us (8%)
  starting transfers between devices  20.7 us (5%)
  between operations  14.3 us (4%)
  other arithmetic  13.2 us (4%)
    pallas_call x2, Pallas kernels, update(): pl.pallas_call(functools.partial(update_kernel, sizes, group, sub_width,...  116 us
    ppermute x6, waiting for transfers between devices, advance(): done = lax.ppermute(xs[-2][len(xs[-1])], 'col', ring)  50 us
    ppermute x8, waiting for transfers between devices, sum_over_rows(): lax.ppermute(sent, 'row', row_partner(mask))  30.8 us
    ppermute x6, waiting for transfers between devices, to_distance(): lax.ppermute(y, 'col', [(c, (c + distance) % col_count) for c in range(co...  28 us
    unnamed x60, local copies, waits for them, and re-layouts  26.1 us
    pallas_call x2, Pallas kernels, pair_products(): pl.pallas_call(functools.partial(kept_kernel, count, bits), grid_spec=plt...  23.1 us
    pallas_call x2, Pallas kernels, pair_products(): pl.pallas_call(functools.partial(sent_kernel, count), grid_spec=pltpu.Pre...  21.2 us
    pallas_call x1, Pallas kernels, convert(): pl.pallas_call(convert_kernel, grid=(row_total // tile, lane_tiles // SUB...  19.2 us
  transfers between devices with their start and end apart: 25, of which 14 were waited for; matrix products, arithmetic and copies ran while one was open for 5% of the time, Pallas kernels for 32%

commit v1 on v0

--- a/solution.py
+++ b/solution.py
@@ -227,51 +227,71 @@
     sign_ref = refs[3] if last else None
     out_ref, cross_ref, rate_ref = refs[3 + last :]
     rows = omega_ref.shape[0]
-    cross = cross_ref.reshape(rows * SUBS, LANES)
     per_block = sub_width // LANES
     blocks = SUBS // per_block
-    distance = pl.program_id(1)
-
-    @pl.when(pl.program_id(0) == 0)
+    width = min(sub_width, 256)
+    pieces = [(b, at) for b in range(blocks) for at in range(0, sub_width, width)]
+    step = pl.program_id(0)
+    ending = step == pl.num_programs(0) - 1
+    distance = lax.rem(step, col_count)
+    before = jnp.maximum(step - 1, 0)
+    old_distance = lax.rem(before, col_count)
+    old_tile = lax.div(before, col_count)
+    new_cross = cross_ref.at[lax.rem(step, 2)].reshape(rows * SUBS, LANES)
+    old_cross = cross_ref.at[lax.rem(step + 1, 2)]
+
+    @pl.when(step < col_count)
     def _():
         rate = rate_ref.at[distance].reshape(rows * SUBS, LANES)
         for c in range(SUBS):
             rate[pl.ds(c, rows, stride=SUBS), :] = jnp.broadcast_to(row_ref[...], (rows, LANES))
 
+    def take_off(first_row, row_count):
+        col_rate = col_ref[...][None]
+        col_shift = col_rate * PENALTY
+        col_smooth = col_rate * scale
+        for first in range(first_row, first_row + row_count, 16):
+            span = slice(first, min(first + 16, first_row + row_count))
+            row_rate = rate_ref[old_distance, span]
+            trial = omega_ref[span] - (row_rate * col_smooth) * old_cross[span]
+            if last:
+                sign = sign_ref[span].astype(jnp.float32)
+                trial = sign * jnp.maximum(sign * trial - row_rate * col_shift, 0.0)
+            out_ref[span] = trial
+
+    share = rows // len(pieces)
     for value in range(col_count):
 
-        @pl.when(distance == value)
+        @pl.when(jnp.logical_and(distance == value, jnp.logical_not(ending)))
         def _():
             met = [x_cols[(group * per_group + s + value) % col_count] for s in range(per_group)]
             left = jnp.concatenate([x[...] for x in xs] + [ys[value][...]], axis=1)
-            for b in range(blocks):
-                right = jnp.concatenate([r[b] for r in (*y_cols, *met)], axis=0)
+            for k, (b, at) in enumerate(pieces):
+                right = jnp.concatenate(
+                    [r[b, :, at : at + width] for r in (*y_cols, *met)], axis=0
+                )
                 total = jnp.dot(left, right, preferred_element_type=jnp.float32)
-                for lane in range(0, sub_width, LANES):
-                    spot = pl.ds(b * per_block + lane // LANES, rows, stride=SUBS)
-                    cross[spot, :] = total[:, lane : lane + LANES]
-
-    col_rate = col_ref[...][None]
-    col_shift = col_rate * PENALTY
-    col_smooth = col_rate * scale
-    for first in range(0, rows, 64):
-        span = slice(first, min(first + 64, rows))
-        row_rate = rate_ref[distance, span]
-        trial = omega_ref[span] - (row_rate * col_smooth) * cross_ref[span]
-        if last:
-            sign = sign_ref[span].astype(jnp.float32)
-            trial = sign * jnp.maximum(sign * trial - row_rate * col_shift, 0.0)
-        out_ref[span] = trial
+                for lane in range(0, width, LANES):
+                    spot = pl.ds(b * per_block + (at + lane) // LANES, rows, stride=SUBS)
+                    new_cross[spot, :] = total[:, lane : lane + LANES]
+                take_off(k * share, share)
+
+    @pl.when(ending)
+    def _():
+        take_off(0, rows)
 
     if last:
-        @pl.when(jnp.logical_and(distance == 0, pl.program_id(0) == info_ref[0] // blocks))
+        diagonal = jnp.logical_and(old_distance == 0, old_tile == info_ref[0] // blocks)
+
+        @pl.when(jnp.logical_and(diagonal, step > 0))
         def _():
+            col_rate = col_ref[...][None]
             first_tile = info_ref[0] % blocks * per_block
-            for first in range(0, rows, 64):
-                span = slice(first, min(first + 64, rows))
+            for first in range(0, rows, 16):
+                span = slice(first, min(first + 16, rows))
                 shape = out_ref[span].shape
-                rate = rate_ref[distance, span] * col_rate
-                trial = omega_ref[span] - rate * (cross_ref[span] * scale)
+                rate = rate_ref[old_distance, span] * col_rate
+                trial = omega_ref[span] - rate * (old_cross[span] * scale)
                 value = 0.5 * (trial + jnp.sqrt(trial * trial + 4.0 * rate))
                 row_ids = lax.broadcasted_iota(jnp.int32, shape, 0) + first
                 tile_ids = lax.broadcasted_iota(jnp.int32, shape, 1) - first_tile
@@ -286,30 +306,50 @@
     blocks = SUBS * LANES // sub_width
     last = sign3 is not None
     sizes = (len(ys), len(xs))
-    grid_block = pl.BlockSpec((tile, SUBS, LANES), lambda j, d, p: (p[1 + d], j, 0))
+    planes = row_total // tile
+    total = planes * (lane_tiles // SUBS)
+
+    def new_tile(t):
+        t = jnp.minimum(t, total - 1)
+        return lax.div(t, planes), lax.rem(t, planes)
+
+    def old_tile(t):
+        t = jnp.maximum(t - 1, 0)
+        return lax.div(t, planes), lax.rem(t, planes)
+
+    def old_block(t, p):
+        j, d = old_tile(t)
+        return p[1 + d], j, 0
+
+    def new_rows(t, p):
+        return p[1 + new_tile(t)[1]], 0
+
+    grid_block = pl.BlockSpec((tile, SUBS, LANES), old_block)
     columns = list(y_cols) + list(x_cols)
     operands = [*xs, *ys, *[b for b, _ in columns], omega3, row_rate, col_rate]
     return pl.pallas_call(
         functools.partial(update_kernel, sizes, group, sub_width, scale, last),
         grid_spec=pltpu.PrefetchScalarGridSpec(
             num_scalar_prefetch=1,
-            grid=(lane_tiles // SUBS, row_total // tile),
-            in_specs=[pl.BlockSpec((tile, part), lambda j, d, p: (p[1 + d], 0)) for _ in xs]
-            + [pl.BlockSpec(y.shape, lambda j, d, p: (0, 0)) for y in ys]
+            grid=(total + 1,),
+            in_specs=[pl.BlockSpec((tile, part), new_rows) for _ in xs]
+            + [pl.BlockSpec(y.shape, lambda t, p: (0, 0)) for y in ys]
             + [
-                pl.BlockSpec((blocks, part, sub_width), lambda j, d, p, at=at: (j, at, 0))
+                pl.BlockSpec(
+                    (blocks, part, sub_width), lambda t, p, at=at: (new_tile(t)[0], at, 0)
+                )
                 for _, at in columns
             ]
             + [
                 grid_block,
-                pl.BlockSpec((tile, 1), lambda j, d, p: (p[1 + d], 0)),
-                pl.BlockSpec((SUBS, LANES), lambda j, d, p: (j, 0)),
+                pl.BlockSpec((tile, 1), new_rows),
+                pl.BlockSpec((SUBS, LANES), lambda t, p: (old_tile(t)[0], 0)),
             ]
             + [grid_block] * last,
             out_specs=grid_block,
             scratch_shapes=[
-                pltpu.VMEM((tile, SUBS, LANES), jnp.float32),
-                pltpu.VMEM((row_total // tile, tile, SUBS, LANES), jnp.float32),
+                pltpu.VMEM((2, tile, SUBS, LANES), jnp.float32),
+                pltpu.VMEM((planes, tile, SUBS, LANES), jnp.float32),
             ],
         ),
         out_shape=jax.ShapeDtypeStruct(omega3.shape, jnp.float32),
@@ -359,6 +399,11 @@
         if not distance:
             return y
         return lax.ppermute(y, "col", [(c, (c + distance) % col_count) for c in range(col_count)])
+
+    def square_sum(pieces, axis):
+        return sum(jnp.sum(jnp.square(p.astype(jnp.float32)), axis=axis) for p in pieces)
+
+    sums = []
 
     def complete(length):
         return len(xs) >= length and len(xs[length - 1]) == PIECES
@@ -397,6 +442,9 @@
                 done.append(y_planes[0][1])
             if y_planes and exchange == 2:
                 done.extend(y_planes[0][2:])
+                sums.append(square_sum([x for pieces in xs for x in pieces], 0))
+                sums.append(square_sum([x_cols[0][0]], 1))
+                done.extend(sums)
             return done
 
         share, turned = sum_over_rows(
@@ -413,15 +461,14 @@
     y_cols.append((last, 0))
     group_rows = part * per_group
 
-    def mean_square(pieces, axis):
-        total = sum(jnp.sum(jnp.square(p.astype(jnp.float32)), axis=axis) for p in pieces)
+    def scale_of(total):
         total = lax.optimization_barrier(total) / sample_total + 1e-06
         return lax.optimization_barrier(total.astype(jnp.bfloat16)).astype(jnp.float32)
 
-    x_pieces = [x for pieces in xs for x in pieces]
-    row_rate = (step_size[0] * lax.rsqrt(mean_square(x_pieces, 0)))[:, None]
-    col_rate = lax.rsqrt(mean_square([block[:, :group_rows] for block, _ in x_cols], 1))
-    col_rate = col_rate.reshape(lane_tiles, LANES)
+    row_sum, col_sum = sums
+    col_sum = col_sum + square_sum([block[:, :group_rows] for block, _ in x_cols[1:]], 1)
+    row_rate = (step_size[0] * lax.rsqrt(scale_of(row_sum)))[:, None]
+    col_rate = lax.rsqrt(scale_of(col_sum)).reshape(lane_tiles, LANES)
 
     planes = (col_index - jnp.arange(col_count, dtype=jnp.int32) + col_count) % col_count
     info = jnp.concatenate([row_index[None], planes])

time: 377 us -> 372 us (0.987)
  Pallas kernels: 184 us -> 190 us
  waiting for transfers between devices: 113 us -> 107 us
  other arithmetic: 13.2 us -> 8.75 us
  local copies, waits for them, and re-layouts: 30.6 us -> 26.8 us
    pallas_call x2, Pallas kernels: 116 us -> 120 us  [update(): pl.pallas_call(functools.partial(update_kernel, sizes, group, sub_width,...]
    reduce_sum x8, other arithmetic: 11.4 us -> 6.97 us  [square_sum(): jnp.sum(jnp.square(p.astype(jnp.float32)), axis=axis)]
    ppermute x8, waiting for transfers between devices: 30.8 us -> 27 us  [sum_over_rows(): lax.ppermute(sent, 'row', row_partner(mask))]
  transfers between devices with their start and end apart: 25 -> 25, of which waited for: 14 -> 12; matrix products, arithmetic and copies ran while one was open for 5% -> 4% of each run, Pallas kernels for 32% -> 34%
where the time goes in v1:
time: 372 us; the launch traced here: 370 us
  Pallas kernels  190 us (51%)
  waiting for transfers between devices  107 us (29%)
  local copies, waits for them, and re-layouts  26.8 us (7%)
  starting transfers between devices  24 us (6%)
  between operations  14.1 us (4%)
  other arithmetic  8.75 us (2%)
    pallas_call x2, Pallas kernels, update(): pl.pallas_call(functools.partial(update_kernel, sizes, group, sub_width,...  120 us
    ppermute x6, waiting for transfers between devices, advance(): done = lax.ppermute(xs[-2][len(xs[-1])], 'col', ring)  50 us
    ppermute x8, waiting for transfers between devices, sum_over_rows(): lax.ppermute(sent, 'row', row_partner(mask))  27 us
    ppermute x6, waiting for transfers between devices, to_distance(): lax.ppermute(y, 'col', [(c, (c + distance) % col_count) for c in range(co...  24.8 us
    pallas_call x2, Pallas kernels, pair_products(): pl.pallas_call(functools.partial(kept_kernel, count, bits), grid_spec=plt...  23.3 us
    unnamed x60, local copies, waits for them, and re-layouts  22.4 us
    pallas_call x2, Pallas kernels, pair_products(): pl.pallas_call(functools.partial(sent_kernel, count), grid_spec=pltpu.Pre...  21.2 us
    pallas_call x1, Pallas kernels, convert(): pl.pallas_call(convert_kernel, grid=(row_total // tile, lane_tiles // SUB...  19.2 us
  transfers between devices with their start and end apart: 25, of which 12 were waited for; matrix products, arithmetic and copies ran while one was open for 4% of the time, Pallas kernels for 34%

profile of v1, /device:TPU:0, one launch (start us, length us, event | category | flops | bytes accessed | tf_op | source)
XLA Modules:
  0.0 370.2 jit_solution(11750639305638661714)
XLA Ops:
  6.5 1.5 fusion.1
  8.0 3.1 collective-permute-start.1
  11.1 1.6 collective-permute-start
  12.7 19.2 %omega_to_bf16.1.refs_4_ = bf16[8,2048,512]{2,1,0:T(8,128)(2,1)S(1)} custom-call(f32[2048,32,128]{2,1,0:T(8,128)} %bitcast.22), custom_call_target="tpu_custom_call" | custom-call | bytes 50331648 | tf_op jit(solution)/shard_map/omega_to_bf16/pallas_call | solution.py:34
  31.9 6.2 %copy-done = bf16[8,2048,512]{2,1,0:T(8,128)(2,1)} copy-done((bf16[8,2048,512]{2,1,0:T(8,128)(2,1)}, bf16[8,2048,512]{2,1,0:T(8,128)(2,1)S(1)}, u32[]{:S(2)}) %copy-start) | copy-done | bytes 16777240
  38.1 9.5 %collective-permute-done.refs_2_.refs_0_ = bf16[192,2048]{1,0:T(8,128)(2,1)S(1)} collective-permute-done((bf16[192,2048]{1,0:T(8,128)(2,1)S(1)}, bf16[192,2048]{1,0:T(8,128)(2,1)S(1)}, u32[]{:S(2)}, u32[]{:S(2)}) %collective-permute-start) | collective-permute-done | bytes 786464 | tf_op jit(solution)/shard_map/ppermute | solution.py:394
  47.6 1.0 pad_maximum_fusion
  48.7 10.6 %products_sent.3 = bf16[4,768,512]{2,1,0:T(8,128)(2,1)} custom-call(s32[4]{0:T(128)S(1)} %get-tuple-element.73.order_ref, bf16[192,2048]{1,0:T(8,128)(2,1)S(1)} %get-tuple-element.76.refs_0_, bf16[192,2048]{1,0:T(8,128)(2,1)S(1)} %get-tuple-element.75.refs_1_, bf16[192,2048]{1,0:T(8,128)(2,1)S(1)} %collective-permute-done.refs_2_.refs_0_, ...), custom_call_target="tpu_custom_call" | custom-call | flops 6442450944 | bytes 14680064 | tf_op jit(solution)/shard_map/products_sent/pallas_call | solution.py:118
  59.3 1.1 copy-done.13
  61.2 1.2 copy-done.1
  62.4 1.0 collective-permute-start.3
  64.3 1.1 copy-done.2
  65.4 16.0 %collective-permute-done.2.refs_0_ = bf16[192,2048]{1,0:T(8,128)(2,1)S(1)} collective-permute-done((bf16[192,2048]{1,0:T(8,128)(2,1)S(1)}, bf16[192,2048]{1,0:T(8,128)(2,1)S(1)}, u32[]{:S(2)}, u32[]{:S(2)}) %collective-permute-start.2) | collective-permute-done | bytes 786464 | tf_op jit(solution)/shard_map/ppermute | solution.py:394
  81.4 1.6 copy-done.27
  83.1 1.1 copy-done.8
  84.2 11.5 %products_kept.3 = (bf16[2,384,512]{2,1,0:T(8,128)(2,1)S(1)}, f32[2,384,512]{2,1,0:T(8,128)}, bf16[2,384,512]{2,1,0:T(8,128)(2,1)S(1)}, f32[2,384,512]{2,1,0:T(8,128)}) custom-call(s32[4]{0:T(128)S(1)} %get-tuple-element.74.order_ref, bf16[192,2048]{1,0:T(8,128)(2,1)S(1)} %copy-done.14, bf16[192,2048]{1,0:T(8,128)(2,1)S(1)} %copy-done.11, ...), custom_call_target="tpu_custom_call" | custom-call | flops 6442450944 | bytes 14680064 | tf_op jit(solution)/shard_map/products_kept/pallas_call | solution.py:134
  95.8 1.5 collective-permute-start.10
  97.2 1.7 collective-permute-start.11
  98.9 16.2 %collective-permute-done.4.refs_0_.refs_2_ = bf16[192,2048]{1,0:T(8,128)(2,1)S(1)} collective-permute-done((bf16[192,2048]{1,0:T(8,128)(2,1)S(1)}, bf16[192,2048]{1,0:T(8,128)(2,1)S(1)}, u32[]{:S(2)}, u32[]{:S(2)}) %collective-permute-start.4) | collective-permute-done | bytes 786464 | tf_op jit(solution)/shard_map/ppermute | solution.py:394
  115.7 1.4 copy-done.17
  117.1 1.4 copy-done.18
  118.8 1.6 collective-permute-start.12
  120.4 0.8 collective-permute-start.13
  123.3 8.3 %collective-permute-done.5.refs_1_.refs_3_ = bf16[192,2048]{1,0:T(8,128)(2,1)S(1)} collective-permute-done((bf16[192,2048]{1,0:T(8,128)(2,1)S(1)}, bf16[192,2048]{1,0:T(8,128)(2,1)S(1)}, u32[]{:S(2)}, u32[]{:S(2)}) %collective-permute-start.5) | collective-permute-done | bytes 786464 | tf_op jit(solution)/shard_map/ppermute | solution.py:394
  132.3 1.1 share.2
  133.5 0.9 constant_dynamic-update-slice_fusion
  134.5 10.7 %products_sent.2 = bf16[4,768,512]{2,1,0:T(8,128)(2,1)} custom-call(s32[4]{0:T(128)S(1)} %get-tuple-element.73.order_ref, bf16[192,2048]{1,0:T(8,128)(2,1)S(1)} %collective-permute-done.2.refs_0_, bf16[192,2048]{1,0:T(8,128)(2,1)S(1)} %collective-permute-done.3.refs_1_, bf16[192,2048]{1,0:T(8,128)(2,1)S(1)} %collective-permute-done.4.refs_0_.refs_2_, ...), custom_call_target="tpu_custom_call" | custom-call | flops 6442450944 | bytes 14680064 | tf_op jit(solution)/shard_map/products_sent/pallas_call | solution.py:118
  147.7 1.2 copy-done.3
  149.6 1.1 copy-done.4
  151.2 11.8 %products_kept.2 = (bf16[2,384,512]{2,1,0:T(8,128)(2,1)S(1)}, f32[2,384,512]{2,1,0:T(8,128)}, bf16[2,384,512]{2,1,0:T(8,128)(2,1)S(1)}, f32[2,384,512]{2,1,0:T(8,128)}) custom-call(s32[4]{0:T(128)S(1)} %get-tuple-element.74.order_ref, bf16[192,2048]{1,0:T(8,128)(2,1)S(1)} %collective-permute-done.2.refs_0_, ...), custom_call_target="tpu_custom_call" | custom-call | flops 6442450944 | bytes 14680064 | tf_op jit(solution)/shard_map/products_kept/pallas_call | solution.py:134
  162.9 1.5 collective-permute-start.7
  164.4 1.5 collective-permute-start.8
  166.5 3.7 collective-permute-start.18
  170.4 3.0 collective-permute-done.14.refs_3_
  173.4 23.7 %collective-permute-done.7.refs_1_ = bf16[2,384,512]{2,1,0:T(8,128)(2,1)S(1)} collective-permute-done((bf16[2,384,512]{2,1,0:T(8,128)(2,1)S(1)}, bf16[2,384,512]{2,1,0:T(8,128)(2,1)S(1)}, u32[]{:S(2)}, u32[]{:S(2)}) %collective-permute-start.7) | collective-permute-done | bytes 786464 | tf_op jit(solution)/shard_map/ppermute | solution.py:211
  197.1 2.7 collective-permute-done.8.refs_3_
  200.0 2.4 collective-permute-start.15
  202.5 1.2 multiply_reduce_fusion.1
  203.7 18.9 %collective-permute-done.17.refs_4_ = bf16[512,768]{1,0:T(8,128)(2,1)S(1)} collective-permute-done((bf16[512,768]{1,0:T(8,128)(2,1)}, bf16[512,768]{1,0:T(8,128)(2,1)S(1)}, u32[]{:S(2)}, u32[]{:S(2)}) %collective-permute-start.17) | collective-permute-done | bytes 786464 | tf_op jit(solution)/shard_map/ppermute | solution.py:401
  222.6 1.1 share.3
  223.8 4.4 %all-gather.9.cloned.1.call-done = bf16[12288,512]{1,0:T(8,128)(2,1)} async-done(((bf16[1536,512]{1,0:T(8,128)(2,1)}), bf16[12288,512]{1,0:T(8,128)(2,1)}) %all-gather.9.cloned.1.call-update) | async-done | bytes 12582928 | tf_op jit(solution)/shard_map/all_gather | solution.py:412
  229.6 1.4 copy.6.refs_13_
  230.9 2.8 collective-permute-start.21
  234.3 4.4 %multiply_reduce_fusion = f32[8,512]{1,0:T(8,128)S(1)} fusion(bf16[8,1536,512]{2,1,0:T(8,128)(2,1)} %bitcast.10), kind=kLoop, calls=%fused_computation | loop fusion | flops 9433088 | bytes 6307840 | tf_op jit(solution)/shard_map/reduce_sum | solution.py:404
  239.3 56.6 %first_terms.1.refs_12_ = f32[2048,32,128]{2,1,0:T(8,128)} custom-call(s32[5]{0:T(128)} %pad_add_fusion.info_ref, bf16[2048,384]{1,0:T(8,128)(2,1)} %copy-done.1, bf16[2048,384]{1,0:T(8,128)(2,1)} %copy-done.2, bf16[512,768]{1,0:T(8,128)(2,1)} %get-tuple-element.57.refs_2_, bf16[512,768]{1,0:T(8,128)(2,1)} %collective-permute-done.14.refs_3_, ...), custom_call_target="tpu_custom_call" | custom-call | flops 25769803776 | bytes 100663296 | tf_op jit(solution)/shard_map/first_terms/pallas_call | solution.py:330
  295.9 2.9 collective-permute-done.20.refs_4_
  298.9 0.8 copy-done.25
  300.0 63.6 %last_terms.1 = f32[2048,32,128]{2,1,0:T(8,128)} custom-call(s32[5]{0:T(128)} %pad_add_fusion.info_ref, bf16[2048,384]{1,0:T(8,128)(2,1)} %copy-done.3, bf16[2048,384]{1,0:T(8,128)(2,1)} %copy-done.4, bf16[512,768]{1,0:T(8,128)(2,1)} %copy-done.19, bf16[512,768]{1,0:T(8,128)(2,1)} %copy-done.26, bf16[512,768]{1,0:T(8,128)(2,1)} %copy-done.25, ...), custom_call_target="tpu_custom_call" | custom-call | flops 25769803776 | bytes 100663296 | tf_op jit(solution)/shard_map/last_terms/pallas_call | solution.py:330
  (104 shorter events, 12.3 us)
Async XLA Ops:
  6.5 144.6 %all-gather.7.cloned.1.call-start = ((), (), s32[]{:S(2)}) async-start(), calls=%async_computation | async-start | bytes 7077888 | tf_op jit(solution)/shard_map/all_gather | solution.py:412
  8.0 40.7 %copy-start.12 = (bf16[192,2048]{1,0:T(8,128)(2,1)}, bf16[192,2048]{1,0:T(8,128)(2,1)S(1)}, u32[]{:S(2)}) copy-start(bf16[192,2048]{1,0:T(8,128)(2,1)S(1)} %get-tuple-element.76.refs_0_) | copy-start | bytes 2359300
  8.0 51.3 %copy-start.10 = (bf16[192,2048]{1,0:T(8,128)(2,1)}, bf16[192,2048]{1,0:T(8,128)(2,1)S(1)}, u32[]{:S(2)}) copy-start(bf16[192,2048]{1,0:T(8,128)(2,1)S(1)} %get-tuple-element.75.refs_1_) | copy-start | bytes 2359300
  8.0 30.0 %collective-permute-start.1 = (bf16[192,2048]{1,0:T(8,128)(2,1)S(1)}, bf16[192,2048]{1,0:T(8,128)(2,1)S(1)}, u32[]{:S(2)}, u32[]{:S(2)}) collective-permute-start(bf16[192,2048]{1,0:T(8,128)(2,1)S(1)} %get-tuple-element.75.refs_1_), channel_id=1, source_target_pairs={{0,1},{1,2},{2,3},{3,0},{4,5},{5,6},{6,7},{7,4},{8,9},{9,10},{10,1... | collective-permute-start | bytes 2359304 | tf_op jit(solution)/shard_map/ppermute | solution.py:394
  11.1 36.4 %collective-permute-start = (bf16[192,2048]{1,0:T(8,128)(2,1)S(1)}, bf16[192,2048]{1,0:T(8,128)(2,1)S(1)}, u32[]{:S(2)}, u32[]{:S(2)}) collective-permute-start(bf16[192,2048]{1,0:T(8,128)(2,1)S(1)} %get-tuple-element.76.refs_0_), channel_id=1, source_target_pairs={{0,1},{1,2},{2,3},{3,0},{4,5},{5,6},{6,7},{7,4},{8,9},{9,10},{10,1... | collective-permute-start | bytes 2359304 | tf_op jit(solution)/shard_map/ppermute | solution.py:394
  31.8 6.2 %copy-start = (bf16[8,2048,512]{2,1,0:T(8,128)(2,1)}, bf16[8,2048,512]{2,1,0:T(8,128)(2,1)S(1)}, u32[]{:S(2)}) copy-start(bf16[8,2048,512]{2,1,0:T(8,128)(2,1)S(1)} %omega_to_bf16.1.refs_4_) | copy-start | bytes 50331652
  38.1 43.4 %copy-start.5 = (bf16[192,2048]{1,0:T(8,128)(2,1)}, bf16[192,2048]{1,0:T(8,128)(2,1)S(1)}, u32[]{:S(2)}) copy-start(bf16[192,2048]{1,0:T(8,128)(2,1)S(1)} %collective-permute-done.1.refs_3_.refs_1_) | copy-start | bytes 2359300
  47.5 15.9 %copy-start.7 = (bf16[192,2048]{1,0:T(8,128)(2,1)}, bf16[192,2048]{1,0:T(8,128)(2,1)S(1)}, u32[]{:S(2)}) copy-start(bf16[192,2048]{1,0:T(8,128)(2,1)S(1)} %collective-permute-done.refs_2_.refs_0_) | copy-start | bytes 2359300
  48.6 179.6 %all-gather.9.cloned.1.call-start = ((), (), s32[]{:S(2)}) async-start(), calls=%async_computation.1 | async-start | bytes 14155776 | tf_op jit(solution)/shard_map/all_gather | solution.py:412
  59.3 22.1 %collective-permute-start.9 = (bf16[4,768,512]{2,1,0:T(8,128)(2,1)}, bf16[4,768,512]{2,1,0:T(8,128)(2,1)S(1)}, u32[]{:S(2)}, u32[]{:S(2)}) collective-permute-start(bf16[4,768,512]{2,1,0:T(8,128)(2,1)} %products_sent.3), channel_id=1, source_target_pairs={{0,4},{4,0},{8,12},{12,8},{16,20},{20,16},{24,28},{28,24},{1,5},{5... | collective-permute-start | bytes 9437192 | tf_op jit(solution)/shard_map/ppermute | solution.py:131
  59.3 22.1 %collective-permute-start.2 = (bf16[192,2048]{1,0:T(8,128)(2,1)S(1)}, bf16[192,2048]{1,0:T(8,128)(2,1)S(1)}, u32[]{:S(2)}, u32[]{:S(2)}) collective-permute-start(bf16[192,2048]{1,0:T(8,128)(2,1)S(1)} %collective-permute-done.refs_2_.refs_0_), channel_id=1, source_target_pairs={{0,1},{1,2},{2,3},{3,0},{4,5},{5,6},{6,7},{7,4},{8,9},{9,10},{10,1... | collective-permute-start | bytes 2359304 | tf_op jit(solution)/shard_map/ppermute | solution.py:394
  61.2 1.2 copy-start.1
  62.4 20.6 %copy-start.11 = (bf16[192,2048]{1,0:T(8,128)(2,1)S(1)}, bf16[192,2048]{1,0:T(8,128)(2,1)}, u32[]{:S(2)}) copy-start(bf16[192,2048]{1,0:T(8,128)(2,1)} %copy-done.10) | copy-start | bytes 2359300
  62.4 20.6 %copy-start.14 = (bf16[192,2048]{1,0:T(8,128)(2,1)S(1)}, bf16[192,2048]{1,0:T(8,128)(2,1)}, u32[]{:S(2)}) copy-start(bf16[192,2048]{1,0:T(8,128)(2,1)} %copy-done.12) | copy-start | bytes 2359300
  62.4 36.5 %collective-permute-start.3 = (bf16[192,2048]{1,0:T(8,128)(2,1)S(1)}, bf16[192,2048]{1,0:T(8,128)(2,1)S(1)}, u32[]{:S(2)}, u32[]{:S(2)}) collective-permute-start(bf16[192,2048]{1,0:T(8,128)(2,1)S(1)} %collective-permute-done.1.refs_3_.refs_1_), channel_id=1, source_target_pairs={{0,1},{1,2},{2,3},{3,0},{4,5},{5,6},{6,7},{7,4},{8,9},{9,10},{10,1... | collective-permute-start | bytes 2359304 | tf_op jit(solution)/shard_map/ppermute | solution.py:394
  81.4 33.7 %collective-permute-start.4 = (bf16[192,2048]{1,0:T(8,128)(2,1)S(1)}, bf16[192,2048]{1,0:T(8,128)(2,1)S(1)}, u32[]{:S(2)}, u32[]{:S(2)}) collective-permute-start(bf16[192,2048]{1,0:T(8,128)(2,1)S(1)} %collective-permute-done.2.refs_0_), channel_id=1, source_target_pairs={{0,1},{1,2},{2,3},{3,0},{4,5},{5,6},{6,7},{7,4},{8,9},{9,10},{10,1... | collective-permute-start | bytes 2359304 | tf_op jit(solution)/shard_map/ppermute | solution.py:394
  81.4 1.6 copy-start.27
  95.8 19.4 %collective-permute-start.10 = (bf16[2,384,512]{2,1,0:T(8,128)(2,1)S(1)}, bf16[2,384,512]{2,1,0:T(8,128)(2,1)S(1)}, u32[]{:S(2)}, u32[]{:S(2)}) collective-permute-start(bf16[2,384,512]{2,1,0:T(8,128)(2,1)S(1)} %get-tuple-element.46), channel_id=1, source_target_pairs={{0,8},{4,12},{8,0},{12,4},{16,24},{20,28},{24,16},{28,20},{1,9},{5... | collective-permute-start | bytes 2359304 | tf_op jit(solution)/shard_map/ppermute | solution.py:211
  97.2 18.5 %collective-permute-start.11 = (bf16[2,384,512]{2,1,0:T(8,128)(2,1)S(1)}, bf16[2,384,512]{2,1,0:T(8,128)(2,1)S(1)}, u32[]{:S(2)}, u32[]{:S(2)}) collective-permute-start(bf16[2,384,512]{2,1,0:T(8,128)(2,1)S(1)} %get-tuple-element.47), channel_id=1, source_target_pairs={{0,16},{4,20},{8,24},{12,28},{16,0},{20,4},{24,8},{28,12},{1,17},{... | collective-permute-start | bytes 2359304 | tf_op jit(solution)/shard_map/ppermute | solution.py:211
  98.9 32.7 %collective-permute-start.5 = (bf16[192,2048]{1,0:T(8,128)(2,1)S(1)}, bf16[192,2048]{1,0:T(8,128)(2,1)S(1)}, u32[]{:S(2)}, u32[]{:S(2)}) collective-permute-start(bf16[192,2048]{1,0:T(8,128)(2,1)S(1)} %collective-permute-done.3.refs_1_), channel_id=1, source_target_pairs={{0,1},{1,2},{2,3},{3,0},{4,5},{5,6},{6,7},{7,4},{8,9},{9,10},{10,1... | collective-permute-start | bytes 2359304 | tf_op jit(solution)/shard_map/ppermute | solution.py:394
  115.7 1.4 copy-start.17
  117.1 1.4 copy-start.18
  118.8 13.5 %collective-permute-start.12 = (bf16[1,384,512]{2,1,0:T(8,128)(2,1)S(1)}, bf16[1,384,512]{2,1,0:T(8,128)(2,1)S(1)}, u32[]{:S(2)}, u32[]{:S(2)}) collective-permute-start(bf16[1,384,512]{2,1,0:T(8,128)(2,1)S(1)} %get-tuple-element.52), channel_id=1, source_target_pairs={{0,16},{4,20},{8,24},{12,28},{16,0},{20,4},{24,8},{28,12},{1,17},{... | collective-permute-start | bytes 1179656 | tf_op jit(solution)/shard_map/ppermute | solution.py:211
  120.4 11.9 %collective-permute-start.13 = (bf16[1,384,512]{2,1,0:T(8,128)(2,1)S(1)}, bf16[1,384,512]{2,1,0:T(8,128)(2,1)S(1)}, u32[]{:S(2)}, u32[]{:S(2)}) collective-permute-start(bf16[1,384,512]{2,1,0:T(8,128)(2,1)S(1)} %get-tuple-element.53), channel_id=1, source_target_pairs={{0,8},{4,12},{8,0},{12,4},{16,24},{20,28},{24,16},{28,20},{1,9},{5... | collective-permute-start | bytes 1179656 | tf_op jit(solution)/shard_map/ppermute | solution.py:211
  134.4 164.4 %all-gather.11.cloned.1.call-start = ((), (), s32[]{:S(2)}) async-start(), calls=%async_computation.2 | async-start | bytes 7077888 | tf_op jit(solution)/shard_map/all_gather | solution.py:412
  134.5 10.7 %copy-start.21 = (bf16[384,2048]{1,0:T(8,128)(2,1)S(1)}, bf16[384,2048]{1,0:T(8,128)(2,1)}, u32[]{:S(2)}) copy-start(bf16[384,2048]{1,0:T(8,128)(2,1)} %param.4) | copy-start | bytes 4718596
  145.1 1.4 copy-start.9
  145.1 6.0 %collective-permute-start.6 = (bf16[4,768,512]{2,1,0:T(8,128)(2,1)}, bf16[4,768,512]{2,1,0:T(8,128)(2,1)}, u32[]{:S(2)}, u32[]{:S(2)}) collective-permute-start(bf16[4,768,512]{2,1,0:T(8,128)(2,1)} %products_sent.2), channel_id=1, source_target_pairs={{0,4},{4,0},{8,12},{12,8},{16,20},{20,16},{24,28},{28,24},{1,5},{5... | collective-permute-start | bytes 9437192 | tf_op jit(solution)/shard_map/ppermute | solution.py:131
  147.7 1.2 copy-start.3
  149.6 1.2 copy-start.4
  150.8 22.6 %collective-permute-start.14 = (bf16[512,768]{1,0:T(8,128)(2,1)}, bf16[512,768]{1,0:T(8,128)(2,1)}, u32[]{:S(2)}, u32[]{:S(2)}) collective-permute-start(bf16[512,768]{1,0:T(8,128)(2,1)} %get-tuple-element.57.refs_2_), channel_id=1, source_target_pairs={{0,1},{1,2},{2,3},{3,0},{4,5},{5,6},{6,7},{7,4},{8,9},{9,10},{10,1... | collective-permute-start | bytes 2359304 | tf_op jit(solution)/shard_map/ppermute | solution.py:401
  151.1 51.3 %copy-start.20 = (bf16[6144,512]{1,0:T(8,128)(2,1)S(1)}, bf16[6144,512]{1,0:T(8,128)(2,1)}, u32[]{:S(2)}) copy-start(bf16[6144,512]{1,0:T(8,128)(2,1)} %all-gather.7.cloned.1.call-done) | copy-start | bytes 18874372
  162.9 34.1 %collective-permute-start.7 = (bf16[2,384,512]{2,1,0:T(8,128)(2,1)S(1)}, bf16[2,384,512]{2,1,0:T(8,128)(2,1)S(1)}, u32[]{:S(2)}, u32[]{:S(2)}) collective-permute-start(bf16[2,384,512]{2,1,0:T(8,128)(2,1)S(1)} %get-tuple-element.42), channel_id=1, source_target_pairs={{0,8},{4,12},{8,0},{12,4},{16,24},{20,28},{24,16},{28,20},{1,9},{5... | collective-permute-start | bytes 2359304 | tf_op jit(solution)/shard_map/ppermute | solution.py:211
  164.4 35.3 %copy-start.15 = (f32[2,384,512]{2,1,0:T(8,128)S(1)}, f32[2,384,512]{2,1,0:T(8,128)}, u32[]{:S(2)}) copy-start(f32[2,384,512]{2,1,0:T(8,128)} %get-tuple-element.41.refs_0_) | copy-start | bytes 4718596
  164.4 35.3 %copy-start.16 = (f32[2,384,512]{2,1,0:T(8,128)S(1)}, f32[2,384,512]{2,1,0:T(8,128)}, u32[]{:S(2)}) copy-start(f32[2,384,512]{2,1,0:T(8,128)} %get-tuple-element.59.refs_2_) | copy-start | bytes 4718596
  164.4 35.3 %collective-permute-start.8 = (bf16[2,384,512]{2,1,0:T(8,128)(2,1)S(1)}, bf16[2,384,512]{2,1,0:T(8,128)(2,1)S(1)}, u32[]{:S(2)}, u32[]{:S(2)}) collective-permute-start(bf16[2,384,512]{2,1,0:T(8,128)(2,1)S(1)} %get-tuple-element.43), channel_id=1, source_target_pairs={{0,16},{4,20},{8,24},{12,28},{16,0},{20,4},{24,8},{28,12},{1,17},{... | collective-permute-start | bytes 2359304 | tf_op jit(solution)/shard_map/ppermute | solution.py:211
  166.5 37.2 %collective-permute-start.18 = (bf16[512,768]{1,0:T(8,128)(2,1)}, bf16[512,768]{1,0:T(8,128)(2,1)S(1)}, u32[]{:S(2)}, u32[]{:S(2)}) collective-permute-start(bf16[512,768]{1,0:T(8,128)(2,1)} %get-tuple-element.57.refs_2_), channel_id=1, source_target_pairs={{0,3},{1,0},{2,1},{3,2},{4,7},{5,4},{6,5},{7,6},{8,11},{9,8},{10,9... | collective-permute-start | bytes 2359304 | tf_op jit(solution)/shard_map/ppermute | solution.py:401
  170.2 52.4 %collective-permute-start.17 = (bf16[512,768]{1,0:T(8,128)(2,1)}, bf16[512,768]{1,0:T(8,128)(2,1)S(1)}, u32[]{:S(2)}, u32[]{:S(2)}) collective-permute-start(bf16[512,768]{1,0:T(8,128)(2,1)} %get-tuple-element.57.refs_2_), channel_id=1, source_target_pairs={{0,2},{1,3},{2,0},{3,1},{4,6},{5,7},{6,4},{7,5},{8,10},{9,11},{10,... | collective-permute-start | bytes 2359304 | tf_op jit(solution)/shard_map/ppermute | solution.py:401
  200.0 22.6 %collective-permute-start.15 = (bf16[1,384,512]{2,1,0:T(8,128)(2,1)S(1)}, bf16[1,384,512]{2,1,0:T(8,128)(2,1)S(1)}, u32[]{:S(2)}, u32[]{:S(2)}) collective-permute-start(bf16[1,384,512]{2,1,0:T(8,128)(2,1)S(1)} %get-tuple-element.62), channel_id=1, source_target_pairs={{0,16},{4,20},{8,24},{12,28},{16,0},{20,4},{24,8},{28,12},{1,17},{... | collective-permute-start | bytes 1179656 | tf_op jit(solution)/shard_map/ppermute | solution.py:211
  202.5 20.2 %collective-permute-start.16 = (bf16[1,384,512]{2,1,0:T(8,128)(2,1)S(1)}, bf16[1,384,512]{2,1,0:T(8,128)(2,1)S(1)}, u32[]{:S(2)}, u32[]{:S(2)}) collective-permute-start(bf16[1,384,512]{2,1,0:T(8,128)(2,1)S(1)} %get-tuple-element.63), channel_id=1, source_target_pairs={{0,8},{4,12},{8,0},{12,4},{16,24},{20,28},{24,16},{28,20},{1,9},{5... | collective-permute-start | bytes 1179656 | tf_op jit(solution)/shard_map/ppermute | solution.py:211
  203.7 24.5 %copy-start.22 = (bf16[512,768]{1,0:T(8,128)(2,1)}, bf16[512,768]{1,0:T(8,128)(2,1)S(1)}, u32[]{:S(2)}) copy-start(bf16[512,768]{1,0:T(8,128)(2,1)S(1)} %collective-permute-done.18.refs_5_) | copy-start | bytes 2359300
  222.6 5.6 %copy-start.23 = (bf16[512,768]{1,0:T(8,128)(2,1)}, bf16[512,768]{1,0:T(8,128)(2,1)S(1)}, u32[]{:S(2)}) copy-start(bf16[512,768]{1,0:T(8,128)(2,1)S(1)} %collective-permute-done.17.refs_4_) | copy-start | bytes 2359300
  223.7 14.9 %copy-start.19 = (bf16[512,768]{1,0:T(8,128)(2,1)}, bf16[512,768]{1,0:T(8,128)(2,1)S(1)}, u32[]{:S(2)}) copy-start(bf16[512,768]{1,0:T(8,128)(2,1)S(1)} %get-tuple-element.67.refs_2_) | copy-start | bytes 2359300
  230.9 64.9 %collective-permute-start.21 = (bf16[512,768]{1,0:T(8,128)(2,1)S(1)}, bf16[512,768]{1,0:T(8,128)(2,1)S(1)}, u32[]{:S(2)}, u32[]{:S(2)}) collective-permute-start(bf16[512,768]{1,0:T(8,128)(2,1)S(1)} %get-tuple-element.67.refs_2_), channel_id=1, source_target_pairs={{0,3},{1,0},{2,1},{3,2},{4,7},{5,4},{6,5},{7,6},{8,11},{9,8},{10,9... | collective-permute-start | bytes 2359304 | tf_op jit(solution)/shard_map/ppermute | solution.py:401
  233.8 65.1 %collective-permute-start.20 = (bf16[512,768]{1,0:T(8,128)(2,1)S(1)}, bf16[512,768]{1,0:T(8,128)(2,1)S(1)}, u32[]{:S(2)}, u32[]{:S(2)}) collective-permute-start(bf16[512,768]{1,0:T(8,128)(2,1)S(1)} %get-tuple-element.67.refs_2_), channel_id=1, source_target_pairs={{0,2},{1,3},{2,0},{3,1},{4,6},{5,7},{6,4},{7,5},{8,10},{9,11},{10,... | collective-permute-start | bytes 2359304 | tf_op jit(solution)/shard_map/ppermute | solution.py:401
  233.8 65.1 %collective-permute-start.19 = (bf16[512,768]{1,0:T(8,128)(2,1)S(1)}, bf16[512,768]{1,0:T(8,128)(2,1)S(1)}, u32[]{:S(2)}, u32[]{:S(2)}) collective-permute-start(bf16[512,768]{1,0:T(8,128)(2,1)S(1)} %get-tuple-element.67.refs_2_), channel_id=1, source_target_pairs={{0,1},{1,2},{2,3},{3,0},{4,5},{5,6},{6,7},{7,4},{8,9},{9,10},{10,1... | collective-permute-start | bytes 2359304 | tf_op jit(solution)/shard_map/ppermute | solution.py:401
  295.9 3.0 copy-start.24
  298.8 1.1 copy-start.26
  (5 other events, 5.4 us)
Sparse Core Ops, SparseCore 0:
  48.8 44.9 all-gather.6
  134.5 93.5 all-gather.8
  230.1 45.0 all-gather.10

commit v2 on v0

--- a/solution.py
+++ b/solution.py
@@ -128,7 +128,7 @@
         cost_estimate=cost,
         name="products_sent",
     )(order_sent, *xs, weights)
-    other = tie(lax.ppermute(sent, "row", row_partner(1)), beside(0))
+    other = tie(lax.ppermute(sent, "row", row_partner(1)), beside(0, sent))
     half = (blocks // 2, total_rows // 2, width)
     half_spec = pl.BlockSpec(half, lambda g, order: (0, 0, 0))
     outs = pl.pallas_call(
@@ -210,11 +210,34 @@
         others = [
             lax.ppermute(sent, "row", row_partner(mask)) for (sent, _), mask in zip(pieces, masks)
         ]
-        others = tie(others, beside(level + 1))
+        others = tie(others, beside(level + 1, pieces[0][0]))
         if level < bits - 1:
             pieces = halve(pieces, others)
     share, turned = finish_share(pieces, others)
     return share, turned
+
+
+def narrow_kernel(sign_ref, out_ref):
+    rows = sign_ref.shape[0]
+    flat = sign_ref.reshape(rows * SUBS, LANES)
+    for c in range(SUBS):
+        piece = flat[pl.ds(c, rows, stride=SUBS), :]
+        out_ref[:, c * LANES : (c + 1) * LANES] = piece.astype(jnp.int8)
+
+
+def narrow(sign3):
+    row_total, lane_tiles, _ = sign3.shape
+    tile = min(512, row_total)
+    return pl.pallas_call(
+        narrow_kernel,
+        grid=(row_total // tile, lane_tiles // SUBS),
+        in_specs=[pl.BlockSpec((tile, SUBS, LANES), lambda i, j: (i, j, 0))],
+        out_specs=pl.BlockSpec((tile, SUBS * LANES), lambda i, j: (i, j)),
+        out_shape=jax.ShapeDtypeStruct((row_total, lane_tiles * LANES), jnp.int8),
+        compiler_params=pltpu.CompilerParams(vmem_limit_bytes=32 * MIB),
+        cost_estimate=pl.CostEstimate(flops=0, bytes_accessed=sign3.size * 5, transcendentals=0),
+        name="narrow_signs",
+    )(sign3)
 
 
 def update_kernel(sizes, group, sub_width, scale, last, info_ref, *refs):
@@ -223,20 +246,20 @@
     ys, refs = refs[:col_count], refs[col_count:]
     y_cols, refs = refs[:per_group], refs[per_group:]
     x_cols, refs = refs[:col_count], refs[col_count:]
-    omega_ref, row_ref, col_ref = refs[:3]
-    sign_ref = refs[3] if last else None
-    out_ref, cross_ref, rate_ref = refs[3 + last :]
-    rows = omega_ref.shape[0]
-    cross = cross_ref.reshape(rows * SUBS, LANES)
+    old_ref, row_ref, col_ref = refs[:3]
+    if last:
+        sign_ref, out_ref, cross_ref = refs[3:]
+    else:
+        out_ref = refs[3]
+    rows = row_ref.shape[0]
     per_block = sub_width // LANES
     blocks = SUBS // per_block
+    width = min(sub_width, 256)
     distance = pl.program_id(1)
-
-    @pl.when(pl.program_id(0) == 0)
-    def _():
-        rate = rate_ref.at[distance].reshape(rows * SUBS, LANES)
-        for c in range(SUBS):
-            rate[pl.ds(c, rows, stride=SUBS), :] = jnp.broadcast_to(row_ref[...], (rows, LANES))
+    native = (out_ref if last else old_ref).reshape(rows * SUBS, LANES)
+    row_rate = jnp.broadcast_to(row_ref[...], (rows, LANES))
+    row_smooth = row_rate * scale
+    row_shift = row_rate * PENALTY
 
     for value in range(col_count):
 
@@ -244,51 +267,62 @@
         def _():
             met = [x_cols[(group * per_group + s + value) % col_count] for s in range(per_group)]
             left = jnp.concatenate([x[...] for x in xs] + [ys[value][...]], axis=1)
-            for b in range(blocks):
-                right = jnp.concatenate([r[b] for r in (*y_cols, *met)], axis=0)
+            for first in range(0, SUBS * LANES, width):
+                b, at = first // sub_width, first % sub_width
+                right = jnp.concatenate(
+                    [r[b, :, at : at + width] for r in (*y_cols, *met)], axis=0
+                )
                 total = jnp.dot(left, right, preferred_element_type=jnp.float32)
+                if last and value == 0:
+                    cross_ref[:, first : first + width] = total
+                for lane in range(0, width, LANES):
+                    columns = slice(first + lane, first + lane + LANES)
+                    spot = pl.ds((first + lane) // LANES, rows, stride=SUBS)
+                    col_rate = col_ref[:, columns]
+                    taken = (row_smooth * col_rate) * total[:, lane : lane + LANES]
+                    if last:
+                        trial = old_ref[:, columns].astype(jnp.float32) - taken
+                        sign = sign_ref[:, columns].astype(jnp.float32)
+                        shift = row_shift * col_rate
+                        native[spot, :] = sign * jnp.maximum(sign * trial - shift, 0.0)
+                    else:
+                        out_ref[:, columns] = (native[spot, :] - taken).astype(out_ref.dtype)
+
+    if last:
+        for b in range(blocks):
+
+            @pl.when(jnp.logical_and(distance == 0, pl.program_id(0) * blocks + b == info_ref[0]))
+            def _():
                 for lane in range(0, sub_width, LANES):
-                    spot = pl.ds(b * per_block + lane // LANES, rows, stride=SUBS)
-                    cross[spot, :] = total[:, lane : lane + LANES]
-
-    col_rate = col_ref[...][None]
-    col_shift = col_rate * PENALTY
-    col_smooth = col_rate * scale
-    for first in range(0, rows, 64):
-        span = slice(first, min(first + 64, rows))
-        row_rate = rate_ref[distance, span]
-        trial = omega_ref[span] - (row_rate * col_smooth) * cross_ref[span]
-        if last:
-            sign = sign_ref[span].astype(jnp.float32)
-            trial = sign * jnp.maximum(sign * trial - row_rate * col_shift, 0.0)
-        out_ref[span] = trial
-
-    if last:
-        @pl.when(jnp.logical_and(distance == 0, pl.program_id(0) == info_ref[0] // blocks))
-        def _():
-            first_tile = info_ref[0] % blocks * per_block
-            for first in range(0, rows, 64):
-                span = slice(first, min(first + 64, rows))
-                shape = out_ref[span].shape
-                rate = rate_ref[distance, span] * col_rate
-                trial = omega_ref[span] - rate * (cross_ref[span] * scale)
-                value = 0.5 * (trial + jnp.sqrt(trial * trial + 4.0 * rate))
-                row_ids = lax.broadcasted_iota(jnp.int32, shape, 0) + first
-                tile_ids = lax.broadcasted_iota(jnp.int32, shape, 1) - first_tile
-                col_ids = tile_ids * LANES + lax.broadcasted_iota(jnp.int32, shape, 2)
-                out_ref[span] = jnp.where(row_ids == col_ids, value, out_ref[span])
-
-
-def update(group, xs, ys, y_cols, x_cols, omega3, row_rate, col_rate, sign3, info, scale):
-    row_total, lane_tiles, _ = omega3.shape
+                    first = b * sub_width + lane
+                    columns = slice(first, first + LANES)
+                    spot = pl.ds(first // LANES, rows, stride=SUBS)
+                    rate = row_rate * col_ref[:, columns]
+                    trial = old_ref[:, columns].astype(jnp.float32)
+                    trial = trial - rate * (cross_ref[:, columns] * scale)
+                    value = 0.5 * (trial + jnp.sqrt(trial * trial + 4.0 * rate))
+                    row_ids = lax.broadcasted_iota(jnp.int32, (rows, LANES), 0)
+                    col_ids = lax.broadcasted_iota(jnp.int32, (rows, LANES), 1) + lane
+                    native[spot, :] = jnp.where(row_ids == col_ids, value, native[spot, :])
+
+
+def update(group, xs, ys, y_cols, x_cols, old, row_rate, col_rate, signs, info, scale):
+    row_total = row_rate.shape[0]
+    lane_tiles = col_rate.shape[1] // LANES
     part = xs[0].shape[1]
     tile = sub_width = ys[0].shape[0]
     blocks = SUBS * LANES // sub_width
-    last = sign3 is not None
+    last = signs is not None
     sizes = (len(ys), len(xs))
-    grid_block = pl.BlockSpec((tile, SUBS, LANES), lambda j, d, p: (p[1 + d], j, 0))
+    native_block = pl.BlockSpec((tile, SUBS, LANES), lambda j, d, p: (p[1 + d], j, 0))
+    row_block = pl.BlockSpec((tile, SUBS * LANES), lambda j, d, p: (p[1 + d], j))
     columns = list(y_cols) + list(x_cols)
-    operands = [*xs, *ys, *[b for b, _ in columns], omega3, row_rate, col_rate]
+    operands = [*xs, *ys, *[b for b, _ in columns], old, row_rate, col_rate]
+    if last:
+        result = jax.ShapeDtypeStruct((row_total, lane_tiles, LANES), jnp.float32)
+    else:
+        result = jax.ShapeDtypeStruct((row_total, lane_tiles * LANES), jnp.bfloat16)
+    elements = row_total * lane_tiles * LANES
     return pl.pallas_call(
         functools.partial(update_kernel, sizes, group, sub_width, scale, last),
         grid_spec=pltpu.PrefetchScalarGridSpec(
@@ -301,26 +335,21 @@
                 for _, at in columns
             ]
             + [
-                grid_block,
+                row_block if last else native_block,
                 pl.BlockSpec((tile, 1), lambda j, d, p: (p[1 + d], 0)),
-                pl.BlockSpec((SUBS, LANES), lambda j, d, p: (j, 0)),
+                pl.BlockSpec((1, SUBS * LANES), lambda j, d, p: (0, j)),
             ]
-            + [grid_block] * last,
-            out_specs=grid_block,
-            scratch_shapes=[
-                pltpu.VMEM((tile, SUBS, LANES), jnp.float32),
-                pltpu.VMEM((row_total // tile, tile, SUBS, LANES), jnp.float32),
-            ],
-        ),
-        out_shape=jax.ShapeDtypeStruct(omega3.shape, jnp.float32),
+            + [row_block] * last,
+            out_specs=native_block if last else row_block,
+            scratch_shapes=[pltpu.VMEM((tile, SUBS * LANES), jnp.float32)] * last,
+        ),
+        out_shape=result,
         compiler_params=pltpu.CompilerParams(vmem_limit_bytes=56 * MIB),
         cost_estimate=pl.CostEstimate(
-            flops=4 * part * len(xs) * omega3.size,
-            bytes_accessed=omega3.size * 12,
-            transcendentals=0,
+            flops=4 * part * len(xs) * elements, bytes_accessed=elements * 8, transcendentals=0
         ),
         name="last_terms" if last else "first_terms",
-    )(info, *operands, *([sign3] if last else []))
+    )(info, *operands, *([signs] if last else []))
 
 
 def body(samples, omega, sign_mask, step_size):
@@ -359,6 +388,11 @@
         if not distance:
             return y
         return lax.ppermute(y, "col", [(c, (c + distance) % col_count) for c in range(col_count)])
+
+    def square_sum(pieces, axis):
+        return sum(jnp.sum(jnp.square(p.astype(jnp.float32)), axis=axis) for p in pieces)
+
+    sums, signs = [], []
 
     def complete(length):
         return len(xs) >= length and len(xs[length - 1]) == PIECES
@@ -384,7 +418,7 @@
         if waiting:
             y_cols.append((block, 1))
 
-        def beside(exchange):
+        def beside(exchange, sent):
             done = []
             if exchange == 0:
                 x_turned.extend(turn(x, sub_width) for x in group)
@@ -395,8 +429,13 @@
                     done.append(advance())
             if y_planes and exchange == 1:
                 done.append(y_planes[0][1])
+                signs.append(narrow(tie(sign3, [sent])))
+                done.extend(signs)
             if y_planes and exchange == 2:
                 done.extend(y_planes[0][2:])
+                sums.append(square_sum([x for pieces in xs for x in pieces], 0))
+                sums.append(square_sum([x_cols[0][0]], 1))
+                done.extend(sums)
             return done
 
         share, turned = sum_over_rows(
@@ -413,15 +452,14 @@
     y_cols.append((last, 0))
     group_rows = part * per_group
 
-    def mean_square(pieces, axis):
-        total = sum(jnp.sum(jnp.square(p.astype(jnp.float32)), axis=axis) for p in pieces)
+    def scale_of(total):
         total = lax.optimization_barrier(total) / sample_total + 1e-06
         return lax.optimization_barrier(total.astype(jnp.bfloat16)).astype(jnp.float32)
 
-    x_pieces = [x for pieces in xs for x in pieces]
-    row_rate = (step_size[0] * lax.rsqrt(mean_square(x_pieces, 0)))[:, None]
-    col_rate = lax.rsqrt(mean_square([block[:, :group_rows] for block, _ in x_cols], 1))
-    col_rate = col_rate.reshape(lane_tiles, LANES)
+    row_sum, col_sum = sums
+    col_sum = col_sum + square_sum([block[:, :group_rows] for block, _ in x_cols[1:]], 1)
+    row_rate = (step_size[0] * lax.rsqrt(scale_of(row_sum)))[:, None]
+    col_rate = lax.rsqrt(scale_of(col_sum)).reshape(1, lane_tiles * LANES)
 
     planes = (col_index - jnp.arange(col_count, dtype=jnp.int32) + col_count) % col_count
     info = jnp.concatenate([row_index[None], planes])
@@ -439,7 +477,7 @@
             updated,
             row_rate,
             col_rate,
-            sign3 if k == GROUPS - 1 else None,
+            signs[0] if k == GROUPS - 1 else None,
             info,
             0.5 / sample_total,
         )

time: 377 us -> 362 us (0.960)
  waiting for transfers between devices: 113 us -> 89.6 us
  Pallas kernels: 184 us -> 194 us
  other arithmetic: 13.2 us -> 8.68 us
    ppermute x8, waiting for transfers between devices: 30.8 us -> 7.5 us  [sum_over_rows(): lax.ppermute(sent, 'row', row_partner(mask))]
    pallas_call x0 -> x1, Pallas kernels: none -> 19.2 us  [narrow(): pl.pallas_call(narrow_kernel, grid=(row_total // tile, lane_tiles // SUBS...]
    pallas_call x2, Pallas kernels: 116 us -> 105 us  [update(): pl.pallas_call(functools.partial(update_kernel, sizes, group, sub_width,...]
    reduce_sum x8, other arithmetic: 11.4 us -> 6.89 us  [square_sum(): jnp.sum(jnp.square(p.astype(jnp.float32)), axis=axis)]
    unnamed x60 -> x65, local copies, waits for them, and re-layouts: 26.1 us -> 26.5 us
  transfers between devices with their start and end apart: 25 -> 25, of which waited for: 14 -> 11; matrix products, arithmetic and copies ran while one was open for 5% -> 4% of each run, Pallas kernels for 32% -> 39%
where the time goes in v2:
time: 362 us; the launch traced here: 360 us
  Pallas kernels  194 us (54%)
  waiting for transfers between devices  89.6 us (25%)
  local copies, waits for them, and re-layouts  30.3 us (8%)
  starting transfers between devices  23.9 us (7%)
  between operations  14.2 us (4%)
  other arithmetic  8.68 us (2%)
    pallas_call x2, Pallas kernels, update(): pl.pallas_call(functools.partial(update_kernel, sizes, group, sub_width,...  105 us
    ppermute x6, waiting for transfers between devices, advance(): done = lax.ppermute(xs[-2][len(xs[-1])], 'col', ring)  49.8 us
    ppermute x6, waiting for transfers between devices, to_distance(): lax.ppermute(y, 'col', [(c, (c + distance) % col_count) for c in range(co...  28 us
    unnamed x65, local copies, waits for them, and re-layouts  26.5 us
    pallas_call x2, Pallas kernels, pair_products(): pl.pallas_call(functools.partial(kept_kernel, count, bits), grid_spec=plt...  23.4 us
    pallas_call x2, Pallas kernels, pair_products(): pl.pallas_call(functools.partial(sent_kernel, count), grid_spec=pltpu.Pre...  21.2 us
    pallas_call x1, Pallas kernels, narrow(): pl.pallas_call(narrow_kernel, grid=(row_total // tile, lane_tiles // SUBS...  19.2 us
    pallas_call x1, Pallas kernels, convert(): pl.pallas_call(convert_kernel, grid=(row_total // tile, lane_tiles // SUB...  19.2 us
  transfers between devices with their start and end apart: 25, of which 11 were waited for; matrix products, arithmetic and copies ran while one was open for 4% of the time, Pallas kernels for 39%

profile of v2, /device:TPU:0, one launch (start us, length us, event | category | flops | bytes accessed | tf_op | source)
XLA Modules:
  0.0 360.2 jit_solution(15527032565881149390)
XLA Ops:
  6.5 1.5 fusion.1
  8.0 3.1 collective-permute-start.1
  11.1 1.6 collective-permute-start
  12.7 19.2 %omega_to_bf16.1.refs_4_ = bf16[8,2048,512]{2,1,0:T(8,128)(2,1)S(1)} custom-call(f32[2048,32,128]{2,1,0:T(8,128)} %bitcast.28), custom_call_target="tpu_custom_call" | custom-call | bytes 50331648 | tf_op jit(solution)/shard_map/omega_to_bf16/pallas_call | solution.py:34
  31.9 6.2 %copy-done.1 = bf16[8,2048,512]{2,1,0:T(8,128)(2,1)} copy-done((bf16[8,2048,512]{2,1,0:T(8,128)(2,1)}, bf16[8,2048,512]{2,1,0:T(8,128)(2,1)S(1)}, u32[]{:S(2)}) %copy-start.1) | copy-done | bytes 16777240
  38.1 9.5 %collective-permute-done.refs_2_.refs_0_ = bf16[192,2048]{1,0:T(8,128)(2,1)S(1)} collective-permute-done((bf16[192,2048]{1,0:T(8,128)(2,1)S(1)}, bf16[192,2048]{1,0:T(8,128)(2,1)S(1)}, u32[]{:S(2)}, u32[]{:S(2)}) %collective-permute-start) | collective-permute-done | bytes 786464 | tf_op jit(solution)/shard_map/ppermute | solution.py:383
  47.6 1.0 pad_maximum_fusion
  48.7 10.6 %products_sent.3 = bf16[4,768,512]{2,1,0:T(8,128)(2,1)} custom-call(s32[4]{0:T(128)S(1)} %get-tuple-element.75.order_ref, bf16[192,2048]{1,0:T(8,128)(2,1)S(1)} %get-tuple-element.78.refs_0_, bf16[192,2048]{1,0:T(8,128)(2,1)S(1)} %get-tuple-element.77.refs_1_, bf16[192,2048]{1,0:T(8,128)(2,1)S(1)} %collective-permute-done.refs_2_.refs_0_, ...), custom_call_target="tpu_custom_call" | custom-call | flops 6442450944 | bytes 14680064 | tf_op jit(solution)/shard_map/products_sent/pallas_call | solution.py:118
  59.3 1.1 copy-done.14
  61.2 1.2 copy-done.2
  62.4 1.1 collective-permute-start.3
  64.3 1.2 copy-done.3
  65.4 16.0 %collective-permute-done.2.refs_0_ = bf16[192,2048]{1,0:T(8,128)(2,1)S(1)} collective-permute-done((bf16[192,2048]{1,0:T(8,128)(2,1)S(1)}, bf16[192,2048]{1,0:T(8,128)(2,1)S(1)}, u32[]{:S(2)}, u32[]{:S(2)}) %collective-permute-start.2) | collective-permute-done | bytes 786464 | tf_op jit(solution)/shard_map/ppermute | solution.py:383
  81.4 1.6 copy-done.27
  83.1 1.1 copy-done.9
  84.2 11.7 %products_kept.3 = (bf16[2,384,512]{2,1,0:T(8,128)(2,1)S(1)}, f32[2,384,512]{2,1,0:T(8,128)}, bf16[2,384,512]{2,1,0:T(8,128)(2,1)S(1)}, f32[2,384,512]{2,1,0:T(8,128)}) custom-call(s32[4]{0:T(128)S(1)} %get-tuple-element.76.order_ref, bf16[192,2048]{1,0:T(8,128)(2,1)S(1)} %copy-done.15, bf16[192,2048]{1,0:T(8,128)(2,1)S(1)} %copy-done.12, ...), custom_call_target="tpu_custom_call" | custom-call | flops 6442450944 | bytes 14680064 | tf_op jit(solution)/shard_map/products_kept/pallas_call | solution.py:134
  95.9 1.5 collective-permute-start.10
  97.4 1.7 collective-permute-start.11
  99.0 16.1 %collective-permute-done.4.refs_0_.refs_2_ = bf16[192,2048]{1,0:T(8,128)(2,1)S(1)} collective-permute-done((bf16[192,2048]{1,0:T(8,128)(2,1)S(1)}, bf16[192,2048]{1,0:T(8,128)(2,1)S(1)}, u32[]{:S(2)}, u32[]{:S(2)}) %collective-permute-start.4) | collective-permute-done | bytes 786464 | tf_op jit(solution)/shard_map/ppermute | solution.py:383
  115.9 1.4 copy-done.18
  117.3 1.4 copy-done.19
  118.9 1.6 collective-permute-start.12
  123.3 8.3 %collective-permute-done.5.refs_1_.refs_3_ = bf16[192,2048]{1,0:T(8,128)(2,1)S(1)} collective-permute-done((bf16[192,2048]{1,0:T(8,128)(2,1)S(1)}, bf16[192,2048]{1,0:T(8,128)(2,1)S(1)}, u32[]{:S(2)}, u32[]{:S(2)}) %collective-permute-start.5) | collective-permute-done | bytes 786464 | tf_op jit(solution)/shard_map/ppermute | solution.py:383
  132.3 1.2 share.2
  133.5 0.9 constant_dynamic-update-slice_fusion
  134.5 10.6 %products_sent.2 = bf16[4,768,512]{2,1,0:T(8,128)(2,1)} custom-call(s32[4]{0:T(128)S(1)} %get-tuple-element.75.order_ref, bf16[192,2048]{1,0:T(8,128)(2,1)S(1)} %collective-permute-done.2.refs_0_, bf16[192,2048]{1,0:T(8,128)(2,1)S(1)} %collective-permute-done.3.refs_1_, bf16[192,2048]{1,0:T(8,128)(2,1)S(1)} %collective-permute-done.4.refs_0_.refs_2_, ...), custom_call_target="tpu_custom_call" | custom-call | flops 6442450944 | bytes 14680064 | tf_op jit(solution)/shard_map/products_sent/pallas_call | solution.py:118
  147.7 1.1 copy-done.4
  149.6 1.2 copy-done.5
  151.2 11.7 %products_kept.2 = (bf16[2,384,512]{2,1,0:T(8,128)(2,1)S(1)}, f32[2,384,512]{2,1,0:T(8,128)}, bf16[2,384,512]{2,1,0:T(8,128)(2,1)S(1)}, f32[2,384,512]{2,1,0:T(8,128)}) custom-call(s32[4]{0:T(128)S(1)} %get-tuple-element.76.order_ref, bf16[192,2048]{1,0:T(8,128)(2,1)S(1)} %collective-permute-done.2.refs_0_, ...), custom_call_target="tpu_custom_call" | custom-call | flops 6442450944 | bytes 14680064 | tf_op jit(solution)/shard_map/products_kept/pallas_call | solution.py:134
  162.9 1.6 collective-permute-start.8
  164.4 1.5 collective-permute-start.7
  166.4 3.7 %collective-permute-start.18 = (bf16[512,768]{1,0:T(8,128)(2,1)}, bf16[512,768]{1,0:T(8,128)(2,1)S(1)}, u32[]{:S(2)}, u32[]{:S(2)}) collective-permute-start(bf16[512,768]{1,0:T(8,128)(2,1)} %get-tuple-element.58.refs_2_), channel_id=1, source_target_pairs={{0,3},{1,0},{2,1},{3,2},{4,7},{5,4},{6,5},{7,6},{8,11},{9,8},{10,9... | collective-permute-start | bytes 2359304 | tf_op jit(solution)/shard_map/ppermute | solution.py:390
  170.4 19.2 %narrow_signs.1.refs_15_ = s8[2048,4096]{1,0:T(32,128)(4,1)S(1)} custom-call(s32[2048,32,128]{2,1,0:T(8,128)} %bitcast.30), custom_call_target="tpu_custom_call" | custom-call | bytes 41943040 | tf_op jit(solution)/shard_map/narrow_signs/pallas_call | solution.py:231
  189.6 3.3 copy-done
  192.9 4.1 %collective-permute-done.8.refs_3_ = bf16[2,384,512]{2,1,0:T(8,128)(2,1)S(1)} collective-permute-done((bf16[2,384,512]{2,1,0:T(8,128)(2,1)S(1)}, bf16[2,384,512]{2,1,0:T(8,128)(2,1)S(1)}, u32[]{:S(2)}, u32[]{:S(2)}) %collective-permute-start.8) | collective-permute-done | bytes 786464 | tf_op jit(solution)/shard_map/ppermute | solution.py:211
  197.0 2.6 collective-permute-done.7.refs_1_
  200.0 2.5 collective-permute-start.16
  202.5 1.2 multiply_reduce_fusion.1
  203.7 18.9 %collective-permute-done.17.refs_4_ = bf16[512,768]{1,0:T(8,128)(2,1)S(1)} collective-permute-done((bf16[512,768]{1,0:T(8,128)(2,1)}, bf16[512,768]{1,0:T(8,128)(2,1)S(1)}, u32[]{:S(2)}, u32[]{:S(2)}) %collective-permute-start.17) | collective-permute-done | bytes 786464 | tf_op jit(solution)/shard_map/ppermute | solution.py:390
  222.6 1.1 share.3
  223.8 3.8 %all-gather.9.cloned.1.call-done = bf16[12288,512]{1,0:T(8,128)(2,1)} async-done(((bf16[1536,512]{1,0:T(8,128)(2,1)}), bf16[12288,512]{1,0:T(8,128)(2,1)}) %all-gather.9.cloned.1.call-update) | async-done | bytes 12582928 | tf_op jit(solution)/shard_map/all_gather | solution.py:401
  229.0 1.4 copy.6.refs_13_
  230.4 2.8 collective-permute-start.21
  233.7 4.3 %multiply_reduce_fusion = f32[8,512]{1,0:T(8,128)S(1)} fusion(bf16[8,1536,512]{2,1,0:T(8,128)(2,1)} %bitcast.14), kind=kLoop, calls=%fused_computation | loop fusion | flops 9433088 | bytes 6307840 | tf_op jit(solution)/shard_map/reduce_sum | solution.py:393
  238.7 50.4 %first_terms.1.refs_12_ = bf16[2048,4096]{1,0:T(8,128)(2,1)} custom-call(s32[5]{0:T(128)} %pad_add_fusion.info_ref, bf16[2048,384]{1,0:T(8,128)(2,1)} %copy-done.2, bf16[2048,384]{1,0:T(8,128)(2,1)} %copy-done.3, bf16[512,768]{1,0:T(8,128)(2,1)} %get-tuple-element.58.refs_2_, bf16[512,768]{1,0:T(8,128)(2,1)} %collective-permute-done.14.refs_3_, ...), custom_call_target="tpu_custom_call" | custom-call | flops 25769803776 | bytes 67108864 | tf_op jit(solution)/shard_map/first_terms/pallas_call | solution.py:326
  289.1 9.1 %collective-permute-done.20.refs_4_ = bf16[512,768]{1,0:T(8,128)(2,1)S(1)} collective-permute-done((bf16[512,768]{1,0:T(8,128)(2,1)S(1)}, bf16[512,768]{1,0:T(8,128)(2,1)S(1)}, u32[]{:S(2)}, u32[]{:S(2)}) %collective-permute-start.20) | collective-permute-done | bytes 786464 | tf_op jit(solution)/shard_map/ppermute | solution.py:390
  298.3 0.9 copy-done.25
  299.5 54.2 %last_terms.1 = f32[2048,32,128]{2,1,0:T(8,128)} custom-call(s32[5]{0:T(128)} %pad_add_fusion.info_ref, bf16[2048,384]{1,0:T(8,128)(2,1)} %copy-done.4, bf16[2048,384]{1,0:T(8,128)(2,1)} %copy-done.5, bf16[512,768]{1,0:T(8,128)(2,1)} %copy-done.20, bf16[512,768]{1,0:T(8,128)(2,1)} %copy-done.26, bf16[512,768]{1,0:T(8,128)(2,1)} %copy-done.25, ...), custom_call_target="tpu_custom_call" | custom-call | flops 25769803776 | bytes 67108864 | tf_op jit(solution)/shard_map/last_terms/pallas_call | solution.py:326
  (110 shorter events, 13.3 us)
Async XLA Ops:
  6.5 144.6 %all-gather.7.cloned.1.call-start = ((), (), s32[]{:S(2)}) async-start(), calls=%async_computation | async-start | bytes 7077888 | tf_op jit(solution)/shard_map/all_gather | solution.py:401
  8.0 40.7 %copy-start.13 = (bf16[192,2048]{1,0:T(8,128)(2,1)}, bf16[192,2048]{1,0:T(8,128)(2,1)S(1)}, u32[]{:S(2)}) copy-start(bf16[192,2048]{1,0:T(8,128)(2,1)S(1)} %get-tuple-element.78.refs_0_) | copy-start | bytes 2359300
  8.0 51.3 %copy-start.11 = (bf16[192,2048]{1,0:T(8,128)(2,1)}, bf16[192,2048]{1,0:T(8,128)(2,1)S(1)}, u32[]{:S(2)}) copy-start(bf16[192,2048]{1,0:T(8,128)(2,1)S(1)} %get-tuple-element.77.refs_1_) | copy-start | bytes 2359300
  8.0 30.0 %collective-permute-start.1 = (bf16[192,2048]{1,0:T(8,128)(2,1)S(1)}, bf16[192,2048]{1,0:T(8,128)(2,1)S(1)}, u32[]{:S(2)}, u32[]{:S(2)}) collective-permute-start(bf16[192,2048]{1,0:T(8,128)(2,1)S(1)} %get-tuple-element.77.refs_1_), channel_id=1, source_target_pairs={{0,1},{1,2},{2,3},{3,0},{4,5},{5,6},{6,7},{7,4},{8,9},{9,10},{10,1... | collective-permute-start | bytes 2359304 | tf_op jit(solution)/shard_map/ppermute | solution.py:383
  11.1 36.4 %collective-permute-start = (bf16[192,2048]{1,0:T(8,128)(2,1)S(1)}, bf16[192,2048]{1,0:T(8,128)(2,1)S(1)}, u32[]{:S(2)}, u32[]{:S(2)}) collective-permute-start(bf16[192,2048]{1,0:T(8,128)(2,1)S(1)} %get-tuple-element.78.refs_0_), channel_id=1, source_target_pairs={{0,1},{1,2},{2,3},{3,0},{4,5},{5,6},{6,7},{7,4},{8,9},{9,10},{10,1... | collective-permute-start | bytes 2359304 | tf_op jit(solution)/shard_map/ppermute | solution.py:383
  31.8 6.2 %copy-start.1 = (bf16[8,2048,512]{2,1,0:T(8,128)(2,1)}, bf16[8,2048,512]{2,1,0:T(8,128)(2,1)S(1)}, u32[]{:S(2)}) copy-start(bf16[8,2048,512]{2,1,0:T(8,128)(2,1)S(1)} %omega_to_bf16.1.refs_4_) | copy-start | bytes 50331652
  38.1 43.4 %copy-start.6 = (bf16[192,2048]{1,0:T(8,128)(2,1)}, bf16[192,2048]{1,0:T(8,128)(2,1)S(1)}, u32[]{:S(2)}) copy-start(bf16[192,2048]{1,0:T(8,128)(2,1)S(1)} %collective-permute-done.1.refs_3_.refs_1_) | copy-start | bytes 2359300
  47.5 15.9 %copy-start.8 = (bf16[192,2048]{1,0:T(8,128)(2,1)}, bf16[192,2048]{1,0:T(8,128)(2,1)S(1)}, u32[]{:S(2)}) copy-start(bf16[192,2048]{1,0:T(8,128)(2,1)S(1)} %collective-permute-done.refs_2_.refs_0_) | copy-start | bytes 2359300
  48.6 179.0 %all-gather.9.cloned.1.call-start = ((), (), s32[]{:S(2)}) async-start(), calls=%async_computation.1 | async-start | bytes 14155776 | tf_op jit(solution)/shard_map/all_gather | solution.py:401
  59.3 22.1 %collective-permute-start.9 = (bf16[4,768,512]{2,1,0:T(8,128)(2,1)}, bf16[4,768,512]{2,1,0:T(8,128)(2,1)S(1)}, u32[]{:S(2)}, u32[]{:S(2)}) collective-permute-start(bf16[4,768,512]{2,1,0:T(8,128)(2,1)} %products_sent.3), channel_id=1, source_target_pairs={{0,4},{4,0},{8,12},{12,8},{16,20},{20,16},{24,28},{28,24},{1,5},{5... | collective-permute-start | bytes 9437192 | tf_op jit(solution)/shard_map/ppermute | solution.py:131
  59.3 22.1 %collective-permute-start.2 = (bf16[192,2048]{1,0:T(8,128)(2,1)S(1)}, bf16[192,2048]{1,0:T(8,128)(2,1)S(1)}, u32[]{:S(2)}, u32[]{:S(2)}) collective-permute-start(bf16[192,2048]{1,0:T(8,128)(2,1)S(1)} %collective-permute-done.refs_2_.refs_0_), channel_id=1, source_target_pairs={{0,1},{1,2},{2,3},{3,0},{4,5},{5,6},{6,7},{7,4},{8,9},{9,10},{10,1... | collective-permute-start | bytes 2359304 | tf_op jit(solution)/shard_map/ppermute | solution.py:383
  62.4 20.7 %copy-start.12 = (bf16[192,2048]{1,0:T(8,128)(2,1)S(1)}, bf16[192,2048]{1,0:T(8,128)(2,1)}, u32[]{:S(2)}) copy-start(bf16[192,2048]{1,0:T(8,128)(2,1)} %copy-done.11) | copy-start | bytes 2359300
  62.4 20.7 %copy-start.15 = (bf16[192,2048]{1,0:T(8,128)(2,1)S(1)}, bf16[192,2048]{1,0:T(8,128)(2,1)}, u32[]{:S(2)}) copy-start(bf16[192,2048]{1,0:T(8,128)(2,1)} %copy-done.13) | copy-start | bytes 2359300
  62.4 36.6 %collective-permute-start.3 = (bf16[192,2048]{1,0:T(8,128)(2,1)S(1)}, bf16[192,2048]{1,0:T(8,128)(2,1)S(1)}, u32[]{:S(2)}, u32[]{:S(2)}) collective-permute-start(bf16[192,2048]{1,0:T(8,128)(2,1)S(1)} %collective-permute-done.1.refs_3_.refs_1_), channel_id=1, source_target_pairs={{0,1},{1,2},{2,3},{3,0},{4,5},{5,6},{6,7},{7,4},{8,9},{9,10},{10,1... | collective-permute-start | bytes 2359304 | tf_op jit(solution)/shard_map/ppermute | solution.py:383
  64.2 1.2 copy-start.3
  81.4 33.7 %collective-permute-start.4 = (bf16[192,2048]{1,0:T(8,128)(2,1)S(1)}, bf16[192,2048]{1,0:T(8,128)(2,1)S(1)}, u32[]{:S(2)}, u32[]{:S(2)}) collective-permute-start(bf16[192,2048]{1,0:T(8,128)(2,1)S(1)} %collective-permute-done.2.refs_0_), channel_id=1, source_target_pairs={{0,1},{1,2},{2,3},{3,0},{4,5},{5,6},{6,7},{7,4},{8,9},{9,10},{10,1... | collective-permute-start | bytes 2359304 | tf_op jit(solution)/shard_map/ppermute | solution.py:383
  81.4 1.7 copy-start.27
  95.9 19.2 %collective-permute-start.10 = (bf16[2,384,512]{2,1,0:T(8,128)(2,1)S(1)}, bf16[2,384,512]{2,1,0:T(8,128)(2,1)S(1)}, u32[]{:S(2)}, u32[]{:S(2)}) collective-permute-start(bf16[2,384,512]{2,1,0:T(8,128)(2,1)S(1)} %get-tuple-element.47), channel_id=1, source_target_pairs={{0,8},{4,12},{8,0},{12,4},{16,24},{20,28},{24,16},{28,20},{1,9},{5... | collective-permute-start | bytes 2359304 | tf_op jit(solution)/shard_map/ppermute | solution.py:211
  97.4 18.5 %collective-permute-start.11 = (bf16[2,384,512]{2,1,0:T(8,128)(2,1)S(1)}, bf16[2,384,512]{2,1,0:T(8,128)(2,1)S(1)}, u32[]{:S(2)}, u32[]{:S(2)}) collective-permute-start(bf16[2,384,512]{2,1,0:T(8,128)(2,1)S(1)} %get-tuple-element.48), channel_id=1, source_target_pairs={{0,16},{4,20},{8,24},{12,28},{16,0},{20,4},{24,8},{28,12},{1,17},{... | collective-permute-start | bytes 2359304 | tf_op jit(solution)/shard_map/ppermute | solution.py:211
  99.0 32.6 %collective-permute-start.5 = (bf16[192,2048]{1,0:T(8,128)(2,1)S(1)}, bf16[192,2048]{1,0:T(8,128)(2,1)S(1)}, u32[]{:S(2)}, u32[]{:S(2)}) collective-permute-start(bf16[192,2048]{1,0:T(8,128)(2,1)S(1)} %collective-permute-done.3.refs_1_), channel_id=1, source_target_pairs={{0,1},{1,2},{2,3},{3,0},{4,5},{5,6},{6,7},{7,4},{8,9},{9,10},{10,1... | collective-permute-start | bytes 2359304 | tf_op jit(solution)/shard_map/ppermute | solution.py:383
  115.9 1.4 copy-start.18
  117.3 1.4 copy-start.19
  118.9 13.3 %collective-permute-start.12 = (bf16[1,384,512]{2,1,0:T(8,128)(2,1)S(1)}, bf16[1,384,512]{2,1,0:T(8,128)(2,1)S(1)}, u32[]{:S(2)}, u32[]{:S(2)}) collective-permute-start(bf16[1,384,512]{2,1,0:T(8,128)(2,1)S(1)} %get-tuple-element.53), channel_id=1, source_target_pairs={{0,16},{4,20},{8,24},{12,28},{16,0},{20,4},{24,8},{28,12},{1,17},{... | collective-permute-start | bytes 1179656 | tf_op jit(solution)/shard_map/ppermute | solution.py:211
  120.6 11.7 %collective-permute-start.13 = (bf16[1,384,512]{2,1,0:T(8,128)(2,1)S(1)}, bf16[1,384,512]{2,1,0:T(8,128)(2,1)S(1)}, u32[]{:S(2)}, u32[]{:S(2)}) collective-permute-start(bf16[1,384,512]{2,1,0:T(8,128)(2,1)S(1)} %get-tuple-element.54), channel_id=1, source_target_pairs={{0,8},{4,12},{8,0},{12,4},{16,24},{20,28},{24,16},{28,20},{1,9},{5... | collective-permute-start | bytes 1179656 | tf_op jit(solution)/shard_map/ppermute | solution.py:211
  134.5 163.8 %all-gather.11.cloned.1.call-start = ((), (), s32[]{:S(2)}) async-start(), calls=%async_computation.2 | async-start | bytes 7077888 | tf_op jit(solution)/shard_map/all_gather | solution.py:401
  134.5 10.7 %copy-start.21 = (bf16[384,2048]{1,0:T(8,128)(2,1)S(1)}, bf16[384,2048]{1,0:T(8,128)(2,1)}, u32[]{:S(2)}) copy-start(bf16[384,2048]{1,0:T(8,128)(2,1)} %param.4) | copy-start | bytes 4718596
  145.2 1.4 copy-start.10
  145.2 6.0 %collective-permute-start.6 = (bf16[4,768,512]{2,1,0:T(8,128)(2,1)}, bf16[4,768,512]{2,1,0:T(8,128)(2,1)}, u32[]{:S(2)}, u32[]{:S(2)}) collective-permute-start(bf16[4,768,512]{2,1,0:T(8,128)(2,1)} %products_sent.2), channel_id=1, source_target_pairs={{0,4},{4,0},{8,12},{12,8},{16,20},{20,16},{24,28},{28,24},{1,5},{5... | collective-permute-start | bytes 9437192 | tf_op jit(solution)/shard_map/ppermute | solution.py:131
  150.8 42.1 %collective-permute-start.14 = (bf16[512,768]{1,0:T(8,128)(2,1)}, bf16[512,768]{1,0:T(8,128)(2,1)}, u32[]{:S(2)}, u32[]{:S(2)}) collective-permute-start(bf16[512,768]{1,0:T(8,128)(2,1)} %get-tuple-element.58.refs_2_), channel_id=1, source_target_pairs={{0,1},{1,2},{2,3},{3,0},{4,5},{5,6},{6,7},{7,4},{8,9},{9,10},{10,1... | collective-permute-start | bytes 2359304 | tf_op jit(solution)/shard_map/ppermute | solution.py:390
  162.9 34.2 %collective-permute-start.8 = (bf16[2,384,512]{2,1,0:T(8,128)(2,1)S(1)}, bf16[2,384,512]{2,1,0:T(8,128)(2,1)S(1)}, u32[]{:S(2)}, u32[]{:S(2)}) collective-permute-start(bf16[2,384,512]{2,1,0:T(8,128)(2,1)S(1)} %get-tuple-element.44), channel_id=1, source_target_pairs={{0,16},{4,20},{8,24},{12,28},{16,0},{20,4},{24,8},{28,12},{1,17},{... | collective-permute-start | bytes 2359304 | tf_op jit(solution)/shard_map/ppermute | solution.py:211
  164.4 35.2 %collective-permute-start.7 = (bf16[2,384,512]{2,1,0:T(8,128)(2,1)S(1)}, bf16[2,384,512]{2,1,0:T(8,128)(2,1)S(1)}, u32[]{:S(2)}, u32[]{:S(2)}) collective-permute-start(bf16[2,384,512]{2,1,0:T(8,128)(2,1)S(1)} %get-tuple-element.43), channel_id=1, source_target_pairs={{0,8},{4,12},{8,0},{12,4},{16,24},{20,28},{24,16},{28,20},{1,9},{5... | collective-permute-start | bytes 2359304 | tf_op jit(solution)/shard_map/ppermute | solution.py:211
  166.4 37.3 %collective-permute-start.18 = (bf16[512,768]{1,0:T(8,128)(2,1)}, bf16[512,768]{1,0:T(8,128)(2,1)S(1)}, u32[]{:S(2)}, u32[]{:S(2)}) collective-permute-start(bf16[512,768]{1,0:T(8,128)(2,1)} %get-tuple-element.58.refs_2_), channel_id=1, source_target_pairs={{0,3},{1,0},{2,1},{3,2},{4,7},{5,4},{6,5},{7,6},{8,11},{9,8},{10,9... | collective-permute-start | bytes 2359304 | tf_op jit(solution)/shard_map/ppermute | solution.py:390
  170.1 52.5 %collective-permute-start.17 = (bf16[512,768]{1,0:T(8,128)(2,1)}, bf16[512,768]{1,0:T(8,128)(2,1)S(1)}, u32[]{:S(2)}, u32[]{:S(2)}) collective-permute-start(bf16[512,768]{1,0:T(8,128)(2,1)} %get-tuple-element.58.refs_2_), channel_id=1, source_target_pairs={{0,2},{1,3},{2,0},{3,1},{4,6},{5,7},{6,4},{7,5},{8,10},{9,11},{10,... | collective-permute-start | bytes 2359304 | tf_op jit(solution)/shard_map/ppermute | solution.py:390
  170.1 32.3 %slice-start = ((s8[6291456]{0:T(1024)(128)(4,1)}), s8[4194304]{0:T(1024)(128)(4,1)S(1)}, s32[]{:S(2)}) async-start(s8[6291456]{0:T(1024)(128)(4,1)} %bitcast.25), calls=%async_computation.3 | async-start | bytes 8388608
  170.3 29.3 %copy-start.16 = (f32[2,384,512]{2,1,0:T(8,128)S(1)}, f32[2,384,512]{2,1,0:T(8,128)}, u32[]{:S(2)}) copy-start(f32[2,384,512]{2,1,0:T(8,128)} %get-tuple-element.42.refs_0_) | copy-start | bytes 4718596
  170.3 29.3 %copy-start.17 = (f32[2,384,512]{2,1,0:T(8,128)S(1)}, f32[2,384,512]{2,1,0:T(8,128)}, u32[]{:S(2)}) copy-start(f32[2,384,512]{2,1,0:T(8,128)} %get-tuple-element.61.refs_2_) | copy-start | bytes 4718596
  170.4 32.1 %slice-start.1 = ((s8[6291456]{0:T(1024)(128)(4,1)}), s8[2097152]{0:T(1024)(128)(4,1)S(1)}, s32[]{:S(2)}) async-start(s8[6291456]{0:T(1024)(128)(4,1)} %bitcast.25), calls=%async_computation.4 | async-start | bytes 4194304
  189.6 3.3 copy-start
  199.9 22.7 %collective-permute-start.15 = (bf16[1,384,512]{2,1,0:T(8,128)(2,1)S(1)}, bf16[1,384,512]{2,1,0:T(8,128)(2,1)S(1)}, u32[]{:S(2)}, u32[]{:S(2)}) collective-permute-start(bf16[1,384,512]{2,1,0:T(8,128)(2,1)S(1)} %get-tuple-element.64), channel_id=1, source_target_pairs={{0,16},{4,20},{8,24},{12,28},{16,0},{20,4},{24,8},{28,12},{1,17},{... | collective-permute-start | bytes 1179656 | tf_op jit(solution)/shard_map/ppermute | solution.py:211
  200.0 22.6 %collective-permute-start.16 = (bf16[1,384,512]{2,1,0:T(8,128)(2,1)S(1)}, bf16[1,384,512]{2,1,0:T(8,128)(2,1)S(1)}, u32[]{:S(2)}, u32[]{:S(2)}) collective-permute-start(bf16[1,384,512]{2,1,0:T(8,128)(2,1)S(1)} %get-tuple-element.65), channel_id=1, source_target_pairs={{0,8},{4,12},{8,0},{12,4},{16,24},{20,28},{24,16},{28,20},{1,9},{5... | collective-permute-start | bytes 1179656 | tf_op jit(solution)/shard_map/ppermute | solution.py:211
  203.7 23.9 %copy-start.22 = (bf16[512,768]{1,0:T(8,128)(2,1)}, bf16[512,768]{1,0:T(8,128)(2,1)S(1)}, u32[]{:S(2)}) copy-start(bf16[512,768]{1,0:T(8,128)(2,1)S(1)} %collective-permute-done.18.refs_5_) | copy-start | bytes 2359300
  222.6 5.0 %copy-start.23 = (bf16[512,768]{1,0:T(8,128)(2,1)}, bf16[512,768]{1,0:T(8,128)(2,1)S(1)}, u32[]{:S(2)}) copy-start(bf16[512,768]{1,0:T(8,128)(2,1)S(1)} %collective-permute-done.17.refs_4_) | copy-start | bytes 2359300
  223.8 14.2 %copy-start.20 = (bf16[512,768]{1,0:T(8,128)(2,1)}, bf16[512,768]{1,0:T(8,128)(2,1)S(1)}, u32[]{:S(2)}) copy-start(bf16[512,768]{1,0:T(8,128)(2,1)S(1)} %get-tuple-element.69.refs_2_) | copy-start | bytes 2359300
  230.4 58.7 %collective-permute-start.21 = (bf16[512,768]{1,0:T(8,128)(2,1)S(1)}, bf16[512,768]{1,0:T(8,128)(2,1)S(1)}, u32[]{:S(2)}, u32[]{:S(2)}) collective-permute-start(bf16[512,768]{1,0:T(8,128)(2,1)S(1)} %get-tuple-element.69.refs_2_), channel_id=1, source_target_pairs={{0,3},{1,0},{2,1},{3,2},{4,7},{5,4},{6,5},{7,6},{8,11},{9,8},{10,9... | collective-permute-start | bytes 2359304 | tf_op jit(solution)/shard_map/ppermute | solution.py:390
  233.2 65.1 %collective-permute-start.20 = (bf16[512,768]{1,0:T(8,128)(2,1)S(1)}, bf16[512,768]{1,0:T(8,128)(2,1)S(1)}, u32[]{:S(2)}, u32[]{:S(2)}) collective-permute-start(bf16[512,768]{1,0:T(8,128)(2,1)S(1)} %get-tuple-element.69.refs_2_), channel_id=1, source_target_pairs={{0,2},{1,3},{2,0},{3,1},{4,6},{5,7},{6,4},{7,5},{8,10},{9,11},{10,... | collective-permute-start | bytes 2359304 | tf_op jit(solution)/shard_map/ppermute | solution.py:390
  233.2 65.1 %collective-permute-start.19 = (bf16[512,768]{1,0:T(8,128)(2,1)S(1)}, bf16[512,768]{1,0:T(8,128)(2,1)S(1)}, u32[]{:S(2)}, u32[]{:S(2)}) collective-permute-start(bf16[512,768]{1,0:T(8,128)(2,1)S(1)} %get-tuple-element.69.refs_2_), channel_id=1, source_target_pairs={{0,1},{1,2},{2,3},{3,0},{4,5},{5,6},{6,7},{7,4},{8,9},{9,10},{10,1... | collective-permute-start | bytes 2359304 | tf_op jit(solution)/shard_map/ppermute | solution.py:390
  289.1 9.2 %copy-start.24 = (bf16[512,768]{1,0:T(8,128)(2,1)}, bf16[512,768]{1,0:T(8,128)(2,1)S(1)}, u32[]{:S(2)}) copy-start(bf16[512,768]{1,0:T(8,128)(2,1)S(1)} %collective-permute-done.21.refs_5_) | copy-start | bytes 2359300
  298.2 1.2 copy-start.26
  (7 other events, 7.8 us)
Sparse Core Ops, SparseCore 0:
  48.8 44.9 all-gather.6
  134.6 92.9 all-gather.8
  229.5 45.3 all-gather.10

commit v3 on v2

--- a/solution.py
+++ b/solution.py
@@ -254,7 +254,7 @@
     rows = row_ref.shape[0]
     per_block = sub_width // LANES
     blocks = SUBS // per_block
-    width = min(sub_width, 256)
+    width = min(sub_width, 512)
     distance = pl.program_id(1)
     native = (out_ref if last else old_ref).reshape(rows * SUBS, LANES)
     row_rate = jnp.broadcast_to(row_ref[...], (rows, LANES))
@@ -392,15 +392,25 @@
     def square_sum(pieces, axis):
         return sum(jnp.sum(jnp.square(p.astype(jnp.float32)), axis=axis) for p in pieces)
 
+    def entry_rows(block, at):
+        return block[:, at * part : (at + 1) * part]
+
     sums, signs = [], []
 
     def complete(length):
         return len(xs) >= length and len(xs[length - 1]) == PIECES
 
+    def columns(entries):
+        return [
+            lax.dynamic_slice_in_dim(x, col_index * sub_width, sub_width, 1)
+            for pieces in entries
+            for x in pieces
+        ]
+
     def gather(rows):
         return lax.all_gather(jnp.concatenate(rows, axis=0), "row", axis=0, tiled=False)
 
-    x_cols, y_cols, waiting = [], [], []
+    x_cols, y_cols, waiting, marks = [], [], [], []
     for k in range(GROUPS):
         first = k * per_group
         while not complete(first + per_group):
@@ -408,22 +418,22 @@
         if not k:
             xs[-1] = tie(xs[-1], [weights])
         group = xs[first : first + per_group]
-        own = [
-            lax.dynamic_slice_in_dim(x, col_index * sub_width, sub_width, 1)
-            for pieces in group
-            for x in pieces
-        ]
-        block = gather(own + waiting)
-        x_cols.append((block, 0))
-        if waiting:
-            y_cols.append((block, 1))
+        if k:
+            block = gather(columns(tie(group[:-1], [marks[1], x_cols[-1][0]])))
+            x_cols.extend((block, s) for s in range(per_group - 1))
+            block = gather(tie(columns(group[-1:]) + waiting, [block]))
+            x_cols.append((block, 0))
+            y_cols.append([(block, 1 + s) for s in range(per_group)])
+        else:
+            block = gather(columns(group))
+            x_cols.extend((block, s) for s in range(per_group))
 
         def beside(exchange, sent):
             done = []
+            marks.append(sent)
             if exchange == 0:
                 x_turned.extend(turn(x, sub_width) for x in group)
                 done.extend(x_turned[first:])
-                done.extend(block for block, _ in x_cols[:-1])
             for _ in range(X_STEPS[min(exchange, len(X_STEPS) - 1)]):
                 if not complete(col_count):
                     done.append(advance())
@@ -434,7 +444,7 @@
             if y_planes and exchange == 2:
                 done.extend(y_planes[0][2:])
                 sums.append(square_sum([x for pieces in xs for x in pieces], 0))
-                sums.append(square_sum([x_cols[0][0]], 1))
+                sums.append(square_sum([entry_rows(*entry) for entry in x_cols[:-1]], 1))
                 done.extend(sums)
             return done
 
@@ -449,31 +459,28 @@
         waiting = [share]
         y_planes.append([to_distance(turned, distance) for distance in range(col_count)])
     last = gather(tie(waiting, [x_cols[-1][0]]))
-    y_cols.append((last, 0))
-    group_rows = part * per_group
+    y_cols.append([(last, s) for s in range(per_group)])
 
     def scale_of(total):
         total = lax.optimization_barrier(total) / sample_total + 1e-06
         return lax.optimization_barrier(total.astype(jnp.bfloat16)).astype(jnp.float32)
 
     row_sum, col_sum = sums
-    col_sum = col_sum + square_sum([block[:, :group_rows] for block, _ in x_cols[1:]], 1)
+    col_sum = col_sum + square_sum([entry_rows(*x_cols[-1])], 1)
     row_rate = (step_size[0] * lax.rsqrt(scale_of(row_sum)))[:, None]
     col_rate = lax.rsqrt(scale_of(col_sum)).reshape(1, lane_tiles * LANES)
 
     planes = (col_index - jnp.arange(col_count, dtype=jnp.int32) + col_count) % col_count
     info = jnp.concatenate([row_index[None], planes])
-    x_entries = [(block, at * per_group + s) for block, at in x_cols for s in range(per_group)]
     updated = omega3
     for k in range(GROUPS):
-        block, at = y_cols[k]
         first = k * per_group
         updated = update(
             k,
             x_turned[first : first + per_group],
             y_planes[k],
-            [(block, at * per_group + s) for s in range(per_group)],
-            x_entries,
+            y_cols[k],
+            x_cols,
             updated,
             row_rate,
             col_rate,

time: 362 us -> 369 us (1.019)
  waiting for transfers between devices: 89.6 us -> 96 us
    ppermute x8, waiting for transfers between devices: 7.5 us -> 18.4 us  [sum_over_rows(): lax.ppermute(sent, 'row', row_partner(mask))]
    ppermute x6, waiting for transfers between devices: 28 us -> 20.8 us  [to_distance(): lax.ppermute(y, 'col', [(c, (c + distance) % col_count) for c in range(co...]
  transfers between devices with their start and end apart: 25 -> 26, of which waited for: 11 -> 14; matrix products, arithmetic and copies ran while one was open for 4% -> 2% of each run, Pallas kernels for 39% -> 38%
where the time goes in v3:
time: 369 us; the launch traced here: 368 us
  Pallas kernels  194 us (53%)
  waiting for transfers between devices  96 us (26%)
  local copies, waits for them, and re-layouts  29.8 us (8%)
  starting transfers between devices  23.2 us (6%)
  between operations  14.2 us (4%)
  other arithmetic  10.7 us (3%)
    pallas_call x2, Pallas kernels, update(): pl.pallas_call(functools.partial(update_kernel, sizes, group, sub_width,...  105 us
    ppermute x6, waiting for transfers between devices, advance(): done = lax.ppermute(xs[-2][len(xs[-1])], 'col', ring)  51.9 us
    unnamed x65, local copies, waits for them, and re-layouts  26.8 us
    pallas_call x2, Pallas kernels, pair_products(): pl.pallas_call(functools.partial(kept_kernel, count, bits), grid_spec=plt...  24.2 us
    pallas_call x2, Pallas kernels, pair_products(): pl.pallas_call(functools.partial(sent_kernel, count), grid_spec=pltpu.Pre...  21.1 us
    ppermute x6, waiting for transfers between devices, to_distance(): lax.ppermute(y, 'col', [(c, (c + distance) % col_count) for c in range(co...  20.8 us
    pallas_call x1, Pallas kernels, convert(): pl.pallas_call(convert_kernel, grid=(row_total // tile, lane_tiles // SUB...  19.2 us
    pallas_call x1, Pallas kernels, narrow(): pl.pallas_call(narrow_kernel, grid=(row_total // tile, lane_tiles // SUBS...  18.6 us
  transfers between devices with their start and end apart: 26, of which 14 were waited for; matrix products, arithmetic and copies ran while one was open for 2% of the time, Pallas kernels for 38%

profile of v3, /device:TPU:0, one launch (start us, length us, event | category | flops | bytes accessed | tf_op | source)
XLA Modules:
  0.0 367.6 jit_solution(3661438411628006608)
XLA Ops:
  6.5 1.5 fusion.2
  8.0 3.1 collective-permute-start.1
  11.1 1.6 collective-permute-start
  12.7 19.2 %omega_to_bf16.1.refs_4_ = bf16[8,2048,512]{2,1,0:T(8,128)(2,1)S(1)} custom-call(f32[2048,32,128]{2,1,0:T(8,128)} %bitcast.27), custom_call_target="tpu_custom_call" | custom-call | bytes 50331648 | tf_op jit(solution)/shard_map/omega_to_bf16/pallas_call | solution.py:34
  31.9 6.2 %copy-done.1 = bf16[8,2048,512]{2,1,0:T(8,128)(2,1)} copy-done((bf16[8,2048,512]{2,1,0:T(8,128)(2,1)}, bf16[8,2048,512]{2,1,0:T(8,128)(2,1)S(1)}, u32[]{:S(2)}) %copy-start.1) | copy-done | bytes 16777240
  38.1 9.5 %collective-permute-done.refs_2_.refs_0_ = bf16[192,2048]{1,0:T(8,128)(2,1)S(1)} collective-permute-done((bf16[192,2048]{1,0:T(8,128)(2,1)S(1)}, bf16[192,2048]{1,0:T(8,128)(2,1)S(1)}, u32[]{:S(2)}, u32[]{:S(2)}) %collective-permute-start) | collective-permute-done | bytes 786464 | tf_op jit(solution)/shard_map/ppermute | solution.py:383
  48.7 10.6 %products_sent.3 = bf16[4,768,512]{2,1,0:T(8,128)(2,1)} custom-call(s32[4]{0:T(128)S(1)} %get-tuple-element.89.order_ref, bf16[192,2048]{1,0:T(8,128)(2,1)S(1)} %get-tuple-element.92.refs_0_, bf16[192,2048]{1,0:T(8,128)(2,1)S(1)} %get-tuple-element.91.refs_1_, bf16[192,2048]{1,0:T(8,128)(2,1)S(1)} %collective-permute-done.refs_2_.refs_0_, ...), custom_call_target="tpu_custom_call" | custom-call | flops 6442450944 | bytes 14680064 | tf_op jit(solution)/shard_map/products_sent/pallas_call | solution.py:118
  60.3 1.1 copy-done.11
  63.4 1.2 copy-done.2
  65.4 1.2 copy-done.3
  66.5 14.9 %collective-permute-done.2.refs_0_ = bf16[192,2048]{1,0:T(8,128)(2,1)S(1)} collective-permute-done((bf16[192,2048]{1,0:T(8,128)(2,1)S(1)}, bf16[192,2048]{1,0:T(8,128)(2,1)S(1)}, u32[]{:S(2)}, u32[]{:S(2)}) %collective-permute-start.2) | collective-permute-done | bytes 786464 | tf_op jit(solution)/shard_map/ppermute | solution.py:383
  81.4 1.6 copy-done.29
  83.1 12.2 %products_kept.3 = (bf16[2,384,512]{2,1,0:T(8,128)(2,1)}, f32[2,384,512]{2,1,0:T(8,128)}, bf16[2,384,512]{2,1,0:T(8,128)(2,1)}, f32[2,384,512]{2,1,0:T(8,128)}) custom-call(s32[4]{0:T(128)S(1)} %get-tuple-element.90.order_ref, bf16[192,2048]{1,0:T(8,128)(2,1)S(1)} %copy-done.15, bf16[192,2048]{1,0:T(8,128)(2,1)S(1)} %copy-done.12, ...), custom_call_target="tpu_custom_call" | custom-call | flops 6442450944 | bytes 14680064 | tf_op jit(solution)/shard_map/products_kept/pallas_call | solution.py:134
  95.3 2.6 collective-permute-done.3.refs_1_
  98.8 1.6 collective-permute-start.11
  100.4 1.5 collective-permute-start.10
  101.9 19.2 %collective-permute-done.4.refs_0_.refs_2_ = bf16[192,2048]{1,0:T(8,128)(2,1)S(1)} collective-permute-done((bf16[192,2048]{1,0:T(8,128)(2,1)S(1)}, bf16[192,2048]{1,0:T(8,128)(2,1)S(1)}, u32[]{:S(2)}, u32[]{:S(2)}) %collective-permute-start.4) | collective-permute-done | bytes 786464 | tf_op jit(solution)/shard_map/ppermute | solution.py:383
  121.1 1.4 collective-permute-done.11.refs_3_
  122.5 2.7 collective-permute-done.10.refs_1_
  125.2 1.4 copy-done.16
  126.6 1.4 copy-done.17
  128.4 2.5 collective-permute-start.13
  130.9 5.8 %collective-permute-done.5.refs_1_.refs_3_ = bf16[192,2048]{1,0:T(8,128)(2,1)S(1)} collective-permute-done((bf16[192,2048]{1,0:T(8,128)(2,1)S(1)}, bf16[192,2048]{1,0:T(8,128)(2,1)S(1)}, u32[]{:S(2)}, u32[]{:S(2)}) %collective-permute-start.5) | collective-permute-done | bytes 786464 | tf_op jit(solution)/shard_map/ppermute | solution.py:383
  136.7 3.8 %collective-permute-done.12.refs_1_ = bf16[1,384,512]{2,1,0:T(8,128)(2,1)S(1)} collective-permute-done((bf16[1,384,512]{2,1,0:T(8,128)(2,1)S(1)}, bf16[1,384,512]{2,1,0:T(8,128)(2,1)S(1)}, u32[]{:S(2)}, u32[]{:S(2)}) %collective-permute-start.12) | collective-permute-done | bytes 393248 | tf_op jit(solution)/shard_map/ppermute | solution.py:211
  140.6 1.2 share.2
  142.7 2.2 pad_maximum_fusion
  145.0 10.5 %products_sent.2 = bf16[4,768,512]{2,1,0:T(8,128)(2,1)} custom-call(s32[4]{0:T(128)S(1)} %get-tuple-element.89.order_ref, bf16[192,2048]{1,0:T(8,128)(2,1)S(1)} %collective-permute-done.2.refs_0_, bf16[192,2048]{1,0:T(8,128)(2,1)S(1)} %collective-permute-done.3.refs_1_, bf16[192,2048]{1,0:T(8,128)(2,1)S(1)} %collective-permute-done.4.refs_0_.refs_2_, ...), custom_call_target="tpu_custom_call" | custom-call | flops 6442450944 | bytes 14680064 | tf_op jit(solution)/shard_map/products_sent/pallas_call | solution.py:118
  158.1 1.1 copy-done.4
  160.0 1.2 copy-done.5
  161.2 1.4 collective-permute-start.14
  162.6 1.7 copy-done.28
  164.2 12.0 %products_kept.2 = (bf16[2,384,512]{2,1,0:T(8,128)(2,1)S(1)}, f32[2,384,512]{2,1,0:T(8,128)}, bf16[2,384,512]{2,1,0:T(8,128)(2,1)S(1)}, f32[2,384,512]{2,1,0:T(8,128)}) custom-call(s32[4]{0:T(128)S(1)} %get-tuple-element.90.order_ref, bf16[192,2048]{1,0:T(8,128)(2,1)S(1)} %collective-permute-done.2.refs_0_, ...), custom_call_target="tpu_custom_call" | custom-call | flops 6442450944 | bytes 14680064 | tf_op jit(solution)/shard_map/products_kept/pallas_call | solution.py:134
  176.2 1.4 collective-permute-start.8
  178.8 2.6 collective-permute-start.18
  182.0 18.6 %narrow_signs.1.refs_15_ = s8[2048,4096]{1,0:T(32,128)(4,1)S(1)} custom-call(s32[2048,32,128]{2,1,0:T(8,128)} %bitcast.29), custom_call_target="tpu_custom_call" | custom-call | bytes 41943040 | tf_op jit(solution)/shard_map/narrow_signs/pallas_call | solution.py:231
  200.6 3.2 copy-done
  203.8 8.9 %collective-permute-done.8.refs_3_ = bf16[2,384,512]{2,1,0:T(8,128)(2,1)S(1)} collective-permute-done((bf16[2,384,512]{2,1,0:T(8,128)(2,1)S(1)}, bf16[2,384,512]{2,1,0:T(8,128)(2,1)S(1)}, u32[]{:S(2)}, u32[]{:S(2)}) %collective-permute-start.8) | collective-permute-done | bytes 786464 | tf_op jit(solution)/shard_map/ppermute | solution.py:211
  212.7 1.5 collective-permute-done.7.refs_1_
  215.0 1.5 collective-permute-start.16
  216.5 1.3 multiply_reduce_fusion.2
  219.1 4.9 %all-gather.13.cloned.1.call-done = bf16[9216,512]{1,0:T(8,128)(2,1)} async-done(((bf16[1152,512]{1,0:T(8,128)(2,1)}), bf16[9216,512]{1,0:T(8,128)(2,1)}) %all-gather.13.cloned.1.call-update) | async-done | bytes 9437200 | tf_op jit(solution)/shard_map/all_gather | solution.py:411
  224.0 2.5 multiply_reduce_fusion
  226.6 6.2 %collective-permute-done.17.refs_4_ = bf16[512,768]{1,0:T(8,128)(2,1)} collective-permute-done((bf16[512,768]{1,0:T(8,128)(2,1)}, bf16[512,768]{1,0:T(8,128)(2,1)}, u32[]{:S(2)}, u32[]{:S(2)}) %collective-permute-start.17) | collective-permute-done | bytes 786464 | tf_op jit(solution)/shard_map/ppermute | solution.py:390
  235.3 1.4 copy.6.refs_13_
  236.6 2.7 collective-permute-start.21
  240.6 50.5 %first_terms.1.refs_12_ = bf16[2048,4096]{1,0:T(8,128)(2,1)} custom-call(s32[5]{0:T(128)} %pad_add_fusion.info_ref, bf16[2048,384]{1,0:T(8,128)(2,1)} %copy-done.2, bf16[2048,384]{1,0:T(8,128)(2,1)} %copy-done.3, bf16[512,768]{1,0:T(8,128)(2,1)} %get-tuple-element.63.refs_2_, bf16[512,768]{1,0:T(8,128)(2,1)} %copy-done.24, ...), custom_call_target="tpu_custom_call" | custom-call | flops 25769803776 | bytes 67108864 | tf_op jit(solution)/shard_map/first_terms/pallas_call | solution.py:326
  291.1 14.5 %collective-permute-done.20.refs_4_ = bf16[512,768]{1,0:T(8,128)(2,1)S(1)} collective-permute-done((bf16[512,768]{1,0:T(8,128)(2,1)S(1)}, bf16[512,768]{1,0:T(8,128)(2,1)S(1)}, u32[]{:S(2)}, u32[]{:S(2)}) %collective-permute-start.20) | collective-permute-done | bytes 786464 | tf_op jit(solution)/shard_map/ppermute | solution.py:390
  306.9 54.2 %last_terms.1 = f32[2048,32,128]{2,1,0:T(8,128)} custom-call(s32[5]{0:T(128)} %pad_add_fusion.info_ref, bf16[2048,384]{1,0:T(8,128)(2,1)} %copy-done.4, bf16[2048,384]{1,0:T(8,128)(2,1)} %copy-done.5, bf16[512,768]{1,0:T(8,128)(2,1)} %copy-done.20, bf16[512,768]{1,0:T(8,128)(2,1)} %copy-done.27, bf16[512,768]{1,0:T(8,128)(2,1)} %copy-done.26, ...), custom_call_target="tpu_custom_call" | custom-call | flops 25769803776 | bytes 67108864 | tf_op jit(solution)/shard_map/last_terms/pallas_call | solution.py:326
  (119 shorter events, 18.5 us)
Async XLA Ops:
  6.5 91.3 %all-gather.9.cloned.1.call-start = ((), (), s32[]{:S(2)}) async-start(), calls=%async_computation | async-start | bytes 7077888 | tf_op jit(solution)/shard_map/all_gather | solution.py:411
  8.0 40.7 %copy-start.10 = (bf16[192,2048]{1,0:T(8,128)(2,1)}, bf16[192,2048]{1,0:T(8,128)(2,1)S(1)}, u32[]{:S(2)}) copy-start(bf16[192,2048]{1,0:T(8,128)(2,1)S(1)} %get-tuple-element.91.refs_1_) | copy-start | bytes 2359300
  8.0 40.7 %copy-start.13 = (bf16[192,2048]{1,0:T(8,128)(2,1)}, bf16[192,2048]{1,0:T(8,128)(2,1)S(1)}, u32[]{:S(2)}) copy-start(bf16[192,2048]{1,0:T(8,128)(2,1)S(1)} %get-tuple-element.92.refs_0_) | copy-start | bytes 2359300
  8.0 30.0 %collective-permute-start.1 = (bf16[192,2048]{1,0:T(8,128)(2,1)S(1)}, bf16[192,2048]{1,0:T(8,128)(2,1)S(1)}, u32[]{:S(2)}, u32[]{:S(2)}) collective-permute-start(bf16[192,2048]{1,0:T(8,128)(2,1)S(1)} %get-tuple-element.91.refs_1_), channel_id=1, source_target_pairs={{0,1},{1,2},{2,3},{3,0},{4,5},{5,6},{6,7},{7,4},{8,9},{9,10},{10,1... | collective-permute-start | bytes 2359304 | tf_op jit(solution)/shard_map/ppermute | solution.py:383
  11.1 36.4 %collective-permute-start = (bf16[192,2048]{1,0:T(8,128)(2,1)S(1)}, bf16[192,2048]{1,0:T(8,128)(2,1)S(1)}, u32[]{:S(2)}, u32[]{:S(2)}) collective-permute-start(bf16[192,2048]{1,0:T(8,128)(2,1)S(1)} %get-tuple-element.92.refs_0_), channel_id=1, source_target_pairs={{0,1},{1,2},{2,3},{3,0},{4,5},{5,6},{6,7},{7,4},{8,9},{9,10},{10,1... | collective-permute-start | bytes 2359304 | tf_op jit(solution)/shard_map/ppermute | solution.py:383
  31.8 6.2 %copy-start.1 = (bf16[8,2048,512]{2,1,0:T(8,128)(2,1)}, bf16[8,2048,512]{2,1,0:T(8,128)(2,1)S(1)}, u32[]{:S(2)}) copy-start(bf16[8,2048,512]{2,1,0:T(8,128)(2,1)S(1)} %omega_to_bf16.1.refs_4_) | copy-start | bytes 50331652
  38.1 43.4 %copy-start.6 = (bf16[192,2048]{1,0:T(8,128)(2,1)}, bf16[192,2048]{1,0:T(8,128)(2,1)S(1)}, u32[]{:S(2)}) copy-start(bf16[192,2048]{1,0:T(8,128)(2,1)S(1)} %collective-permute-done.1.refs_3_.refs_1_) | copy-start | bytes 2359300
  47.5 33.9 %copy-start.8 = (bf16[192,2048]{1,0:T(8,128)(2,1)}, bf16[192,2048]{1,0:T(8,128)(2,1)S(1)}, u32[]{:S(2)}) copy-start(bf16[192,2048]{1,0:T(8,128)(2,1)S(1)} %collective-permute-done.refs_2_.refs_0_) | copy-start | bytes 2359300
  48.6 94.0 %all-gather.11.cloned.1.call-start = ((), (), s32[]{:S(2)}) async-start(), calls=%async_computation.1 | async-start | bytes 3538944 | tf_op jit(solution)/shard_map/all_gather | solution.py:411
  59.3 22.1 %collective-permute-start.9 = (bf16[4,768,512]{2,1,0:T(8,128)(2,1)}, bf16[4,768,512]{2,1,0:T(8,128)(2,1)S(1)}, u32[]{:S(2)}, u32[]{:S(2)}) collective-permute-start(bf16[4,768,512]{2,1,0:T(8,128)(2,1)} %products_sent.3), channel_id=1, source_target_pairs={{0,4},{4,0},{8,12},{12,8},{16,20},{20,16},{24,28},{28,24},{1,5},{5... | collective-permute-start | bytes 9437192 | tf_op jit(solution)/shard_map/ppermute | solution.py:131
  59.3 22.1 %collective-permute-start.2 = (bf16[192,2048]{1,0:T(8,128)(2,1)S(1)}, bf16[192,2048]{1,0:T(8,128)(2,1)S(1)}, u32[]{:S(2)}, u32[]{:S(2)}) collective-permute-start(bf16[192,2048]{1,0:T(8,128)(2,1)S(1)} %collective-permute-done.refs_2_.refs_0_), channel_id=1, source_target_pairs={{0,1},{1,2},{2,3},{3,0},{4,5},{5,6},{6,7},{7,4},{8,9},{9,10},{10,1... | collective-permute-start | bytes 2359304 | tf_op jit(solution)/shard_map/ppermute | solution.py:383
  59.3 38.6 %collective-permute-start.3 = (bf16[192,2048]{1,0:T(8,128)(2,1)S(1)}, bf16[192,2048]{1,0:T(8,128)(2,1)S(1)}, u32[]{:S(2)}, u32[]{:S(2)}) collective-permute-start(bf16[192,2048]{1,0:T(8,128)(2,1)S(1)} %collective-permute-done.1.refs_3_.refs_1_), channel_id=1, source_target_pairs={{0,1},{1,2},{2,3},{3,0},{4,5},{5,6},{6,7},{7,4},{8,9},{9,10},{10,1... | collective-permute-start | bytes 2359304 | tf_op jit(solution)/shard_map/ppermute | solution.py:383
  64.5 18.5 %copy-start.12 = (bf16[192,2048]{1,0:T(8,128)(2,1)S(1)}, bf16[192,2048]{1,0:T(8,128)(2,1)}, u32[]{:S(2)}) copy-start(bf16[192,2048]{1,0:T(8,128)(2,1)} %copy-done.10) | copy-start | bytes 2359300
  64.5 18.5 %copy-start.15 = (bf16[192,2048]{1,0:T(8,128)(2,1)S(1)}, bf16[192,2048]{1,0:T(8,128)(2,1)}, u32[]{:S(2)}) copy-start(bf16[192,2048]{1,0:T(8,128)(2,1)} %copy-done.13) | copy-start | bytes 2359300
  81.4 1.7 copy-start.29
  98.7 125.3 %all-gather.13.cloned.1.call-start = ((), (), s32[]{:S(2)}) async-start(), calls=%async_computation.2 | async-start | bytes 10616832 | tf_op jit(solution)/shard_map/all_gather | solution.py:411
  98.8 22.3 %collective-permute-start.4 = (bf16[192,2048]{1,0:T(8,128)(2,1)S(1)}, bf16[192,2048]{1,0:T(8,128)(2,1)S(1)}, u32[]{:S(2)}, u32[]{:S(2)}) collective-permute-start(bf16[192,2048]{1,0:T(8,128)(2,1)S(1)} %collective-permute-done.2.refs_0_), channel_id=1, source_target_pairs={{0,1},{1,2},{2,3},{3,0},{4,5},{5,6},{6,7},{7,4},{8,9},{9,10},{10,1... | collective-permute-start | bytes 2359304 | tf_op jit(solution)/shard_map/ppermute | solution.py:383
  98.8 23.7 %collective-permute-start.11 = (bf16[2,384,512]{2,1,0:T(8,128)(2,1)}, bf16[2,384,512]{2,1,0:T(8,128)(2,1)S(1)}, u32[]{:S(2)}, u32[]{:S(2)}) collective-permute-start(bf16[2,384,512]{2,1,0:T(8,128)(2,1)} %get-tuple-element.53), channel_id=1, source_target_pairs={{0,16},{4,20},{8,24},{12,28},{16,0},{20,4},{24,8},{28,12},{1,17},{... | collective-permute-start | bytes 2359304 | tf_op jit(solution)/shard_map/ppermute | solution.py:211
  100.4 24.8 %collective-permute-start.10 = (bf16[2,384,512]{2,1,0:T(8,128)(2,1)}, bf16[2,384,512]{2,1,0:T(8,128)(2,1)S(1)}, u32[]{:S(2)}, u32[]{:S(2)}) collective-permute-start(bf16[2,384,512]{2,1,0:T(8,128)(2,1)} %get-tuple-element.52), channel_id=1, source_target_pairs={{0,8},{4,12},{8,0},{12,4},{16,24},{20,28},{24,16},{28,20},{1,9},{5... | collective-permute-start | bytes 2359304 | tf_op jit(solution)/shard_map/ppermute | solution.py:211
  101.9 34.7 %collective-permute-start.5 = (bf16[192,2048]{1,0:T(8,128)(2,1)S(1)}, bf16[192,2048]{1,0:T(8,128)(2,1)S(1)}, u32[]{:S(2)}, u32[]{:S(2)}) collective-permute-start(bf16[192,2048]{1,0:T(8,128)(2,1)S(1)} %collective-permute-done.3.refs_1_), channel_id=1, source_target_pairs={{0,1},{1,2},{2,3},{3,0},{4,5},{5,6},{6,7},{7,4},{8,9},{9,10},{10,1... | collective-permute-start | bytes 2359304 | tf_op jit(solution)/shard_map/ppermute | solution.py:383
  125.2 1.4 copy-start.16
  126.6 1.4 copy-start.17
  128.3 12.2 %collective-permute-start.12 = (bf16[1,384,512]{2,1,0:T(8,128)(2,1)S(1)}, bf16[1,384,512]{2,1,0:T(8,128)(2,1)S(1)}, u32[]{:S(2)}, u32[]{:S(2)}) collective-permute-start(bf16[1,384,512]{2,1,0:T(8,128)(2,1)S(1)} %get-tuple-element.58), channel_id=1, source_target_pairs={{0,16},{4,20},{8,24},{12,28},{16,0},{20,4},{24,8},{28,12},{1,17},{... | collective-permute-start | bytes 1179656 | tf_op jit(solution)/shard_map/ppermute | solution.py:211
  128.4 12.2 %collective-permute-start.13 = (bf16[1,384,512]{2,1,0:T(8,128)(2,1)S(1)}, bf16[1,384,512]{2,1,0:T(8,128)(2,1)S(1)}, u32[]{:S(2)}, u32[]{:S(2)}) collective-permute-start(bf16[1,384,512]{2,1,0:T(8,128)(2,1)S(1)} %get-tuple-element.59), channel_id=1, source_target_pairs={{0,8},{4,12},{8,0},{12,4},{16,24},{20,28},{24,16},{28,20},{1,9},{5... | collective-permute-start | bytes 1179656 | tf_op jit(solution)/shard_map/ppermute | solution.py:211
  144.9 160.8 %all-gather.15.cloned.1.call-start = ((), (), s32[]{:S(2)}) async-start(), calls=%async_computation.3 | async-start | bytes 7077888 | tf_op jit(solution)/shard_map/all_gather | solution.py:411
  145.0 10.6 %copy-start.23 = (bf16[384,2048]{1,0:T(8,128)(2,1)S(1)}, bf16[384,2048]{1,0:T(8,128)(2,1)}, u32[]{:S(2)}) copy-start(bf16[384,2048]{1,0:T(8,128)(2,1)} %param.4) | copy-start | bytes 4718596
  155.5 1.4 copy-start.9
  155.5 7.0 %collective-permute-start.6 = (bf16[4,768,512]{2,1,0:T(8,128)(2,1)}, bf16[4,768,512]{2,1,0:T(8,128)(2,1)S(1)}, u32[]{:S(2)}, u32[]{:S(2)}) collective-permute-start(bf16[4,768,512]{2,1,0:T(8,128)(2,1)} %products_sent.2), channel_id=1, source_target_pairs={{0,4},{4,0},{8,12},{12,8},{16,20},{20,16},{24,28},{28,24},{1,5},{5... | collective-permute-start | bytes 9437192 | tf_op jit(solution)/shard_map/ppermute | solution.py:131
  161.2 42.6 %collective-permute-start.14 = (bf16[512,768]{1,0:T(8,128)(2,1)}, bf16[512,768]{1,0:T(8,128)(2,1)S(1)}, u32[]{:S(2)}, u32[]{:S(2)}) collective-permute-start(bf16[512,768]{1,0:T(8,128)(2,1)} %get-tuple-element.63.refs_2_), channel_id=1, source_target_pairs={{0,1},{1,2},{2,3},{3,0},{4,5},{5,6},{6,7},{7,4},{8,9},{9,10},{10,1... | collective-permute-start | bytes 2359304 | tf_op jit(solution)/shard_map/ppermute | solution.py:390
  162.6 1.7 copy-start.28
  176.2 36.4 %collective-permute-start.8 = (bf16[2,384,512]{2,1,0:T(8,128)(2,1)S(1)}, bf16[2,384,512]{2,1,0:T(8,128)(2,1)S(1)}, u32[]{:S(2)}, u32[]{:S(2)}) collective-permute-start(bf16[2,384,512]{2,1,0:T(8,128)(2,1)S(1)} %get-tuple-element.49), channel_id=1, source_target_pairs={{0,16},{4,20},{8,24},{12,28},{16,0},{20,4},{24,8},{28,12},{1,17},{... | collective-permute-start | bytes 2359304 | tf_op jit(solution)/shard_map/ppermute | solution.py:211
  177.7 36.5 %collective-permute-start.7 = (bf16[2,384,512]{2,1,0:T(8,128)(2,1)S(1)}, bf16[2,384,512]{2,1,0:T(8,128)(2,1)S(1)}, u32[]{:S(2)}, u32[]{:S(2)}) collective-permute-start(bf16[2,384,512]{2,1,0:T(8,128)(2,1)S(1)} %get-tuple-element.48), channel_id=1, source_target_pairs={{0,8},{4,12},{8,0},{12,4},{16,24},{20,28},{24,16},{28,20},{1,9},{5... | collective-permute-start | bytes 2359304 | tf_op jit(solution)/shard_map/ppermute | solution.py:211
  178.4 38.1 %slice-start = ((s8[6291456]{0:T(1024)(128)(4,1)}), s8[4194304]{0:T(1024)(128)(4,1)S(1)}, s32[]{:S(2)}) async-start(s8[6291456]{0:T(1024)(128)(4,1)} %bitcast.24), calls=%async_computation.4 | async-start | bytes 8388608
  178.8 47.8 %collective-permute-start.18 = (bf16[512,768]{1,0:T(8,128)(2,1)}, bf16[512,768]{1,0:T(8,128)(2,1)}, u32[]{:S(2)}, u32[]{:S(2)}) collective-permute-start(bf16[512,768]{1,0:T(8,128)(2,1)} %get-tuple-element.63.refs_2_), channel_id=1, source_target_pairs={{0,3},{1,0},{2,1},{3,2},{4,7},{5,4},{6,5},{7,6},{8,11},{9,8},{10,9... | collective-permute-start | bytes 2359304 | tf_op jit(solution)/shard_map/ppermute | solution.py:390
  181.4 51.4 %collective-permute-start.17 = (bf16[512,768]{1,0:T(8,128)(2,1)}, bf16[512,768]{1,0:T(8,128)(2,1)}, u32[]{:S(2)}, u32[]{:S(2)}) collective-permute-start(bf16[512,768]{1,0:T(8,128)(2,1)} %get-tuple-element.63.refs_2_), channel_id=1, source_target_pairs={{0,2},{1,3},{2,0},{3,1},{4,6},{5,7},{6,4},{7,5},{8,10},{9,11},{10,... | collective-permute-start | bytes 2359304 | tf_op jit(solution)/shard_map/ppermute | solution.py:390
  182.0 32.2 %copy-start.18 = (f32[2,384,512]{2,1,0:T(8,128)S(1)}, f32[2,384,512]{2,1,0:T(8,128)}, u32[]{:S(2)}) copy-start(f32[2,384,512]{2,1,0:T(8,128)} %get-tuple-element.47.refs_0_) | copy-start | bytes 4718596
  182.0 32.2 %copy-start.19 = (f32[2,384,512]{2,1,0:T(8,128)S(1)}, f32[2,384,512]{2,1,0:T(8,128)}, u32[]{:S(2)}) copy-start(f32[2,384,512]{2,1,0:T(8,128)} %get-tuple-element.66.refs_2_) | copy-start | bytes 4718596
  182.0 34.5 %slice-start.1 = ((s8[6291456]{0:T(1024)(128)(4,1)}), s8[2097152]{0:T(1024)(128)(4,1)S(1)}, s32[]{:S(2)}) async-start(s8[6291456]{0:T(1024)(128)(4,1)} %bitcast.24), calls=%async_computation.5 | async-start | bytes 4194304
  200.6 3.2 copy-start
  203.8 10.6 %copy-start.24 = (bf16[512,768]{1,0:T(8,128)(2,1)}, bf16[512,768]{1,0:T(8,128)(2,1)S(1)}, u32[]{:S(2)}) copy-start(bf16[512,768]{1,0:T(8,128)(2,1)S(1)} %collective-permute-done.14.refs_3_) | copy-start | bytes 2359300
  214.4 18.4 %collective-permute-start.15 = (bf16[1,384,512]{2,1,0:T(8,128)(2,1)S(1)}, bf16[1,384,512]{2,1,0:T(8,128)(2,1)S(1)}, u32[]{:S(2)}, u32[]{:S(2)}) collective-permute-start(bf16[1,384,512]{2,1,0:T(8,128)(2,1)S(1)} %get-tuple-element.69), channel_id=1, source_target_pairs={{0,16},{4,20},{8,24},{12,28},{16,0},{20,4},{24,8},{28,12},{1,17},{... | collective-permute-start | bytes 1179656 | tf_op jit(solution)/shard_map/ppermute | solution.py:211
  215.0 17.8 %collective-permute-start.16 = (bf16[1,384,512]{2,1,0:T(8,128)(2,1)S(1)}, bf16[1,384,512]{2,1,0:T(8,128)(2,1)S(1)}, u32[]{:S(2)}, u32[]{:S(2)}) collective-permute-start(bf16[1,384,512]{2,1,0:T(8,128)(2,1)S(1)} %get-tuple-element.70), channel_id=1, source_target_pairs={{0,8},{4,12},{8,0},{12,4},{16,24},{20,28},{24,16},{28,20},{1,9},{5... | collective-permute-start | bytes 1179656 | tf_op jit(solution)/shard_map/ppermute | solution.py:211
  216.5 1.9 copy-start.22
  233.9 57.2 %copy-start.20 = (bf16[512,768]{1,0:T(8,128)(2,1)}, bf16[512,768]{1,0:T(8,128)(2,1)S(1)}, u32[]{:S(2)}) copy-start(bf16[512,768]{1,0:T(8,128)(2,1)S(1)} %get-tuple-element.76.refs_2_) | copy-start | bytes 2359300
  236.6 54.5 %collective-permute-start.21 = (bf16[512,768]{1,0:T(8,128)(2,1)S(1)}, bf16[512,768]{1,0:T(8,128)(2,1)S(1)}, u32[]{:S(2)}, u32[]{:S(2)}) collective-permute-start(bf16[512,768]{1,0:T(8,128)(2,1)S(1)} %get-tuple-element.76.refs_2_), channel_id=1, source_target_pairs={{0,3},{1,0},{2,1},{3,2},{4,7},{5,4},{6,5},{7,6},{8,11},{9,8},{10,9... | collective-permute-start | bytes 2359304 | tf_op jit(solution)/shard_map/ppermute | solution.py:390
  239.4 66.3 %collective-permute-start.20 = (bf16[512,768]{1,0:T(8,128)(2,1)S(1)}, bf16[512,768]{1,0:T(8,128)(2,1)S(1)}, u32[]{:S(2)}, u32[]{:S(2)}) collective-permute-start(bf16[512,768]{1,0:T(8,128)(2,1)S(1)} %get-tuple-element.76.refs_2_), channel_id=1, source_target_pairs={{0,2},{1,3},{2,0},{3,1},{4,6},{5,7},{6,4},{7,5},{8,10},{9,11},{10,... | collective-permute-start | bytes 2359304 | tf_op jit(solution)/shard_map/ppermute | solution.py:390
  239.4 66.3 %collective-permute-start.19 = (bf16[512,768]{1,0:T(8,128)(2,1)S(1)}, bf16[512,768]{1,0:T(8,128)(2,1)S(1)}, u32[]{:S(2)}, u32[]{:S(2)}) collective-permute-start(bf16[512,768]{1,0:T(8,128)(2,1)S(1)} %get-tuple-element.76.refs_2_), channel_id=1, source_target_pairs={{0,1},{1,2},{2,3},{3,0},{4,5},{5,6},{6,7},{7,4},{8,9},{9,10},{10,1... | collective-permute-start | bytes 2359304 | tf_op jit(solution)/shard_map/ppermute | solution.py:390
  291.1 14.6 %copy-start.25 = (bf16[512,768]{1,0:T(8,128)(2,1)}, bf16[512,768]{1,0:T(8,128)(2,1)S(1)}, u32[]{:S(2)}) copy-start(bf16[512,768]{1,0:T(8,128)(2,1)S(1)} %collective-permute-done.21.refs_5_) | copy-start | bytes 2359300
  (10 other events, 11.1 us)
Sparse Core Ops, SparseCore 0:
  48.7 44.8 all-gather.8
  98.8 37.8 all-gather.10
  145.1 78.8 all-gather.12
  234.0 45.1 all-gather.14

commit v4 on v2

--- a/solution.py
+++ b/solution.py
@@ -82,10 +82,12 @@
     return sum(((value >> b) & 1) << (bits - 1 - b) for b in range(bits))
 
 
-def kept_kernel(count, bits, order_ref, *refs):
-    x_refs, w_ref, other_ref = refs[:count], refs[count], refs[count + 1]
-    halves = (refs[count + 2 : count + 4], refs[count + 4 : count + 6])
-    total = multiply_rows(x_refs, w_ref[0]) + other_ref[0].astype(jnp.float32)
+def kept_kernel(count, other_count, bits, order_ref, *refs):
+    x_refs, w_ref, refs = refs[:count], refs[count], refs[count + 1 :]
+    other_refs, refs = refs[:other_count], refs[other_count:]
+    halves = (refs[:2], refs[2:])
+    other = jnp.concatenate([r[0] for r in other_refs], axis=0)
+    total = multiply_rows(x_refs, w_ref[0]) + other.astype(jnp.float32)
     rows = total.shape[0] // 2
     step = pl.program_id(0)
     split = 1 << (bits - 1)
@@ -99,44 +101,55 @@
                 target[place % split] = total[h * rows : (h + 1) * rows].astype(target.dtype)
 
 
-def pair_products(xs, weights, order_sent, order_kept, row_partner, beside):
-    count = len(xs)
+def product_parts(xs, weights):
     rows, depth = xs[0].shape
     group_count, _, width = weights.shape
     blocks = group_count // 2
-    bits = blocks.bit_length() - 1
-    total_rows = count * rows
+    total_rows = len(xs) * rows
     x_spec = pl.BlockSpec((rows, depth), lambda g, order: (0, 0))
     w_spec = pl.BlockSpec((1, depth, width), lambda g, order: (order[g], 0, 0))
-    block_spec = pl.BlockSpec((1, total_rows, width), lambda g, order: (g, 0, 0))
     cost = pl.CostEstimate(
         flops=2 * total_rows * depth * blocks * width,
-        bytes_accessed=weights.size + 2 * count * xs[0].size + 2 * blocks * total_rows * width,
+        bytes_accessed=weights.size + 2 * len(xs) * xs[0].size + 2 * blocks * total_rows * width,
         transcendentals=0,
     )
     params = pltpu.CompilerParams(vmem_limit_bytes=48 * MIB)
-    sent = pl.pallas_call(
-        functools.partial(sent_kernel, count),
+    return blocks, total_rows, width, [x_spec] * len(xs) + [w_spec], cost, params
+
+
+def products_sent(xs, weights, order_sent):
+    blocks, total_rows, width, specs, cost, params = product_parts(xs, weights)
+    return pl.pallas_call(
+        functools.partial(sent_kernel, len(xs)),
         grid_spec=pltpu.PrefetchScalarGridSpec(
             num_scalar_prefetch=1,
             grid=(blocks,),
-            in_specs=[x_spec] * count + [w_spec],
-            out_specs=block_spec,
+            in_specs=specs,
+            out_specs=pl.BlockSpec((1, total_rows, width), lambda g, order: (g, 0, 0)),
         ),
         out_shape=jax.ShapeDtypeStruct((blocks, total_rows, width), jnp.bfloat16),
         compiler_params=params,
         cost_estimate=cost,
         name="products_sent",
     )(order_sent, *xs, weights)
-    other = tie(lax.ppermute(sent, "row", row_partner(1)), beside(0, sent))
+
+
+def pair_products(xs, weights, sents, order_kept, row_partner, beside):
+    blocks, total_rows, width, specs, cost, params = product_parts(xs, weights)
+    bits = blocks.bit_length() - 1
+    others = tie([lax.ppermute(s, "row", row_partner(1)) for s in sents], beside(0, sents[-1]))
     half = (blocks // 2, total_rows // 2, width)
     half_spec = pl.BlockSpec(half, lambda g, order: (0, 0, 0))
     outs = pl.pallas_call(
-        functools.partial(kept_kernel, count, bits),
+        functools.partial(kept_kernel, len(xs), len(others), bits),
         grid_spec=pltpu.PrefetchScalarGridSpec(
             num_scalar_prefetch=1,
             grid=(blocks,),
-            in_specs=[x_spec] * count + [w_spec, block_spec],
+            in_specs=specs
+            + [
+                pl.BlockSpec((1, other.shape[1], width), lambda g, order: (g, 0, 0))
+                for other in others
+            ],
             out_specs=[half_spec] * 4,
         ),
         out_shape=[
@@ -147,7 +160,7 @@
         compiler_params=params,
         cost_estimate=cost,
         name="products_kept",
-    )(order_kept, *xs, weights, other)
+    )(order_kept, *xs, weights, *others)
     return [(outs[0], outs[1]), (outs[2], outs[3])]
 
 
@@ -202,8 +215,8 @@
     )(pieces[0][1], others[0], pieces[1][1], others[1])
 
 
-def sum_over_rows(xs, weights, order_sent, order_kept, row_partner, beside):
-    pieces = pair_products(xs, weights, order_sent, order_kept, row_partner, beside)
+def sum_over_rows(xs, weights, sents, order_kept, row_partner, beside):
+    pieces = pair_products(xs, weights, sents, order_kept, row_partner, beside)
     bits = weights.shape[0].bit_length() - 2
     for level in range(bits):
         masks = (2 << level, 1 << (bits - level))
@@ -405,9 +418,13 @@
         first = k * per_group
         while not complete(first + per_group):
             advance()
+        sents = []
         if not k:
-            xs[-1] = tie(xs[-1], [weights])
+            sents.append(products_sent(xs[0], weights, order_sent))
+            xs[1] = tie(xs[1], sents)
         group = xs[first : first + per_group]
+        rest = [x for pieces in group[len(sents) :] for x in pieces]
+        sents.append(products_sent(rest, weights, order_sent))
         own = [
             lax.dynamic_slice_in_dim(x, col_index * sub_width, sub_width, 1)
             for pieces in group
@@ -441,7 +458,7 @@
         share, turned = sum_over_rows(
             [x for pieces in group for x in pieces],
             weights,
-            order_sent,
+            sents,
             order_kept,
             row_partner,
             beside,

time: 362 us -> 361 us (level)
    ppermute x6, waiting for transfers between devices: 49.8 us -> 44.1 us  [advance(): done = lax.ppermute(xs[-2][len(xs[-1])], 'col', ring)]
    pallas_call x4 -> x5, Pallas kernels: 44.6 us -> 48 us  [the longest x3 24.5 us: products_sent(): pl.pallas_call(functools.partial(sent_kernel, len(xs)), grid_spec=pltpu.P...]
    unnamed x65 -> x69, local copies, waits for them, and re-layouts: 26.5 us -> 26.5 us
  transfers between devices with their start and end apart: 25 -> 26, of which waited for: 11 -> 11; matrix products, arithmetic and copies ran while one was open for 4% -> 4% of each run, Pallas kernels for 39% -> 40%
where the time goes in v4:
time: 361 us; the launch traced here: 360 us
  Pallas kernels  197 us (55%)
  waiting for transfers between devices  86.2 us (24%)
  local copies, waits for them, and re-layouts  30.3 us (8%)
  starting transfers between devices  23.6 us (7%)
  between operations  14.2 us (4%)
  other arithmetic  8.49 us (2%)
    pallas_call x2, Pallas kernels, update(): pl.pallas_call(functools.partial(update_kernel, sizes, group, sub_width,...  105 us
    ppermute x6, waiting for transfers between devices, advance(): done = lax.ppermute(xs[-2][len(xs[-1])], 'col', ring)  44.1 us
    ppermute x6, waiting for transfers between devices, to_distance(): lax.ppermute(y, 'col', [(c, (c + distance) % col_count) for c in range(co...  28.1 us
    unnamed x69, local copies, waits for them, and re-layouts  26.5 us
    pallas_call x3, Pallas kernels, products_sent(): pl.pallas_call(functools.partial(sent_kernel, len(xs)), grid_spec=pltpu.P...  24.5 us
    pallas_call x2, Pallas kernels, pair_products(): pl.pallas_call(functools.partial(kept_kernel, len(xs), len(others), bits)...  23.5 us
    pallas_call x1, Pallas kernels, narrow(): pl.pallas_call(narrow_kernel, grid=(row_total // tile, lane_tiles // SUBS...  19.3 us
    pallas_call x1, Pallas kernels, convert(): pl.pallas_call(convert_kernel, grid=(row_total // tile, lane_tiles // SUB...  19.2 us
  transfers between devices with their start and end apart: 26, of which 11 were waited for; matrix products, arithmetic and copies ran while one was open for 4% of the time, Pallas kernels for 40%

profile of v4, /device:TPU:0, one launch (start us, length us, event | category | flops | bytes accessed | tf_op | source)
XLA Modules:
  0.0 359.7 jit_solution(7244360341119924704)
XLA Ops:
  6.5 1.5 fusion.1
  8.0 3.1 collective-permute-start.1
  11.1 1.6 collective-permute-start
  12.7 19.2 %omega_to_bf16.1.refs_2_.refs_4_ = bf16[8,2048,512]{2,1,0:T(8,128)(2,1)S(1)} custom-call(f32[2048,32,128]{2,1,0:T(8,128)} %bitcast.28), custom_call_target="tpu_custom_call" | custom-call | bytes 50331648 | tf_op jit(solution)/shard_map/omega_to_bf16/pallas_call | solution.py:34
  31.8 6.2 %copy-done = bf16[8,2048,512]{2,1,0:T(8,128)(2,1)} copy-done((bf16[8,2048,512]{2,1,0:T(8,128)(2,1)}, bf16[8,2048,512]{2,1,0:T(8,128)(2,1)S(1)}, u32[]{:S(2)}) %copy-start) | copy-done | bytes 16777240
  38.0 6.8 %products_sent.3 = bf16[4,384,512]{2,1,0:T(8,128)(2,1)S(1)} custom-call(s32[4]{0:T(128)S(1)} %get-tuple-element.77.order_ref, bf16[192,2048]{1,0:T(8,128)(2,1)S(1)} %get-tuple-element.80.refs_0_, bf16[192,2048]{1,0:T(8,128)(2,1)S(1)} %get-tuple-element.79.refs_1_, bf16[8,2048,512]{2,1,0:T(8,128)(2,1)} %copy-done), custom_call_target="tpu_custom_call" | custom-call | flops 3221225472 | bytes 11534336 | tf_op jit(solution)/shard_map/products_sent/pallas_call | solution.py:122
  44.9 1.2 copy-done.16
  46.1 1.5 collective-permute-done.refs_0_.refs_2_
  48.6 6.8 %products_sent.5 = bf16[4,384,512]{2,1,0:T(8,128)(2,1)S(1)} custom-call(s32[4]{0:T(128)S(1)} %get-tuple-element.77.order_ref, bf16[192,2048]{1,0:T(8,128)(2,1)S(1)} %collective-permute-done.refs_0_.refs_2_, bf16[192,2048]{1,0:T(8,128)(2,1)S(1)} %collective-permute-done.1.refs_1_.refs_3_, bf16[8,2048,512]{2,1,0:T(8,128)(2,1)} %copy-done), custom_call_target="tpu_custom_call" | custom-call | flops 3221225472 | bytes 11534336 | tf_op jit(solution)/shard_map/products_sent/pallas_call | solution.py:122
  57.0 1.2 collective-permute-start.3
  59.0 1.2 copy-done.3
  60.2 18.1 %collective-permute-done.2.refs_0_ = bf16[192,2048]{1,0:T(8,128)(2,1)S(1)} collective-permute-done((bf16[192,2048]{1,0:T(8,128)(2,1)S(1)}, bf16[192,2048]{1,0:T(8,128)(2,1)S(1)}, u32[]{:S(2)}, u32[]{:S(2)}) %collective-permute-start.2) | collective-permute-done | bytes 786464 | tf_op jit(solution)/shard_map/ppermute | solution.py:396
  78.3 1.1 copy-done.28
  80.0 11.8 %products_kept.3 = (bf16[2,384,512]{2,1,0:T(8,128)(2,1)S(1)}, f32[2,384,512]{2,1,0:T(8,128)}, bf16[2,384,512]{2,1,0:T(8,128)(2,1)S(1)}, f32[2,384,512]{2,1,0:T(8,128)}) custom-call(s32[4]{0:T(128)S(1)} %get-tuple-element.78.order_ref, bf16[192,2048]{1,0:T(8,128)(2,1)S(1)} %get-tuple-element.80.refs_0_, bf16[192,2048]{1,0:T(8,128)(2,1)S(1)} %get-tuple-element.79.refs_1_, ...), custom_call_target="tpu_custom_call" | custom-call | flops 6442450944 | bytes 14680064 | tf_op jit(solution)/shard_map/products_kept/pallas_call | solution.py:143
  91.8 1.5 collective-permute-start.11
  93.3 1.6 collective-permute-start.12
  95.1 16.8 %collective-permute-done.4.refs_0_.refs_2_ = bf16[192,2048]{1,0:T(8,128)(2,1)S(1)} collective-permute-done((bf16[192,2048]{1,0:T(8,128)(2,1)S(1)}, bf16[192,2048]{1,0:T(8,128)(2,1)S(1)}, u32[]{:S(2)}, u32[]{:S(2)}) %collective-permute-start.4) | collective-permute-done | bytes 786464 | tf_op jit(solution)/shard_map/ppermute | solution.py:396
  112.0 1.7 copy-done.19
  113.7 1.4 copy-done.20
  115.3 1.6 collective-permute-start.13
  116.9 1.5 collective-permute-start.14
  120.5 7.4 %collective-permute-done.5.refs_1_.refs_3_ = bf16[192,2048]{1,0:T(8,128)(2,1)S(1)} collective-permute-done((bf16[192,2048]{1,0:T(8,128)(2,1)S(1)}, bf16[192,2048]{1,0:T(8,128)(2,1)S(1)}, u32[]{:S(2)}, u32[]{:S(2)}) %collective-permute-start.5) | collective-permute-done | bytes 786464 | tf_op jit(solution)/shard_map/ppermute | solution.py:396
  128.7 1.2 share.2
  131.5 1.1 copy-done.11
  132.7 1.1 copy-done.14
  133.8 10.8 %products_sent.4 = bf16[4,768,512]{2,1,0:T(8,128)(2,1)} custom-call(s32[4]{0:T(128)S(1)} %get-tuple-element.77.order_ref, bf16[192,2048]{1,0:T(8,128)(2,1)S(1)} %copy-done.7, bf16[192,2048]{1,0:T(8,128)(2,1)S(1)} %copy-done.9, bf16[192,2048]{1,0:T(8,128)(2,1)S(1)} %copy-done.11, bf16[192,2048]{1,0:T(8,128)(2,1)S(1)} %copy-done.14, bf16[8,2048,512]{2,1,0:T(8,128)(2,1)} %copy-done), custom_call_target="tpu_custom_call" | custom-call | flops 6442450944 | bytes 14680064 | tf_op jit(solution)/shard_map/products_sent/pallas_call | solution.py:122
  146.1 1.1 copy-done.4
  148.1 1.2 copy-done.5
  149.3 1.4 collective-permute-done.6.refs_5_
  150.6 11.7 %products_kept.2 = (bf16[2,384,512]{2,1,0:T(8,128)(2,1)S(1)}, f32[2,384,512]{2,1,0:T(8,128)}, bf16[2,384,512]{2,1,0:T(8,128)(2,1)S(1)}, f32[2,384,512]{2,1,0:T(8,128)}) custom-call(s32[4]{0:T(128)S(1)} %get-tuple-element.78.order_ref, bf16[192,2048]{1,0:T(8,128)(2,1)S(1)} %copy-done.7, bf16[192,2048]{1,0:T(8,128)(2,1)S(1)} %copy-done.9, ...), custom_call_target="tpu_custom_call" | custom-call | flops 6442450944 | bytes 14680064 | tf_op jit(solution)/shard_map/products_kept/pallas_call | solution.py:143
  162.3 1.1 collective-permute-start.8
  163.5 1.5 collective-permute-start.7
  165.5 2.7 collective-permute-start.19
  168.4 19.3 %narrow_signs.1.refs_15_ = s8[2048,4096]{1,0:T(32,128)(4,1)S(1)} custom-call(s32[2048,32,128]{2,1,0:T(8,128)} %bitcast.30), custom_call_target="tpu_custom_call" | custom-call | bytes 41943040 | tf_op jit(solution)/shard_map/narrow_signs/pallas_call | solution.py:244
  187.7 3.3 copy-done.1
  191.1 7.7 %collective-permute-done.8.refs_3_ = bf16[2,384,512]{2,1,0:T(8,128)(2,1)S(1)} collective-permute-done((bf16[2,384,512]{2,1,0:T(8,128)(2,1)S(1)}, bf16[2,384,512]{2,1,0:T(8,128)(2,1)S(1)}, u32[]{:S(2)}, u32[]{:S(2)}) %collective-permute-start.8) | collective-permute-done | bytes 786464 | tf_op jit(solution)/shard_map/ppermute | solution.py:224
  198.8 1.3 collective-permute-done.7.refs_1_
  201.3 1.2 collective-permute-start.17
  202.5 1.2 multiply_reduce_fusion.1
  203.7 18.1 %collective-permute-done.18.refs_4_ = bf16[512,768]{1,0:T(8,128)(2,1)S(1)} collective-permute-done((bf16[512,768]{1,0:T(8,128)(2,1)}, bf16[512,768]{1,0:T(8,128)(2,1)S(1)}, u32[]{:S(2)}, u32[]{:S(2)}) %collective-permute-start.18) | collective-permute-done | bytes 786464 | tf_op jit(solution)/shard_map/ppermute | solution.py:403
  221.8 1.1 share.3
  222.9 3.5 all-gather.9.cloned.1.call-done
  227.7 1.4 copy.6.refs_13_
  229.1 2.8 collective-permute-start.22
  232.5 4.3 %multiply_reduce_fusion = f32[8,512]{1,0:T(8,128)S(1)} fusion(bf16[8,1536,512]{2,1,0:T(8,128)(2,1)} %bitcast.14), kind=kLoop, calls=%fused_computation | loop fusion | flops 9433088 | bytes 6307840 | tf_op jit(solution)/shard_map/reduce_sum | solution.py:406
  237.4 50.4 %first_terms.1.refs_12_ = bf16[2048,4096]{1,0:T(8,128)(2,1)} custom-call(s32[5]{0:T(128)} %pad_add_fusion.info_ref, bf16[2048,384]{1,0:T(8,128)(2,1)} %copy-done.2, bf16[2048,384]{1,0:T(8,128)(2,1)} %copy-done.3, bf16[512,768]{1,0:T(8,128)(2,1)} %get-tuple-element.60.refs_2_, bf16[512,768]{1,0:T(8,128)(2,1)} %collective-permute-done.15.refs_3_, ...), custom_call_target="tpu_custom_call" | custom-call | flops 25769803776 | bytes 67108864 | tf_op jit(solution)/shard_map/first_terms/pallas_call | solution.py:339
  287.8 10.0 %collective-permute-done.21.refs_4_ = bf16[512,768]{1,0:T(8,128)(2,1)S(1)} collective-permute-done((bf16[512,768]{1,0:T(8,128)(2,1)S(1)}, bf16[512,768]{1,0:T(8,128)(2,1)S(1)}, u32[]{:S(2)}, u32[]{:S(2)}) %collective-permute-start.21) | collective-permute-done | bytes 786464 | tf_op jit(solution)/shard_map/ppermute | solution.py:403
  299.0 54.2 %last_terms.1 = f32[2048,32,128]{2,1,0:T(8,128)} custom-call(s32[5]{0:T(128)} %pad_add_fusion.info_ref, bf16[2048,384]{1,0:T(8,128)(2,1)} %copy-done.4, bf16[2048,384]{1,0:T(8,128)(2,1)} %copy-done.5, bf16[512,768]{1,0:T(8,128)(2,1)} %copy-done.21, bf16[512,768]{1,0:T(8,128)(2,1)} %copy-done.27, bf16[512,768]{1,0:T(8,128)(2,1)} %copy-done.26, ...), custom_call_target="tpu_custom_call" | custom-call | flops 25769803776 | bytes 67108864 | tf_op jit(solution)/shard_map/last_terms/pallas_call | solution.py:339
  (117 shorter events, 16.2 us)
Async XLA Ops:
  6.5 144.1 %all-gather.7.cloned.1.call-start = ((), (), s32[]{:S(2)}) async-start(), calls=%async_computation | async-start | bytes 7077888 | tf_op jit(solution)/shard_map/all_gather | solution.py:414
  8.0 38.0 %collective-permute-start.1 = (bf16[192,2048]{1,0:T(8,128)(2,1)S(1)}, bf16[192,2048]{1,0:T(8,128)(2,1)S(1)}, u32[]{:S(2)}, u32[]{:S(2)}) collective-permute-start(bf16[192,2048]{1,0:T(8,128)(2,1)S(1)} %get-tuple-element.79.refs_1_), channel_id=1, source_target_pairs={{0,1},{1,2},{2,3},{3,0},{4,5},{5,6},{6,7},{7,4},{8,9},{9,10},{10,1... | collective-permute-start | bytes 2359304 | tf_op jit(solution)/shard_map/ppermute | solution.py:396
  11.1 36.4 %collective-permute-start = (bf16[192,2048]{1,0:T(8,128)(2,1)S(1)}, bf16[192,2048]{1,0:T(8,128)(2,1)S(1)}, u32[]{:S(2)}, u32[]{:S(2)}) collective-permute-start(bf16[192,2048]{1,0:T(8,128)(2,1)S(1)} %get-tuple-element.80.refs_0_), channel_id=1, source_target_pairs={{0,1},{1,2},{2,3},{3,0},{4,5},{5,6},{6,7},{7,4},{8,9},{9,10},{10,1... | collective-permute-start | bytes 2359304 | tf_op jit(solution)/shard_map/ppermute | solution.py:396
  31.8 6.2 %copy-start = (bf16[8,2048,512]{2,1,0:T(8,128)(2,1)}, bf16[8,2048,512]{2,1,0:T(8,128)(2,1)S(1)}, u32[]{:S(2)}) copy-start(bf16[8,2048,512]{2,1,0:T(8,128)(2,1)S(1)} %omega_to_bf16.1.refs_2_.refs_4_) | copy-start | bytes 50331652
  48.5 177.9 %all-gather.9.cloned.1.call-start = ((), (), s32[]{:S(2)}) async-start(), calls=%async_computation.1 | async-start | bytes 14155776 | tf_op jit(solution)/shard_map/all_gather | solution.py:414
  48.5 29.7 %collective-permute-start.9 = (bf16[4,384,512]{2,1,0:T(8,128)(2,1)}, bf16[4,384,512]{2,1,0:T(8,128)(2,1)S(1)}, u32[]{:S(2)}, u32[]{:S(2)}) collective-permute-start(bf16[4,384,512]{2,1,0:T(8,128)(2,1)} %copy-done.16), channel_id=1, source_target_pairs={{0,4},{4,0},{8,12},{12,8},{16,20},{20,16},{24,28},{28,24},{1,5},{5... | collective-permute-start | bytes 4718600 | tf_op jit(solution)/shard_map/ppermute | solution.py:140
  55.5 22.8 %collective-permute-start.10 = (bf16[4,384,512]{2,1,0:T(8,128)(2,1)S(1)}, bf16[4,384,512]{2,1,0:T(8,128)(2,1)S(1)}, u32[]{:S(2)}, u32[]{:S(2)}) collective-permute-start(bf16[4,384,512]{2,1,0:T(8,128)(2,1)S(1)} %products_sent.5), channel_id=1, source_target_pairs={{0,4},{4,0},{8,12},{12,8},{16,20},{20,16},{24,28},{28,24},{1,5},{5... | collective-permute-start | bytes 4718600 | tf_op jit(solution)/shard_map/ppermute | solution.py:140
  56.1 22.2 %collective-permute-start.2 = (bf16[192,2048]{1,0:T(8,128)(2,1)S(1)}, bf16[192,2048]{1,0:T(8,128)(2,1)S(1)}, u32[]{:S(2)}, u32[]{:S(2)}) collective-permute-start(bf16[192,2048]{1,0:T(8,128)(2,1)S(1)} %collective-permute-done.refs_0_.refs_2_), channel_id=1, source_target_pairs={{0,1},{1,2},{2,3},{3,0},{4,5},{5,6},{6,7},{7,4},{8,9},{9,10},{10,1... | collective-permute-start | bytes 2359304 | tf_op jit(solution)/shard_map/ppermute | solution.py:396
  57.0 2.0 copy-start.2
  57.0 38.1 %collective-permute-start.3 = (bf16[192,2048]{1,0:T(8,128)(2,1)S(1)}, bf16[192,2048]{1,0:T(8,128)(2,1)S(1)}, u32[]{:S(2)}, u32[]{:S(2)}) collective-permute-start(bf16[192,2048]{1,0:T(8,128)(2,1)S(1)} %collective-permute-done.1.refs_1_.refs_3_), channel_id=1, source_target_pairs={{0,1},{1,2},{2,3},{3,0},{4,5},{5,6},{6,7},{7,4},{8,9},{9,10},{10,1... | collective-permute-start | bytes 2359304 | tf_op jit(solution)/shard_map/ppermute | solution.py:396
  78.3 40.1 %copy-start.6 = (bf16[192,2048]{1,0:T(8,128)(2,1)}, bf16[192,2048]{1,0:T(8,128)(2,1)S(1)}, u32[]{:S(2)}) copy-start(bf16[192,2048]{1,0:T(8,128)(2,1)S(1)} %collective-permute-done.2.refs_0_) | copy-start | bytes 2359300
  78.3 33.7 %collective-permute-start.4 = (bf16[192,2048]{1,0:T(8,128)(2,1)S(1)}, bf16[192,2048]{1,0:T(8,128)(2,1)S(1)}, u32[]{:S(2)}, u32[]{:S(2)}) collective-permute-start(bf16[192,2048]{1,0:T(8,128)(2,1)S(1)} %collective-permute-done.2.refs_0_), channel_id=1, source_target_pairs={{0,1},{1,2},{2,3},{3,0},{4,5},{5,6},{6,7},{7,4},{8,9},{9,10},{10,1... | collective-permute-start | bytes 2359304 | tf_op jit(solution)/shard_map/ppermute | solution.py:396
  78.3 1.7 copy-start.29
  91.8 20.2 %collective-permute-start.11 = (bf16[2,384,512]{2,1,0:T(8,128)(2,1)S(1)}, bf16[2,384,512]{2,1,0:T(8,128)(2,1)S(1)}, u32[]{:S(2)}, u32[]{:S(2)}) collective-permute-start(bf16[2,384,512]{2,1,0:T(8,128)(2,1)S(1)} %get-tuple-element.49), channel_id=1, source_target_pairs={{0,8},{4,12},{8,0},{12,4},{16,24},{20,28},{24,16},{28,20},{1,9},{5... | collective-permute-start | bytes 2359304 | tf_op jit(solution)/shard_map/ppermute | solution.py:224
  93.3 18.7 %collective-permute-start.12 = (bf16[2,384,512]{2,1,0:T(8,128)(2,1)S(1)}, bf16[2,384,512]{2,1,0:T(8,128)(2,1)S(1)}, u32[]{:S(2)}, u32[]{:S(2)}) collective-permute-start(bf16[2,384,512]{2,1,0:T(8,128)(2,1)S(1)} %get-tuple-element.50), channel_id=1, source_target_pairs={{0,16},{4,20},{8,24},{12,28},{16,0},{20,4},{24,8},{28,12},{1,17},{... | collective-permute-start | bytes 2359304 | tf_op jit(solution)/shard_map/ppermute | solution.py:224
  95.1 24.0 %copy-start.8 = (bf16[192,2048]{1,0:T(8,128)(2,1)}, bf16[192,2048]{1,0:T(8,128)(2,1)S(1)}, u32[]{:S(2)}) copy-start(bf16[192,2048]{1,0:T(8,128)(2,1)S(1)} %collective-permute-done.3.refs_1_) | copy-start | bytes 2359300
  95.1 32.8 %collective-permute-start.5 = (bf16[192,2048]{1,0:T(8,128)(2,1)S(1)}, bf16[192,2048]{1,0:T(8,128)(2,1)S(1)}, u32[]{:S(2)}, u32[]{:S(2)}) collective-permute-start(bf16[192,2048]{1,0:T(8,128)(2,1)S(1)} %collective-permute-done.3.refs_1_), channel_id=1, source_target_pairs={{0,1},{1,2},{2,3},{3,0},{4,5},{5,6},{6,7},{7,4},{8,9},{9,10},{10,1... | collective-permute-start | bytes 2359304 | tf_op jit(solution)/shard_map/ppermute | solution.py:396
  112.0 7.8 %copy-start.10 = (bf16[192,2048]{1,0:T(8,128)(2,1)}, bf16[192,2048]{1,0:T(8,128)(2,1)S(1)}, u32[]{:S(2)}) copy-start(bf16[192,2048]{1,0:T(8,128)(2,1)S(1)} %collective-permute-done.4.refs_0_.refs_2_) | copy-start | bytes 2359300
  112.0 1.7 copy-start.19
  115.3 13.3 %collective-permute-start.13 = (bf16[1,384,512]{2,1,0:T(8,128)(2,1)S(1)}, bf16[1,384,512]{2,1,0:T(8,128)(2,1)S(1)}, u32[]{:S(2)}, u32[]{:S(2)}) collective-permute-start(bf16[1,384,512]{2,1,0:T(8,128)(2,1)S(1)} %get-tuple-element.55), channel_id=1, source_target_pairs={{0,16},{4,20},{8,24},{12,28},{16,0},{20,4},{24,8},{28,12},{1,17},{... | collective-permute-start | bytes 1179656 | tf_op jit(solution)/shard_map/ppermute | solution.py:224
  116.9 11.8 %collective-permute-start.14 = (bf16[1,384,512]{2,1,0:T(8,128)(2,1)S(1)}, bf16[1,384,512]{2,1,0:T(8,128)(2,1)S(1)}, u32[]{:S(2)}, u32[]{:S(2)}) collective-permute-start(bf16[1,384,512]{2,1,0:T(8,128)(2,1)S(1)} %get-tuple-element.56), channel_id=1, source_target_pairs={{0,8},{4,12},{8,0},{12,4},{16,24},{20,28},{24,16},{28,20},{1,9},{5... | collective-permute-start | bytes 1179656 | tf_op jit(solution)/shard_map/ppermute | solution.py:224
  127.9 2.0 copy-start.13
  129.9 1.4 copy-start.7
  129.9 1.7 copy-start.9
  130.9 167.0 %all-gather.11.cloned.1.call-start = ((), (), s32[]{:S(2)}) async-start(), calls=%async_computation.2 | async-start | bytes 7077888 | tf_op jit(solution)/shard_map/all_gather | solution.py:414
  133.8 10.8 %copy-start.22 = (bf16[384,2048]{1,0:T(8,128)(2,1)S(1)}, bf16[384,2048]{1,0:T(8,128)(2,1)}, u32[]{:S(2)}) copy-start(bf16[384,2048]{1,0:T(8,128)(2,1)} %param.4) | copy-start | bytes 4718596
  144.6 6.0 %collective-permute-start.6 = (bf16[4,768,512]{2,1,0:T(8,128)(2,1)}, bf16[4,768,512]{2,1,0:T(8,128)(2,1)}, u32[]{:S(2)}, u32[]{:S(2)}) collective-permute-start(bf16[4,768,512]{2,1,0:T(8,128)(2,1)} %products_sent.4), channel_id=1, source_target_pairs={{0,4},{4,0},{8,12},{12,8},{16,20},{20,16},{24,28},{28,24},{1,5},{5... | collective-permute-start | bytes 9437192 | tf_op jit(solution)/shard_map/ppermute | solution.py:140
  147.3 3.4 copy-start.12
  147.3 3.4 copy-start.15
  149.3 41.8 %collective-permute-start.15 = (bf16[512,768]{1,0:T(8,128)(2,1)}, bf16[512,768]{1,0:T(8,128)(2,1)}, u32[]{:S(2)}, u32[]{:S(2)}) collective-permute-start(bf16[512,768]{1,0:T(8,128)(2,1)} %get-tuple-element.60.refs_2_), channel_id=1, source_target_pairs={{0,1},{1,2},{2,3},{3,0},{4,5},{5,6},{6,7},{7,4},{8,9},{9,10},{10,1... | collective-permute-start | bytes 2359304 | tf_op jit(solution)/shard_map/ppermute | solution.py:403
  162.3 36.5 %collective-permute-start.8 = (bf16[2,384,512]{2,1,0:T(8,128)(2,1)S(1)}, bf16[2,384,512]{2,1,0:T(8,128)(2,1)S(1)}, u32[]{:S(2)}, u32[]{:S(2)}) collective-permute-start(bf16[2,384,512]{2,1,0:T(8,128)(2,1)S(1)} %get-tuple-element.45), channel_id=1, source_target_pairs={{0,16},{4,20},{8,24},{12,28},{16,0},{20,4},{24,8},{28,12},{1,17},{... | collective-permute-start | bytes 2359304 | tf_op jit(solution)/shard_map/ppermute | solution.py:224
  163.5 36.7 %collective-permute-start.7 = (bf16[2,384,512]{2,1,0:T(8,128)(2,1)S(1)}, bf16[2,384,512]{2,1,0:T(8,128)(2,1)S(1)}, u32[]{:S(2)}, u32[]{:S(2)}) collective-permute-start(bf16[2,384,512]{2,1,0:T(8,128)(2,1)S(1)} %get-tuple-element.44), channel_id=1, source_target_pairs={{0,8},{4,12},{8,0},{12,4},{16,24},{20,28},{24,16},{28,20},{1,9},{5... | collective-permute-start | bytes 2359304 | tf_op jit(solution)/shard_map/ppermute | solution.py:224
  165.5 38.2 %collective-permute-start.19 = (bf16[512,768]{1,0:T(8,128)(2,1)}, bf16[512,768]{1,0:T(8,128)(2,1)S(1)}, u32[]{:S(2)}, u32[]{:S(2)}) collective-permute-start(bf16[512,768]{1,0:T(8,128)(2,1)} %get-tuple-element.60.refs_2_), channel_id=1, source_target_pairs={{0,3},{1,0},{2,1},{3,2},{4,7},{5,4},{6,5},{7,6},{8,11},{9,8},{10,9... | collective-permute-start | bytes 2359304 | tf_op jit(solution)/shard_map/ppermute | solution.py:403
  168.2 53.6 %collective-permute-start.18 = (bf16[512,768]{1,0:T(8,128)(2,1)}, bf16[512,768]{1,0:T(8,128)(2,1)S(1)}, u32[]{:S(2)}, u32[]{:S(2)}) collective-permute-start(bf16[512,768]{1,0:T(8,128)(2,1)} %get-tuple-element.60.refs_2_), channel_id=1, source_target_pairs={{0,2},{1,3},{2,0},{3,1},{4,6},{5,7},{6,4},{7,5},{8,10},{9,11},{10,... | collective-permute-start | bytes 2359304 | tf_op jit(solution)/shard_map/ppermute | solution.py:403
  168.2 34.2 %slice-start = ((s8[6291456]{0:T(1024)(128)(4,1)}), s8[4194304]{0:T(1024)(128)(4,1)S(1)}, s32[]{:S(2)}) async-start(s8[6291456]{0:T(1024)(128)(4,1)} %bitcast.25), calls=%async_computation.3 | async-start | bytes 8388608
  168.4 31.7 %copy-start.17 = (f32[2,384,512]{2,1,0:T(8,128)S(1)}, f32[2,384,512]{2,1,0:T(8,128)}, u32[]{:S(2)}) copy-start(f32[2,384,512]{2,1,0:T(8,128)} %get-tuple-element.43.refs_0_) | copy-start | bytes 4718596
  168.4 31.7 %copy-start.18 = (f32[2,384,512]{2,1,0:T(8,128)S(1)}, f32[2,384,512]{2,1,0:T(8,128)}, u32[]{:S(2)}) copy-start(f32[2,384,512]{2,1,0:T(8,128)} %get-tuple-element.63.refs_2_) | copy-start | bytes 4718596
  168.4 34.0 %slice-start.1 = ((s8[6291456]{0:T(1024)(128)(4,1)}), s8[2097152]{0:T(1024)(128)(4,1)S(1)}, s32[]{:S(2)}) async-start(s8[6291456]{0:T(1024)(128)(4,1)} %bitcast.25), calls=%async_computation.4 | async-start | bytes 4194304
  187.7 3.3 copy-start.1
  200.4 21.4 %collective-permute-start.16 = (bf16[1,384,512]{2,1,0:T(8,128)(2,1)S(1)}, bf16[1,384,512]{2,1,0:T(8,128)(2,1)S(1)}, u32[]{:S(2)}, u32[]{:S(2)}) collective-permute-start(bf16[1,384,512]{2,1,0:T(8,128)(2,1)S(1)} %get-tuple-element.66), channel_id=1, source_target_pairs={{0,16},{4,20},{8,24},{12,28},{16,0},{20,4},{24,8},{28,12},{1,17},{... | collective-permute-start | bytes 1179656 | tf_op jit(solution)/shard_map/ppermute | solution.py:224
  201.3 20.5 %collective-permute-start.17 = (bf16[1,384,512]{2,1,0:T(8,128)(2,1)S(1)}, bf16[1,384,512]{2,1,0:T(8,128)(2,1)S(1)}, u32[]{:S(2)}, u32[]{:S(2)}) collective-permute-start(bf16[1,384,512]{2,1,0:T(8,128)(2,1)S(1)} %get-tuple-element.67), channel_id=1, source_target_pairs={{0,8},{4,12},{8,0},{12,4},{16,24},{20,28},{24,16},{28,20},{1,9},{5... | collective-permute-start | bytes 1179656 | tf_op jit(solution)/shard_map/ppermute | solution.py:224
  203.7 22.7 %copy-start.23 = (bf16[512,768]{1,0:T(8,128)(2,1)}, bf16[512,768]{1,0:T(8,128)(2,1)S(1)}, u32[]{:S(2)}) copy-start(bf16[512,768]{1,0:T(8,128)(2,1)S(1)} %collective-permute-done.19.refs_5_) | copy-start | bytes 2359300
  221.8 4.6 %copy-start.24 = (bf16[512,768]{1,0:T(8,128)(2,1)}, bf16[512,768]{1,0:T(8,128)(2,1)S(1)}, u32[]{:S(2)}) copy-start(bf16[512,768]{1,0:T(8,128)(2,1)S(1)} %collective-permute-done.18.refs_4_) | copy-start | bytes 2359300
  222.9 13.8 %copy-start.21 = (bf16[512,768]{1,0:T(8,128)(2,1)}, bf16[512,768]{1,0:T(8,128)(2,1)S(1)}, u32[]{:S(2)}) copy-start(bf16[512,768]{1,0:T(8,128)(2,1)S(1)} %get-tuple-element.71.refs_2_) | copy-start | bytes 2359300
  229.1 58.7 %collective-permute-start.22 = (bf16[512,768]{1,0:T(8,128)(2,1)S(1)}, bf16[512,768]{1,0:T(8,128)(2,1)S(1)}, u32[]{:S(2)}, u32[]{:S(2)}) collective-permute-start(bf16[512,768]{1,0:T(8,128)(2,1)S(1)} %get-tuple-element.71.refs_2_), channel_id=1, source_target_pairs={{0,3},{1,0},{2,1},{3,2},{4,7},{5,4},{6,5},{7,6},{8,11},{9,8},{10,9... | collective-permute-start | bytes 2359304 | tf_op jit(solution)/shard_map/ppermute | solution.py:403
  231.9 65.9 %collective-permute-start.21 = (bf16[512,768]{1,0:T(8,128)(2,1)S(1)}, bf16[512,768]{1,0:T(8,128)(2,1)S(1)}, u32[]{:S(2)}, u32[]{:S(2)}) collective-permute-start(bf16[512,768]{1,0:T(8,128)(2,1)S(1)} %get-tuple-element.71.refs_2_), channel_id=1, source_target_pairs={{0,2},{1,3},{2,0},{3,1},{4,6},{5,7},{6,4},{7,5},{8,10},{9,11},{10,... | collective-permute-start | bytes 2359304 | tf_op jit(solution)/shard_map/ppermute | solution.py:403
  231.9 65.9 %collective-permute-start.20 = (bf16[512,768]{1,0:T(8,128)(2,1)S(1)}, bf16[512,768]{1,0:T(8,128)(2,1)S(1)}, u32[]{:S(2)}, u32[]{:S(2)}) collective-permute-start(bf16[512,768]{1,0:T(8,128)(2,1)S(1)} %get-tuple-element.71.refs_2_), channel_id=1, source_target_pairs={{0,1},{1,2},{2,3},{3,0},{4,5},{5,6},{6,7},{7,4},{8,9},{9,10},{10,1... | collective-permute-start | bytes 2359304 | tf_op jit(solution)/shard_map/ppermute | solution.py:403
  287.8 10.0 %copy-start.25 = (bf16[512,768]{1,0:T(8,128)(2,1)}, bf16[512,768]{1,0:T(8,128)(2,1)S(1)}, u32[]{:S(2)}) copy-start(bf16[512,768]{1,0:T(8,128)(2,1)S(1)} %collective-permute-done.22.refs_5_) | copy-start | bytes 2359300
  (10 other events, 11.6 us)
Sparse Core Ops, SparseCore 0:
  48.6 44.9 all-gather.6
  131.0 95.3 all-gather.8
  228.3 45.3 all-gather.10
